TPU v7x, 128 devices: a whole 4x4x4 slice. The times are simulated.
128 devices in a mesh: row: 8 (over x, core), col: 16 (over z, y).
Axes of the slice: x: 4, y: 4, z: 4, core: 2. Of those that a mesh axis runs over, the one named last changes fastest.
Arguments:
- depth_tiles: bfloat16 [8, 8192, 1024], P('row', 'col'), may hold values from -6 to 6
- conf_tiles: bfloat16 [8, 8192, 1024], P('row', 'col'), may hold values from 0.19921875 to 2
- tile_owner: int32 [8, 8192], P('row', 'col'), may hold values from 0 to 15, as said below
- tile_offset: int32 [8, 8192], P('row', 'col'), may hold values from 0 to 511
- tile_count: int32 [8, 16], P('row', 'col'), may hold values from 320 to 512, as said below
- prior: float32 [4096, 16384], P('row', 'col'), may hold values from -6 to 6
- edge_rows: float32 [4096, 16384], P('row', 'col'), may hold values from 0.25 to 4
- edge_cols: float32 [4096, 16384], P('row', 'col'), may hold values from 0.25 to 4
Outputs:
- height: float32 [4096, 16384], P('row', 'col')
- residual: float32 [4096, 16384], P('row', 'col')
Inputs may be any that keep to these rules, and one draw needn't show every extreme that they name: `tile_owner`: the 512 tiles of a keyframe come in 8 consecutive runs of 64; each run goes to one owner, the runs of a keyframe to distinct owners; the first run of every keyframe of one grid row block goes to the same owner. The live tiles of a keyframe are its first tile_count tiles.
All inputs are finite; a program needn't handle non-finite values.
Results may differ from a plain program's by a relative error of at most 0.0003.
Values may be sent and summed in bfloat16 or wider, within the bound.
No kernel may reach another device: no remote copies, remote signals or barrier semaphores. Data moves between devices by JAX's collectives and lax.ppermute only.
A program may use at most 128 MiB of HBM per device.

v0:
```python
import jax
import jax.numpy as jnp
from jax import lax
from jax.sharding import PartitionSpec as P

TS = 32
GROUPS = 8
ITERS = 2


LAM = 0.05
HUBER = 0.5


def from_behind(shard, axis, by):
    devices = lax.axis_size(axis)
    pairs = [(i, i + by) for i in range(devices) if 0 <= i + by < devices]
    return lax.ppermute(shard, axis, pairs)


def padded_2(block, sides, width):
    for axis, dim in sides:
        count = lax.axis_size(axis)
        forward = [(i, i + 1) for i in range(count - 1)]
        backward = [(target, source) for source, target in forward]
        low = lax.ppermute(
            lax.slice_in_dim(block, block.shape[dim] - width, None, axis=dim), axis, forward
        )
        high = lax.ppermute(lax.slice_in_dim(block, 0, width, axis=dim), axis, backward)
        block = jnp.concatenate([low, block, high], axis=dim)
    return block


def to_tiles(grid, tile_side):
    grid_rows, grid_cols = grid.shape
    blocked = grid.reshape(grid_rows // tile_side, tile_side, grid_cols // tile_side, tile_side)
    return blocked.transpose(0, 2, 1, 3).reshape(-1, tile_side * tile_side)


def from_tiles(tiles, grid_rows, grid_cols, tile_side):
    blocked = tiles.reshape(grid_rows // tile_side, grid_cols // tile_side, tile_side, tile_side)
    return blocked.transpose(0, 2, 1, 3).reshape(grid_rows, grid_cols)


def huber_weight(depths, confidence, prior_at):
    return confidence * HUBER / jnp.maximum(jnp.abs(depths - prior_at), HUBER)


def make_operator(weight_sum, edge_rows, edge_cols):
    grid_rows, grid_cols = edge_rows.shape
    last_row = (lax.axis_index("row") == lax.axis_size("row") - 1) & (
        jnp.arange(grid_rows)[:, None] == grid_rows - 1
    )
    last_col = (lax.axis_index("col") == lax.axis_size("col") - 1) & (
        jnp.arange(grid_cols)[None, :] == grid_cols - 1
    )
    row_edge = jnp.where(last_row, jnp.float32(0.0), edge_rows)
    col_edge = jnp.where(last_col, jnp.float32(0.0), edge_cols)
    edge_upper = from_behind(row_edge[-1:, :], "row", 1)
    edge_left = from_behind(col_edge[:, -1:], "col", 1)
    row_above = jnp.concatenate([edge_upper, row_edge[:-1, :]], axis=0)
    col_before = jnp.concatenate([edge_left, col_edge[:, :-1]], axis=1)
    diagonal = weight_sum + LAM + row_edge + row_above + col_edge + col_before

    def operate(field):
        padded = padded_2(field, (("row", 0), ("col", 1)), 1)
        return (
            diagonal * field
            - row_edge * padded[2:, 1:-1]
            - row_above * padded[:-2, 1:-1]
            - col_edge * padded[1:-1, 2:]
            - col_before * padded[1:-1, :-2]
        )

    return operate


def squares(residual):
    return lax.psum(jnp.sum(residual * residual), ("row", "col"))


def shards(
    depth_tiles, conf_tiles, tile_owner, tile_offset, tile_count, prior, edge_rows, edge_cols
):
    grid_rows, grid_cols = prior.shape
    tile_cells = TS * TS
    tile_blocks = grid_rows // TS * (grid_cols // TS)
    tile_total = depth_tiles.shape[1]
    per_owner = tile_total // GROUPS
    columns = lax.axis_size("col")
    slot_total = columns * per_owner
    owners = tile_owner[0]
    offsets = tile_offset[0]
    live_count = tile_count[0, 0]
    tile_ids = jnp.arange(tile_total, dtype=jnp.int32)
    same_owner = owners[:, None] == owners[None, :]
    ranking = jnp.sum(same_owner & (tile_ids[None, :] < tile_ids[:, None]), axis=1)
    is_live = tile_ids < live_count
    slot_ids = jnp.arange(slot_total, dtype=jnp.int32)
    placing = ((owners * per_owner + ranking)[None, :] == slot_ids[:, None]) & is_live[None, :]
    targets = jnp.sum(jnp.where(placing, offsets[None, :] + 1, 0), axis=1) - 1
    prior_tiles = to_tiles(prior, TS)
    block_ids = jnp.arange(tile_blocks, dtype=jnp.int32)
    stacked = jnp.stack([depth_tiles[0], conf_tiles[0]], axis=1)
    payload = jnp.einsum(
        "sk,kct->sct", placing.astype(jnp.bfloat16), stacked, preferred_element_type=jnp.float32
    ).astype(jnp.bfloat16)
    received, arrived_target = (
        lax.all_to_all(
            payload.reshape(columns, per_owner, 2, tile_cells),
            "col",
            split_axis=0,
            concat_axis=0,
            tiled=True,
        ),
        lax.all_to_all(
            targets.reshape(columns, per_owner), "col", split_axis=0, concat_axis=0, tiled=True
        ),
    )
    received = received.reshape(slot_total, 2, tile_cells)
    arrived_target = arrived_target.reshape(slot_total)
    matches = (arrived_target[:, None] == block_ids[None, :]).astype(jnp.float32)
    prior_at = jnp.dot(matches, prior_tiles, precision=lax.Precision.HIGHEST)
    depths = received[:, 0].astype(jnp.float32)
    weights = huber_weight(depths, received[:, 1].astype(jnp.float32), prior_at)
    arrived = jnp.concatenate([weights, weights * depths], axis=1)
    totals = jnp.dot(matches.T, arrived, precision=lax.Precision.HIGHEST)
    weight_sum = from_tiles(totals[:, :tile_cells], grid_rows, grid_cols, TS)
    data_sum = from_tiles(totals[:, tile_cells:], grid_rows, grid_cols, TS)
    operate = make_operator(weight_sum, edge_rows, edge_cols)
    right_side = data_sum + LAM * prior
    height = prior
    residual = right_side - operate(prior)
    direction = residual
    norm_now = squares(residual)
    for iteration in range(ITERS):
        image = operate(direction)
        alpha = norm_now / lax.psum(jnp.sum(direction * image), ("row", "col"))
        height = height + alpha * direction
        residual = residual - alpha * image
        norm_next = squares(residual)
        direction = residual + norm_next / norm_now * direction
        norm_now = norm_next
    return (height, residual)


def solution(mesh):
    return jax.shard_map(
        shards,
        mesh=mesh,
        in_specs=(
            P("row", "col", None),
            P("row", "col", None),
            P("row", "col"),
            P("row", "col"),
            P("row", "col"),
            P("row", "col"),
            P("row", "col"),
            P("row", "col"),
        ),
        out_specs=(P("row", "col"), P("row", "col")),
        check_vma=False,
    )
```

profile of v0, /device:TPU:1, one launch (start us, length us, event | category | flops | bytes accessed | tf_op | source)
XLA Modules:
  0.0 452.9 jit_solution(16734493607322899017)
XLA Ops:
  0.6 1.0 convert_reduce_fusion
  1.6 0.7 multiply_add_fusion.2
  3.0 0.7 broadcast_add_fusion.1
  3.7 0.5 select_reduce_fusion
  4.2 0.7 sub.55
  4.9 8.6 %all-to-all-start = ((s32[16,1,64]{2,1,0:T(1,128)}), s32[16,1,64]{2,1,0:T(1,128)S(1)}, u32[]{:S(2)}, u32[]{:S(2)}) async-start(s32[16,1,64]{2,1,0:T(1,128)} %sub.55), calls=%async_computation | async-start | bytes 16384 | tf_op jit(solution)/shard_map/all_to_all | solution.py:116
  13.5 3.9 convolution_convert_fusion
  17.3 2.4 copy.25
  19.8 6.7 %all-to-all-start.1 = ((bf16[16,64,2,1024]{3,1,2,0:T(8,128)(2,1)}), bf16[16,64,2,1024]{3,1,2,0:T(8,128)(2,1)}, u32[]{:S(2)}, u32[]{:S(2)}) async-start(bf16[16,64,2,1024]{3,1,2,0:T(8,128)(2,1)} %copy.25), calls=%async_computation.1 | async-start | bytes 8388608 | tf_op jit(solution)/shard_map/all_to_all | solution.py:109
  26.5 1.8 broadcast_select_fusion
  28.3 1.0 slice.146
  29.3 3.2 collective-permute-start.1
  32.5 0.8 fusion.55
  33.3 4.0 collective-permute-start.2
  37.3 3.0 collective-permute-start.3
  40.3 1.8 broadcast_select_fusion.1
  42.2 1.3 copy-done.5
  43.5 2.6 collective-permute-start
  46.1 6.5 %reshape.73 = f32[16,32,32,32]{3,2,1,0:T(8,128)} reshape(f32[512,1024]{1,0:T(8,128)} %param.13) | data formatting | bytes 4194304 | tf_op jit(solution)/shard_map/reshape | solution.py:36
  52.6 13.1 %copy.37 = f32[16,32,32,32]{3,1,2,0:T(8,128)} copy(f32[16,32,32,32]{3,2,1,0:T(8,128)} %reshape.73) | data formatting | bytes 4194304 | tf_op jit(solution)/shard_map/reshape | solution.py:36
  65.7 7.9 %reshape.74 = f32[512,1024]{1,0:T(8,128)} reshape(f32[16,32,32,32]{3,2,1,0:T(8,128)} %bitcast.41) | data formatting | bytes 4194304 | tf_op jit(solution)/shard_map/reshape | solution.py:37
  73.6 0.5 broadcast.66
  74.1 0.7 reduce.3
  74.8 0.1 pad_maximum_fusion.34
  75.0 1.3 collective-permute-start.4
  76.3 4.4 collective-permute-start.5
  80.7 6.4 %all-to-all-done.1 = bf16[16,64,2,1024]{3,1,2,0:T(8,128)(2,1)} async-done(((bf16[16,64,2,1024]{3,1,2,0:T(8,128)(2,1)}), bf16[16,64,2,1024]{3,1,2,0:T(8,128)(2,1)}, u32[]{:S(2)}, u32[]{:S(2)}) %all-to-all-start.1) | async-done | bytes 4194336 | tf_op jit(solution)/shard_map/all_to_all | solution.py:109
  87.1 2.6 copy.26
  89.7 1.8 fusion.52
  91.5 3.9 copy.32
  95.4 2.5 copy.33
  97.9 10.0 %convert_multiply_fusion = (f32[1024,1024]{0,1:T(8,128)S(1)}, f32[1024,1024]{0,1:T(8,128)S(1)}) fusion(bf16[1024,1,1024]{0,2,1:T(8,128)(2,1)} %copy.33, f32[512,1024]{1,0:T(8,128)} %reshape.74, s32[1024]{0:T(1024)S(1)} %eq.81, bf16[1024,1,1024]{0,2,1:T(8,128)(2,1)} %copy.32), kind=kOutput, calls=%fused_computation.6 | convolution fusion | flops 6451363840 | bytes 14684160 | tf_op jit(solution)/shard_map/dot_general | solution.py:123
  108.0 7.9 %fusion = f32[512,2048]{1,0:T(8,128)S(1)} fusion(f32[1024,1024]{0,1:T(8,128)S(1)} %get-tuple-element.27, f32[1024,1024]{0,1:T(8,128)S(1)} %get-tuple-element.28, s32[1024]{0:T(1024)S(1)} %eq.81), kind=kOutput, calls=%fused_computation | convolution fusion | flops 12888047616 | bytes 12587008 | tf_op jit(solution)/shard_map/dot_general | solution.py:127
  115.9 1.9 fusion.51
  117.8 6.6 %add.69 = f32[16,32,32,32]{3,2,1,0:T(8,128)} reshape(f32[512,1024]{1,0:T(8,128)} %get-tuple-element.10) | data formatting | bytes 4194304 | tf_op jit(solution)/shard_map/add | solution.py:63
  124.4 13.1 %copy.31 = f32[16,32,32,32]{3,2,1,0:T(8,128)} copy(f32[16,32,32,32]{3,1,2,0:T(8,128)} %bitcast.42) | data formatting | bytes 4194304 | tf_op jit(solution)/shard_map/add | solution.py:63
  137.5 7.7 %add.71 = f32[512,1024]{1,0:T(8,128)} reshape(f32[16,32,32,32]{3,2,1,0:T(8,128)} %copy.31) | data formatting | bytes 4194304 | tf_op jit(solution)/shard_map/add | solution.py:63
  145.2 4.9 %reshape.75 = f32[16,32,32,32]{3,2,1,0:T(8,128)} reshape(f32[512,1024]{1,0:T(8,128)S(1)} %get-tuple-element.9) | data formatting | bytes 4194304 | tf_op jit(solution)/shard_map/reshape | solution.py:41
  150.2 13.1 %copy.36 = f32[16,32,32,32]{3,1,2,0:T(8,128)} copy(f32[16,32,32,32]{3,2,1,0:T(8,128)} %reshape.75) | data formatting | bytes 4194304 | tf_op jit(solution)/shard_map/reshape | solution.py:41
  163.3 7.7 %reshape.76 = f32[512,1024]{1,0:T(8,128)} reshape(f32[16,32,32,32]{3,2,1,0:T(8,128)} %bitcast.43) | data formatting | bytes 4194304 | tf_op jit(solution)/shard_map/reshape | solution.py:42
  171.1 11.8 %fusion.25 = f32[512,1024]{1,0:T(8,128)S(1)} fusion(f32[514,1]{1,0:T(8,128)S(1)} %collective-permute-done.5, f32[1,1024]{1,0:T(1,128)S(1)} %collective-permute-done.2, f32[512,1024]{1,0:T(8,128)} %param.13, f32[1,1024]{1,0:T(1,128)S(1)} %collective-permute-done.3, f32[514,1]{1,0:T(8,128)S(1)} %collective-permute-done.4, f32[512,1024]{1,0:T(8,128)} %add.71, ...), kind=kLoop, calls=%fused_computation.47 | loop fusion | flops 14680064 | bytes 16791056 | tf_op jit(solution)/shard_map/sub | solution.py:133
  182.9 6.4 %collective-permute-start.6 = (f32[1,1024]{1,0:T(1,128)S(1)}, f32[1,1024]{1,0:T(1,128)S(1)}, u32[]{:S(2)}, u32[]{:S(2)}) collective-permute-start(f32[1,1024]{1,0:T(1,128)S(1)} %get-tuple-element.24), channel_id=1, source_target_pairs={{16,0},{32,16},{48,32},{64,48},{80,64},{96,80},{112,96},{17,1},{33... | collective-permute-start | bytes 12296 | tf_op jit(solution)/shard_map/ppermute | solution.py:29
  189.4 3.0 collective-permute-start.7
  192.4 0.7 collective-permute-done.7
  193.1 0.1 pad_maximum_fusion.31
  193.3 1.3 collective-permute-start.8
  194.6 4.0 collective-permute-start.9
  198.6 4.8 %collective-permute-done.8 = f32[514,1]{1,0:T(8,128)S(1)} collective-permute-done((f32[514,1]{1,0:T(8,128)S(1)}, f32[514,1]{1,0:T(8,128)S(1)}, u32[]{:S(2)}, u32[]{:S(2)}) %collective-permute-start.8) | collective-permute-done | bytes 2088 | tf_op jit(solution)/shard_map/ppermute | solution.py:29
  203.4 1.1 collective-permute-done.9
  204.6 7.5 %multiply_reduce_fusion.2 = (f32[]{:T(128)}, f32[]{:T(128)}, f32[512,1024]{1,0:T(8,128)}) fusion(f32[512,1024]{1,0:T(8,128)S(1)} %fusion.25, f32[1,1024]{1,0:T(1,128)S(1)} %collective-permute-done.6, f32[1,1024]{1,0:T(1,128)S(1)} %collective-permute-done.7, f32[514,1]{1,0:T(8,128)S(1)} %collective-permute-done.9, f32[514,1]{1,0:T(8,128)S(1)} %collective-permute-done.8, ...), kind=kLoop, calls=%fused_computation.73 | loop fusion | flops 15204350 | bytes 14693912 | tf_op jit(solution)/shard_map/reduce_sum | solution.py:138
  212.1 68.4 %all-reduce = (f32[]{:T(128)}, f32[]{:T(128)}) all-reduce(f32[]{:T(128)} %get-tuple-element.3, f32[]{:T(128)} %get-tuple-element.2), channel_id=1, replica_groups=mesh['row'=8,'col'=16] {'row','col'}, use_global_device_ids=true, to_apply=%region_3.4 | all-reduce | flops 2 | bytes 16 | tf_op jit(solution)/shard_map/psum | solution.py:79
  281.7 2.7 multiply_reduce_fusion.1
  284.4 62.5 %psum.30 = f32[]{:T(128)} all-reduce(f32[]{:T(128)} %multiply_reduce_fusion.1), channel_id=1, replica_groups=mesh['row'=8,'col'=16] {'row','col'}, use_global_device_ids=true, to_apply=%region_7.8 | all-reduce | flops 1 | bytes 8 | tf_op jit(solution)/shard_map/psum | solution.py:79
  348.3 2.2 multiply_add_fusion.1
  350.6 2.8 collective-permute-start.10
  353.3 3.1 collective-permute-start.11
  356.4 0.7 collective-permute-done.11
  357.3 1.3 collective-permute-start.12
  358.6 4.0 collective-permute-start.13
  362.6 4.8 %collective-permute-done.12 = f32[514,1]{1,0:T(8,128)S(1)} collective-permute-done((f32[514,1]{1,0:T(8,128)S(1)}, f32[514,1]{1,0:T(8,128)S(1)}, u32[]{:S(2)}, u32[]{:S(2)}) %collective-permute-start.12) | collective-permute-done | bytes 2088 | tf_op jit(solution)/shard_map/ppermute | solution.py:29
  367.4 1.2 collective-permute-done.13
  368.6 7.8 %multiply_reduce_fusion = (f32[]{:T(128)}, f32[512,1024]{1,0:T(8,128)}) fusion(f32[512,1024]{1,0:T(8,128)S(1)} %multiply_add_fusion.1, f32[1,1024]{1,0:T(1,128)S(1)} %collective-permute-done.10, f32[1,1024]{1,0:T(1,128)S(1)} %collective-permute-done.11, f32[514,1]{1,0:T(8,128)S(1)} %collective-permute-done.13, f32[514,1]{1,0:T(8,128)S(1)} %collective-permute-done.12, ...), kind=kLoop, calls=%fused_computation.69 | loop fusion | flops 14155775 | bytes 14693908 | tf_op jit(solution)/shard_map/reduce_sum | solution.py:138
  376.4 67.8 %psum.31 = f32[]{:T(128)} all-reduce(f32[]{:T(128)} %get-tuple-element.6), channel_id=1, replica_groups=mesh['row'=8,'col'=16] {'row','col'}, use_global_device_ids=true, to_apply=%region_9.10 | all-reduce | flops 1 | bytes 8 | tf_op jit(solution)/shard_map/psum | solution.py:138
  445.5 7.0 %multiply_subtract_fusion = (f32[512,1024]{1,0:T(8,128)}, f32[512,1024]{1,0:T(8,128)}) fusion(f32[512,1024]{1,0:T(8,128)} %get-tuple-element.7, f32[]{:T(128)S(6)} %div.15, f32[512,1024]{1,0:T(8,128)S(1)} %fusion.25, f32[512,1024]{1,0:T(8,128)} %get-tuple-element.8, f32[]{:T(128)S(6)} %div.13, f32[512,1024]{1,0:T(8,128)} %copy-done.4, f32[512,1024]{1,0:T(8,128)} %param.13), kind=kLoop, calls=%fused_computation.67 | loop fusion | flops 4194304 | bytes 14680072 | tf_op jit(solution)/shard_map/sub | solution.py:140
  (43 shorter events, 0.4 us)
Async XLA Ops:
  4.9 14.9 %all-to-all-start = ((s32[16,1,64]{2,1,0:T(1,128)}), s32[16,1,64]{2,1,0:T(1,128)S(1)}, u32[]{:S(2)}, u32[]{:S(2)}) async-start(s32[16,1,64]{2,1,0:T(1,128)} %sub.55), calls=%async_computation | async-start | bytes 16384 | tf_op jit(solution)/shard_map/all_to_all | solution.py:116
  19.8 67.3 %all-to-all-start.1 = ((bf16[16,64,2,1024]{3,1,2,0:T(8,128)(2,1)}), bf16[16,64,2,1024]{3,1,2,0:T(8,128)(2,1)}, u32[]{:S(2)}, u32[]{:S(2)}) async-start(bf16[16,64,2,1024]{3,1,2,0:T(8,128)(2,1)} %copy.25), calls=%async_computation.1 | async-start | bytes 8388608 | tf_op jit(solution)/shard_map/all_to_all | solution.py:109
  28.3 13.9 %copy-start = (f32[512,1024]{1,0:T(8,128)}, f32[512,1024]{1,0:T(8,128)S(1)}, u32[]{:S(2)}) copy-start(f32[512,1024]{1,0:T(8,128)S(1)} %broadcast_select_fusion) | copy-start | bytes 6291460
  29.3 141.7 %collective-permute-start.1 = (f32[512,1]{1,0:T(8,128)}, f32[512,1]{1,0:T(8,128)S(1)}, u32[]{:S(2)}, u32[]{:S(2)}) collective-permute-start(f32[512,1]{1,0:T(8,128)} %slice.146), channel_id=1, source_target_pairs={{0,1},{1,2},{2,3},{3,4},{4,5},{5,6},{6,7},{7,8},{8,9},{9,10},{10,1... | collective-permute-start | bytes 6152 | tf_op jit(solution)/shard_map/ppermute | solution.py:18
  33.3 41.5 %collective-permute-start.2 = (f32[1,1024]{1,0:T(1,128)S(1)}, f32[1,1024]{1,0:T(1,128)S(1)}, u32[]{:S(2)}, u32[]{:S(2)}) collective-permute-start(f32[1,1024]{1,0:T(1,128)S(1)} %get-tuple-element.26), channel_id=1, source_target_pairs={{16,0},{32,16},{48,32},{64,48},{80,64},{96,80},{112,96},{17,1},{33... | collective-permute-start | bytes 12296 | tf_op jit(solution)/shard_map/ppermute | solution.py:29
  37.3 37.5 %collective-permute-start.3 = (f32[1,1024]{1,0:T(1,128)S(1)}, f32[1,1024]{1,0:T(1,128)S(1)}, u32[]{:S(2)}, u32[]{:S(2)}) collective-permute-start(f32[1,1024]{1,0:T(1,128)S(1)} %get-tuple-element.25), channel_id=1, source_target_pairs={{0,16},{16,32},{32,48},{48,64},{64,80},{80,96},{96,112},{1,17},{17... | collective-permute-start | bytes 12296 | tf_op jit(solution)/shard_map/ppermute | solution.py:26
  42.2 1.3 copy-start.5
  43.5 127.5 %collective-permute-start = (f32[1,1024]{1,0:T(1,128)S(1)}, f32[1,1024]{1,0:T(1,128)S(1)}, u32[]{:S(2)}, u32[]{:S(2)}) collective-permute-start(f32[1,1024]{1,0:T(1,128)S(1)} %slice.144), channel_id=1, source_target_pairs={{0,16},{16,32},{32,48},{48,64},{64,80},{80,96},{96,112},{1,17},{17... | collective-permute-start | bytes 12296 | tf_op jit(solution)/shard_map/ppermute | solution.py:18
  65.7 9.1 %copy-start.3 = (f32[512,1024]{1,0:T(8,128)S(1)}, f32[512,1024]{1,0:T(8,128)}, u32[]{:S(2)}) copy-start(f32[512,1024]{1,0:T(8,128)} %param.13) | copy-start | bytes 6291460
  75.0 96.0 %collective-permute-start.4 = (f32[514,1]{1,0:T(8,128)S(1)}, f32[514,1]{1,0:T(8,128)S(1)}, u32[]{:S(2)}, u32[]{:S(2)}) collective-permute-start(f32[514,1]{1,0:T(8,128)S(1)} %get-tuple-element.17), channel_id=1, source_target_pairs={{1,0},{2,1},{3,2},{4,3},{5,4},{6,5},{7,6},{8,7},{9,8},{10,9},{11,1... | collective-permute-start | bytes 6176 | tf_op jit(solution)/shard_map/ppermute | solution.py:29
  76.3 94.7 %collective-permute-start.5 = (f32[514,1]{1,0:T(8,128)S(1)}, f32[514,1]{1,0:T(8,128)S(1)}, u32[]{:S(2)}, u32[]{:S(2)}) collective-permute-start(f32[514,1]{1,0:T(8,128)S(1)} %get-tuple-element.18), channel_id=1, source_target_pairs={{0,1},{1,2},{2,3},{3,4},{4,5},{5,6},{6,7},{7,8},{8,9},{9,10},{10,1... | collective-permute-start | bytes 6176 | tf_op jit(solution)/shard_map/ppermute | solution.py:26
  171.0 33.5 %copy-start.6 = (f32[512,1024]{1,0:T(8,128)S(1)}, f32[512,1024]{1,0:T(8,128)}, u32[]{:S(2)}) copy-start(f32[512,1024]{1,0:T(8,128)} %copy-done.5) | copy-start | bytes 6291460
  171.0 33.5 %copy-start.8 = (f32[512,1024]{1,0:T(8,128)S(1)}, f32[512,1024]{1,0:T(8,128)}, u32[]{:S(2)}) copy-start(f32[512,1024]{1,0:T(8,128)} %param.15) | copy-start | bytes 6291460
  171.0 33.5 %copy-start.10 = (f32[512,1024]{1,0:T(8,128)S(1)}, f32[512,1024]{1,0:T(8,128)}, u32[]{:S(2)}) copy-start(f32[512,1024]{1,0:T(8,128)} %add.71) | copy-start | bytes 6291460
  171.0 33.5 %copy-start.12 = (f32[512,1024]{1,0:T(8,128)S(1)}, f32[512,1024]{1,0:T(8,128)}, u32[]{:S(2)}) copy-start(f32[512,1024]{1,0:T(8,128)} %param.14) | copy-start | bytes 6291460
  182.9 21.7 %copy-start.1 = (f32[512,1024]{1,0:T(8,128)S(1)}, f32[512,1024]{1,0:T(8,128)}, u32[]{:S(2)}) copy-start(f32[512,1024]{1,0:T(8,128)} %copy-done) | copy-start | bytes 6291460
  182.9 9.5 %collective-permute-start.6 = (f32[1,1024]{1,0:T(1,128)S(1)}, f32[1,1024]{1,0:T(1,128)S(1)}, u32[]{:S(2)}, u32[]{:S(2)}) collective-permute-start(f32[1,1024]{1,0:T(1,128)S(1)} %get-tuple-element.24), channel_id=1, source_target_pairs={{16,0},{32,16},{48,32},{64,48},{80,64},{96,80},{112,96},{17,1},{33... | collective-permute-start | bytes 12296 | tf_op jit(solution)/shard_map/ppermute | solution.py:29
  189.4 3.8 collective-permute-start.7
  193.3 10.2 %collective-permute-start.8 = (f32[514,1]{1,0:T(8,128)S(1)}, f32[514,1]{1,0:T(8,128)S(1)}, u32[]{:S(2)}, u32[]{:S(2)}) collective-permute-start(f32[514,1]{1,0:T(8,128)S(1)} %get-tuple-element.15), channel_id=1, source_target_pairs={{1,0},{2,1},{3,2},{4,3},{5,4},{6,5},{7,6},{8,7},{9,8},{10,9},{11,1... | collective-permute-start | bytes 6176 | tf_op jit(solution)/shard_map/ppermute | solution.py:29
  194.6 10.0 %collective-permute-start.9 = (f32[514,1]{1,0:T(8,128)S(1)}, f32[514,1]{1,0:T(8,128)S(1)}, u32[]{:S(2)}, u32[]{:S(2)}) collective-permute-start(f32[514,1]{1,0:T(8,128)S(1)} %get-tuple-element.16), channel_id=1, source_target_pairs={{0,1},{1,2},{2,3},{3,4},{4,5},{5,6},{6,7},{7,8},{8,9},{9,10},{10,1... | collective-permute-start | bytes 6176 | tf_op jit(solution)/shard_map/ppermute | solution.py:26
  348.3 20.3 %copy-start.7 = (f32[512,1024]{1,0:T(8,128)S(1)}, f32[512,1024]{1,0:T(8,128)}, u32[]{:S(2)}) copy-start(f32[512,1024]{1,0:T(8,128)} %copy-done.5) | copy-start | bytes 6291460
  348.3 20.3 %copy-start.9 = (f32[512,1024]{1,0:T(8,128)S(1)}, f32[512,1024]{1,0:T(8,128)}, u32[]{:S(2)}) copy-start(f32[512,1024]{1,0:T(8,128)} %param.15) | copy-start | bytes 6291460
  348.3 20.3 %copy-start.11 = (f32[512,1024]{1,0:T(8,128)S(1)}, f32[512,1024]{1,0:T(8,128)}, u32[]{:S(2)}) copy-start(f32[512,1024]{1,0:T(8,128)} %add.71) | copy-start | bytes 6291460
  350.5 25.9 %copy-start.4 = (f32[512,1024]{1,0:T(8,128)}, f32[512,1024]{1,0:T(8,128)S(1)}, u32[]{:S(2)}) copy-start(f32[512,1024]{1,0:T(8,128)S(1)} %multiply_add_fusion.1) | copy-start | bytes 6291460
  350.5 18.1 %copy-start.2 = (f32[512,1024]{1,0:T(8,128)S(1)}, f32[512,1024]{1,0:T(8,128)}, u32[]{:S(2)}) copy-start(f32[512,1024]{1,0:T(8,128)} %copy-done) | copy-start | bytes 6291460
  350.6 5.8 %collective-permute-start.10 = (f32[1,1024]{1,0:T(1,128)S(1)}, f32[1,1024]{1,0:T(1,128)S(1)}, u32[]{:S(2)}, u32[]{:S(2)}) collective-permute-start(f32[1,1024]{1,0:T(1,128)S(1)} %get-tuple-element.22), channel_id=1, source_target_pairs={{16,0},{32,16},{48,32},{64,48},{80,64},{96,80},{112,96},{17,1},{33... | collective-permute-start | bytes 12296 | tf_op jit(solution)/shard_map/ppermute | solution.py:29
  353.3 3.8 collective-permute-start.11
  357.3 10.1 %collective-permute-start.12 = (f32[514,1]{1,0:T(8,128)S(1)}, f32[514,1]{1,0:T(8,128)S(1)}, u32[]{:S(2)}, u32[]{:S(2)}) collective-permute-start(f32[514,1]{1,0:T(8,128)S(1)} %get-tuple-element.13), channel_id=1, source_target_pairs={{1,0},{2,1},{3,2},{4,3},{5,4},{6,5},{7,6},{8,7},{9,8},{10,9},{11,1... | collective-permute-start | bytes 6176 | tf_op jit(solution)/shard_map/ppermute | solution.py:29
  358.6 10.0 %collective-permute-start.13 = (f32[514,1]{1,0:T(8,128)S(1)}, f32[514,1]{1,0:T(8,128)S(1)}, u32[]{:S(2)}, u32[]{:S(2)}) collective-permute-start(f32[514,1]{1,0:T(8,128)S(1)} %get-tuple-element.14), channel_id=1, source_target_pairs={{0,1},{1,2},{2,3},{3,4},{4,5},{5,6},{6,7},{7,8},{8,9},{9,10},{10,1... | collective-permute-start | bytes 6176 | tf_op jit(solution)/shard_map/ppermute | solution.py:26
where the time goes:
time: 459 us; the launch traced here: 453 us
  blocking collectives  199 us (43%)
  local copies, waits for them, and re-layouts  98.4 us (21%)
  starting transfers between devices  59.6 us (13%)
  other arithmetic  48.6 us (11%)
  matrix products  21.8 us (5%)
  waiting for transfers between devices  19.8 us (4%)
  between operations  5.97 us (1%)
    psum x2, blocking collectives, squares(): return lax.psum(jnp.sum(residual * residual), ('row', 'col'))  131 us
    psum x1, blocking collectives, shards(): alpha = norm_now / lax.psum(jnp.sum(direction * image), ('row', 'col'))  67.8 us
    add x3, local copies, waits for them, and re-layouts, make_operator(): diagonal = weight_sum + LAM + row_edge + row_above + col_edge + col_before  27.4 us
    ppermute x6, starting transfers between devices, padded_2(): lax.ppermute(lax.slice_in_dim(block, block.shape[dim] - width, None, axis...  21.5 us
    reshape x2, local copies, waits for them, and re-layouts, to_tiles(): grid.reshape(grid_rows // tile_side, tile_side, grid_cols // tile_side, t...  19.6 us
    reshape x2, local copies, waits for them, and re-layouts, from_tiles(): tiles.reshape(grid_rows // tile_side, grid_cols // tile_side, tile_side,...  18.1 us
    ppermute x6, starting transfers between devices, padded_2(): lax.ppermute(lax.slice_in_dim(block, 0, width, axis=dim), axis, backward)  17.1 us
    reduce_sum x2, other arithmetic, shards(): alpha = norm_now / lax.psum(jnp.sum(direction * image), ('row', 'col'))  15.3 us
  transfers between devices with their start and end apart: 16, of which 7 were waited for; matrix products, arithmetic and copies ran while one was open for 27% of the time, Pallas kernels for 0%

commit v1 on v0

v1 whole, which is shorter than its diff:
```python
import functools

import jax
import jax.numpy as jnp
from jax import lax
from jax.experimental import pallas as pl
from jax.experimental.pallas import tpu as pltpu
from jax.sharding import PartitionSpec as P

TS = 32
GROUPS = 8
LAM = 0.05
HUBER = 0.5
META = 16
LANES = 128
F32 = jnp.float32
VMEM_LIMIT = 56 * 1024 * 1024


def lane_ids(shape):
    return lax.broadcasted_iota(jnp.int32, shape, len(shape) - 1)


def row_ids(shape):
    return lax.broadcasted_iota(jnp.int32, shape, len(shape) - 2)


def rows_up(block, below):
    count = block.shape[0]
    return jnp.where(row_ids(block.shape) == count - 1, below, pltpu.roll(block, count - 1, axis=0))


def rows_down(block, above):
    return jnp.where(row_ids(block.shape) == 0, above, pltpu.roll(block, 1, axis=0))


def cols_up(block, after):
    count = block.shape[1]
    rolled = pltpu.roll(block, count - 1, axis=1)
    tail = rolled[:, count - LANES :]
    tail = jnp.where(lane_ids(tail.shape) == LANES - 1, after, tail)
    if count == LANES:
        return tail
    return jnp.concatenate([rolled[:, : count - LANES], tail], axis=1)


def cols_down(block, before):
    rolled = pltpu.roll(block, 1, axis=1)
    head = rolled[:, :LANES]
    head = jnp.where(lane_ids(head.shape) == 0, before, head)
    if block.shape[1] == LANES:
        return head
    return jnp.concatenate([head, rolled[:, LANES:]], axis=1)


def swap_blocks(four):
    lane = lane_ids((8, LANES))
    low_half = lane < 64
    even = (lane & 32) == 0
    half = [None] * 4
    for q in range(2):
        a, b = four[q], four[q + 2]
        half[q] = jnp.where(low_half, a, pltpu.roll(b, 64, axis=1))
        half[q + 2] = jnp.where(low_half, pltpu.roll(a, 64, axis=1), b)
    out = [None] * 4
    for q in (0, 2):
        a, b = half[q], half[q + 1]
        out[q] = jnp.where(even, a, pltpu.roll(b, 32, axis=1))
        out[q + 1] = jnp.where(even, pltpu.roll(a, 96, axis=1), b)
    return out


def pack_kernel(
    owner_ref, count_ref, offset_ref, depth_hbm, conf_hbm, out_hbm,
    depth, conf, packed, blank, scratch, in_sems, blank_sems, out_sems,
):
    slots = out_hbm.shape[0]
    run = depth.shape[0] // GROUPS
    chunks = depth.shape[1] // LANES
    cells = run * chunks
    loads = []
    for g in range(GROUPS):
        part = pl.ds(g * run, run)
        for which, (source, target) in enumerate(((depth_hbm, depth), (conf_hbm, conf))):
            copy = pltpu.make_async_copy(source.at[part], target.at[part], in_sems.at[which, g])
            copy.start()
            loads.append(copy)
    blank[...] = jnp.zeros_like(blank)
    marks = []
    for s in range(slots):
        copy = pltpu.make_async_copy(
            blank, out_hbm.at[s, pl.ds(2 * cells, META)], blank_sems.at[s]
        )
        copy.start()
        marks.append(copy)
    rows = row_ids((META, LANES))
    count = count_ref[0, 0]
    for pair in range(GROUPS // 2):
        offsets = jnp.broadcast_to(offset_ref[:, pair * LANES : (pair + 1) * LANES], (META, LANES))
        high = (offsets >> 4).astype(F32)
        low = (offsets & 15).astype(F32)
        for side in range(2):
            g = 2 * pair + side
            if side:
                high, low = pltpu.roll(high, run, axis=1), pltpu.roll(low, run, axis=1)
            live = jnp.clip(count - g * run, 0, run).astype(F32)
            meta = jnp.where(rows == 0, high, jnp.where(rows == 1, low, jnp.where(rows == 2, live, 0.0)))
            packed[g, 2 * cells :, :] = meta.astype(jnp.bfloat16)
    for copy in marks:
        copy.wait()
    stores = []
    for g in range(GROUPS):
        for which, source in enumerate((depth, conf)):
            loads[2 * g + which].wait()
            for m in range(run // 16):
                buffer = scratch.at[(which * 4 + m) % scratch.shape[0]]
                block = source[g * run + 16 * m : g * run + 16 * m + 16, :].astype(F32)
                for c in range(chunks):
                    buffer[pl.ds(c, 16, stride=chunks), :] = block[:, c * LANES : (c + 1) * LANES]
                first = which * cells + m * 16 * chunks
                packed[g, first : first + 16 * chunks, :] = buffer[...].astype(jnp.bfloat16)
        copy = pltpu.make_async_copy(packed.at[g], out_hbm.at[owner_ref[0, g * run]], out_sems.at[g])
        copy.start()
        stores.append(copy)
    for copy in stores:
        copy.wait()


def pack(owners, offsets, count, depth, conf, slots):
    tiles, cells = depth.shape
    run = tiles // GROUPS
    rows = 2 * run * (cells // LANES) + META
    return pl.pallas_call(
        pack_kernel,
        out_shape=jax.ShapeDtypeStruct((slots, rows, LANES), jnp.bfloat16),
        in_specs=[
            pl.BlockSpec(memory_space=pltpu.SMEM),
            pl.BlockSpec(memory_space=pltpu.SMEM),
            pl.BlockSpec(memory_space=pltpu.VMEM),
            pl.BlockSpec(memory_space=pl.ANY),
            pl.BlockSpec(memory_space=pl.ANY),
        ],
        out_specs=pl.BlockSpec(memory_space=pl.ANY),
        scratch_shapes=[
            pltpu.VMEM((tiles, cells), jnp.bfloat16),
            pltpu.VMEM((tiles, cells), jnp.bfloat16),
            pltpu.VMEM((GROUPS, rows, LANES), jnp.bfloat16),
            pltpu.VMEM((META, LANES), jnp.bfloat16),
            pltpu.VMEM((8, 16 * (cells // LANES), LANES), F32),
            pltpu.SemaphoreType.DMA((2, GROUPS)),
            pltpu.SemaphoreType.DMA((slots,)),
            pltpu.SemaphoreType.DMA((GROUPS,)),
        ],
        compiler_params=pltpu.CompilerParams(vmem_limit_bytes=16 * 1024 * 1024),
        cost_estimate=pl.CostEstimate(flops=1 << 20, bytes_accessed=4 << 20, transcendentals=0),
        name="pack",
    )(owners, count, offsets, depth, conf)


def strips_kernel(top, bottom, kx_bottom, left, right, ky_right, up_out, down_out, left_out, right_out):
    up_out[...] = top[0:1, :]
    down_out[0:1, :] = bottom[7:8, :]
    down_out[1:2, :] = kx_bottom[7:8, :]
    lane = lane_ids(left.shape)
    left_out[...] = left[...].T[0:1, :]
    both = jnp.where(lane == LANES - 1, right[...], pltpu.roll(ky_right[...], LANES - 1, axis=1))
    turned = both.T
    right_out[0:1, :] = turned[LANES - 1 : LANES, :]
    right_out[1:2, :] = turned[LANES - 2 : LANES - 1, :]


def strips(prior, kx, ky):
    rows, cols = prior.shape
    last_rows = pl.BlockSpec((8, cols), lambda i: (rows // 8 - 1, 0))
    last_cols = pl.BlockSpec((rows, LANES), lambda i: (0, cols // LANES - 1))
    whole = lambda shape: pl.BlockSpec(shape, lambda i: (0, 0))
    shapes = ((1, cols), (2, cols), (1, rows), (2, rows))
    return pl.pallas_call(
        strips_kernel,
        grid=(1,),
        out_shape=[jax.ShapeDtypeStruct(s, F32) for s in shapes],
        in_specs=[
            whole((8, cols)), last_rows, last_rows, whole((rows, LANES)), last_cols, last_cols,
        ],
        out_specs=[whole(s) for s in shapes],
        name="strips",
    )(prior, prior, kx, prior, prior, ky)


def column_block(row):
    return jnp.broadcast_to(row, (LANES, row.shape[1])).T


def prepare_kernel(
    flags, prior, kx, ky, from_up, from_down, from_left, from_right,
    flow_out, diag_out, tiles_out, left_p, left_k, right_p, staging,
):
    rows, cols = prior.shape
    steps = rows // 8
    is_last_row, is_last_col = flags[0, 0] == 1, flags[0, 1] == 1
    left_p[...] = column_block(from_left[0:1, :])
    left_k[...] = column_block(from_left[1:2, :])
    own_edge = prior[:, cols - LANES :]
    own_edge = jnp.broadcast_to(own_edge[:, LANES - 1 :], (rows, LANES))
    right_p[...] = jnp.where(is_last_col, own_edge, column_block(from_right[0:1, :]))
    keep_col = jnp.where(is_last_col & (lane_ids((8, cols)) == cols - 1), 0.0, 1.0)

    def step(i, carry):
        above_flow, above_k = carry
        part = pl.ds(pl.multiple_of(i * 8, 8), 8)
        p, k, h = prior[part, :], kx[part, :], ky[part, :]
        following = prior[pl.ds(jnp.minimum(i * 8 + 8, rows - 1), 1), :]
        edge = jnp.where(is_last_row, prior[rows - 1 : rows, :], from_down[...])
        below = jnp.where(i == steps - 1, edge, following)
        down_flow = k * (rows_up(p, below) - p)
        right_flow = h * (cols_up(p, right_p[part, :]) - p)
        first_flow = left_k[part, :] * (p[:, :LANES] - left_p[part, :])
        first_flow = jnp.broadcast_to(first_flow[:, 0:1], (8, LANES))
        flow_out[part, :] = (
            (down_flow - rows_down(down_flow, above_flow))
            + (right_flow - cols_down(right_flow, first_flow))
        )
        last = (row_ids(k.shape) == 7) & (i == steps - 1) & is_last_row
        k = jnp.where(last, 0.0, k)
        h = h * keep_col
        diag_out[part, :] = (
            LAM + (k + rows_down(k, above_k)) + (h + cols_down(h, left_k[part, :]))
        )
        return down_flow[7:8, :], k[7:8, :]

    first = from_up[1:2, :]
    lax.fori_loop(0, steps, step, (first * (prior[0:1, :] - from_up[0:1, :]), first))

    def to_tiles(strip, carry):
        base = pl.multiple_of(strip * TS, TS)
        for b in range(cols // LANES):
            buffer = staging.at[b]
            buffer[...] = prior[pl.ds(base, TS), b * LANES : (b + 1) * LANES]
            four = swap_blocks([buffer[pl.ds(a, 8, stride=4), :] for a in range(4)])
            first_tile = strip * (cols // TS) + 4 * b
            for q in range(4):
                tiles_out[pl.ds(pl.multiple_of((first_tile + q) * 8, 8), 8), :] = four[q]
        return carry

    lax.fori_loop(0, rows // TS, to_tiles, 0)


def prepare(flags, prior, kx, ky, from_up, from_down, from_left, from_right):
    rows, cols = prior.shape
    vmem = pl.BlockSpec(memory_space=pltpu.VMEM)
    cells = rows * cols
    return pl.pallas_call(
        prepare_kernel,
        out_shape=[
            jax.ShapeDtypeStruct((rows, cols), F32),
            jax.ShapeDtypeStruct((rows, cols), F32),
            jax.ShapeDtypeStruct((cells // LANES, LANES), F32),
        ],
        in_specs=[pl.BlockSpec(memory_space=pltpu.SMEM)] + [vmem] * 7,
        out_specs=[vmem] * 3,
        scratch_shapes=[pltpu.VMEM((rows, LANES), F32)] * 3
        + [pltpu.VMEM((cols // LANES, TS, LANES), F32)],
        compiler_params=pltpu.CompilerParams(vmem_limit_bytes=24 * 1024 * 1024),
        cost_estimate=pl.CostEstimate(flops=20 * cells, bytes_accessed=24 * cells, transcendentals=0),
        name="prepare",
    )(flags, prior, kx, ky, from_up, from_down, from_left, from_right)


BANKS = 4
BATCH = 16


def join_kernel(
    got_hbm, prior_hbm, flow_hbm, diag_hbm, kx_top, ky_top, kx_bottom, ky_bottom,
    kx_left, ky_left, kx_right, ky_right,
    r_out, diag_out, up_out, down_out, left_out, right_out,
    got, prior, flow, diag, meta, table_v, table, staging, *rest,
):
    weights, pulls = rest[:BANKS], rest[BANKS : 2 * BANKS]
    got_sems, sems = rest[2 * BANKS], rest[2 * BANKS + 1]
    slots, rows_in = got_hbm.shape[0], got_hbm.shape[1]
    cells = (rows_in - META) // 2
    run = cells // 8
    rows, cols = r_out.shape
    meta_copy = pltpu.make_async_copy(
        got_hbm.at[:, pl.ds(2 * cells, META)], meta, sems.at[0]
    )
    meta_copy.start()
    prior_copy = pltpu.make_async_copy(prior_hbm, prior, sems.at[1])
    prior_copy.start()
    copies = []
    for s in range(slots):
        copy = pltpu.make_async_copy(
            got_hbm.at[s, pl.ds(0, 2 * cells)], got.at[s], got_sems.at[s]
        )
        copy.start()
        copies.append(copy)
    flow_copy = pltpu.make_async_copy(flow_hbm, flow, sems.at[2])
    flow_copy.start()
    diag_copy = pltpu.make_async_copy(diag_hbm, diag, sems.at[3])
    diag_copy.start()

    zero = jnp.zeros((TS, LANES), F32)

    def clear(i, carry):
        part = pl.ds(pl.multiple_of(i * TS, TS), TS)
        for bank in weights + pulls:
            bank[part, :] = zero
        return carry

    lax.fori_loop(0, rows * cols // LANES // TS, clear, 0)
    meta_copy.wait()
    for s in range(slots):
        fields = meta[s].astype(F32)
        target = fields[0:1, :] * 16.0 + fields[1:2, :]
        table_v[s, 0:1, :] = target.astype(jnp.int32)
        table_v[s, 1:2, :] = fields[2:3, :].astype(jnp.int32)
    table_copy = pltpu.make_async_copy(table_v, table, sems.at[4])
    table_copy.start()
    table_copy.wait()
    prior_copy.wait()

    for s in range(slots):
        copies[s].wait()
        live = table[s, 1, 0]

        def batch(step, carry, s=s, live=live):
            first = step * BATCH
            places, terms = [], []
            for pair in range(BATCH // 2):
                at = pl.multiple_of((first + 2 * pair) * 8, 16)
                depths = got[s, pl.ds(at, 16), :].astype(F32)
                confs = got[s, pl.ds(cells + at, 16), :].astype(F32) * HUBER
                for side in range(2):
                    tile = first + 2 * pair + side
                    place = pl.ds(pl.multiple_of(table[s, 0, tile] * 8, 8), 8)
                    error = depths[8 * side : 8 * side + 8] - prior[place, :]
                    weight = confs[8 * side : 8 * side + 8] / jnp.maximum(jnp.abs(error), HUBER)
                    weight = jnp.where(tile < live, weight, 0.0)
                    places.append(place)
                    terms.append((weight, weight * error))
            for k, (place, (weight, pull)) in enumerate(zip(places, terms)):
                weights[k % BANKS][place, :] += weight
                pulls[k % BANKS][place, :] += pull
            return carry

        lax.fori_loop(0, (live + BATCH - 1) // BATCH, batch, 0)

    flow_copy.wait()
    diag_copy.wait()

    def to_grid(strip, carry):
        base = pl.multiple_of(strip * TS, TS)
        for b in range(cols // LANES):
            place = pl.ds(pl.multiple_of((strip * (cols // TS) + 4 * b) * 8, TS), TS)
            lanes = slice(b * LANES, (b + 1) * LANES)
            for n, (banks, base_ref, out) in enumerate(
                ((weights, diag, diag_out), (pulls, flow, r_out))
            ):
                total = (banks[0][place, :] + banks[1][place, :]) + (
                    banks[2][place, :] + banks[3][place, :]
                )
                four = swap_blocks([total[8 * q : 8 * q + 8] for q in range(4)])
                buffer = staging.at[2 * b + n]
                for a in range(4):
                    buffer[pl.ds(a, 8, stride=4), :] = four[a]
                out[pl.ds(base, TS), lanes] = buffer[...] + base_ref[pl.ds(base, TS), lanes]
        return carry

    lax.fori_loop(0, rows // TS, to_grid, 0)

    zero_row = jnp.zeros((1, cols), F32)
    zero_cols = jnp.zeros((8, LANES), F32)

    def across(field, k):
        flow = k * field
        return k * cols_up(field, zero_cols) + cols_down(flow, zero_cols)

    top = r_out[0:8, :]
    image = diag_out[0:8, :] * top - kx_top[...] * rows_up(top, zero_row) - across(top, ky_top[...])
    up_out[0:1, :] = top[0:1, :]
    up_out[1:2, :] = image[0:1, :]
    low = r_out[rows - 8 : rows, :]
    image = (
        diag_out[rows - 8 : rows, :] * low
        - rows_down(kx_bottom[...] * low, zero_row)
        - across(low, ky_bottom[...])
    )
    down_out[0:1, :] = low[7:8, :]
    down_out[1:2, :] = image[7:8, :]
    zero_lane = jnp.zeros((1, LANES), F32)

    def along(field, d, k):
        return d * field - k * rows_up(field, zero_lane) - rows_down(k * field, zero_lane)

    lane = lane_ids((rows, LANES))
    side = r_out[:, 0:LANES]
    image = along(side, diag_out[:, 0:LANES], kx_left[...])
    image = image - ky_left[...] * pltpu.roll(side, LANES - 1, axis=1)
    turned = jnp.where(lane == 0, side, pltpu.roll(image, 1, axis=1)).T
    left_out[...] = turned[0:2, :]
    side = r_out[:, cols - LANES :]
    image = along(side, diag_out[:, cols - LANES :], kx_right[...])
    image = image - pltpu.roll(ky_right[...] * side, 1, axis=1)
    turned = jnp.where(lane == LANES - 1, side, pltpu.roll(image, LANES - 1, axis=1)).T
    right_out[0:1, :] = turned[LANES - 1 : LANES, :]
    right_out[1:2, :] = turned[LANES - 2 : LANES - 1, :]


def join(got, prior_tiles, flow, diag, kx, ky):
    rows, cols = flow.shape
    cells = rows * cols
    slots, rows_in, _ = got.shape
    whole = lambda shape: pl.BlockSpec(shape, lambda i: (0, 0))
    top, bottom = whole((8, cols)), pl.BlockSpec((8, cols), lambda i: (rows // 8 - 1, 0))
    left, right = whole((rows, LANES)), pl.BlockSpec((rows, LANES), lambda i: (0, cols // LANES - 1))
    shapes = ((rows, cols), (rows, cols), (2, cols), (2, cols), (2, rows), (2, rows))
    return pl.pallas_call(
        join_kernel,
        grid=(1,),
        out_shape=[jax.ShapeDtypeStruct(s, F32) for s in shapes],
        in_specs=[pl.BlockSpec(memory_space=pl.ANY)] * 4
        + [top, top, bottom, bottom, left, left, right, right],
        out_specs=[whole(s) for s in shapes],
        scratch_shapes=[
            pltpu.VMEM((slots, rows_in - META, LANES), jnp.bfloat16),
            pltpu.VMEM((cells // LANES, LANES), F32),
            pltpu.VMEM((rows, cols), F32),
            pltpu.VMEM((rows, cols), F32),
            pltpu.VMEM((slots, META, LANES), jnp.bfloat16),
            pltpu.VMEM((slots, 8, LANES), jnp.int32),
            pltpu.SMEM((slots, 8, LANES), jnp.int32),
            pltpu.VMEM((2 * cols // LANES, TS, LANES), F32),
        ]
        + [pltpu.VMEM((cells // LANES, LANES), F32)] * (2 * BANKS)
        + [pltpu.SemaphoreType.DMA((slots,)), pltpu.SemaphoreType.DMA((5,))],
        compiler_params=pltpu.CompilerParams(vmem_limit_bytes=VMEM_LIMIT),
        cost_estimate=pl.CostEstimate(flops=30 * cells, bytes_accessed=24 * cells, transcendentals=0),
        name="join",
    )(got, prior_tiles, flow, diag, kx, ky, kx, ky, kx, ky, kx, ky)


def add_pair(total, other):
    (a, rest_a), (b, rest_b) = total, other
    s = a + b
    back = s - a
    error = (a - (s - back)) + (b - back)
    return s, rest_a + rest_b + error


def fold(pair, axis):
    size = pair[0].shape[axis] // 2
    while size:
        other = tuple(pltpu.roll(part, size, axis=axis) for part in pair)
        pair = add_pair(pair, other)
        size //= 2
    return pair


def moments_kernel(
    flags, r_ref, diag_ref, kx_ref, ky_ref, r_up, r_down, r_left, r_right, k_up, k_left,
    q_out, s_out, table_out, left_r, left_k, left_q, right_r, right_q,
):
    rows, cols = r_ref.shape
    steps = rows // 8
    keep_row = jnp.where(flags[0, 0] == 1, 0.0, 1.0).astype(F32)
    keep_col = jnp.where(flags[0, 1] == 1, 0.0, 1.0).astype(F32)
    up_k = k_up[1:2, :]
    left_r[...] = column_block(r_left[0:1, :])
    left_k[...] = column_block(k_left[1:2, :])
    right_r[...] = column_block(r_right[0:1, :])
    edge_r = jnp.broadcast_to(r_ref[:, 0:1], (rows, LANES))
    left_q[...] = column_block(r_left[1:2, :]) - left_k[...] * edge_r
    own_flow = ky_ref[:, cols - LANES :] * r_ref[:, cols - LANES :]
    own_flow = jnp.broadcast_to(own_flow[:, LANES - 1 :], (rows, LANES))
    right_q[...] = (column_block(r_right[1:2, :]) - own_flow) * keep_col
    up_q = r_up[1:2, :] - up_k * r_ref[0:1, :]
    down_q = (r_down[1:2, :] - kx_ref[rows - 1 : rows, :] * r_ref[rows - 1 : rows, :]) * keep_row

    def operate(source, i, part, above_flow, below_edge, before, after):
        field = source[part, :]
        following = source[pl.ds(jnp.minimum(i * 8 + 8, rows - 1), 1), :]
        below = jnp.where(i == steps - 1, below_edge, following)
        k, h = kx_ref[part, :], ky_ref[part, :]
        row_flow = k * field
        col_flow = h * field
        entering = (left_k[part, :] * before[part, :])
        image = (
            diag_ref[part, :] * field
            - k * rows_up(field, below)
            - rows_down(row_flow, above_flow)
            - h * cols_up(field, after[part, :])
            - cols_down(col_flow, entering)
        )
        return field, image, row_flow[7:8, :]

    def folded(values):
        parts = [values[:, b * LANES : (b + 1) * LANES] for b in range(cols // LANES)]
        while len(parts) > 1:
            parts = [a + b for a, b in zip(parts[::2], parts[1::2])]
        return parts[0]

    def first(i, carry):
        above, m0, m1, m2 = carry
        part = pl.ds(pl.multiple_of(i * 8, 8), 8)
        field, image, above = operate(r_ref, i, part, above, r_down[0:1, :], left_r, right_r)
        q_out[part, :] = image
        return (
            above,
            m0 + folded(field * field),
            m1 + folded(field * image),
            m2 + folded(image * image),
        )

    zero = jnp.zeros((8, LANES), F32)
    _, m0, m1, m2 = lax.fori_loop(0, steps, first, (up_k * r_up[0:1, :], zero, zero, zero))

    def second(i, carry):
        above, m3 = carry
        part = pl.ds(pl.multiple_of(i * 8, 8), 8)
        field, image, above = operate(q_out, i, part, above, down_q, left_q, right_q)
        s_out[part, :] = image
        return above, m3 + folded(field * image)

    _, m3 = lax.fori_loop(0, steps, second, (up_k * up_q, zero))

    sums = []
    for m in (m0, m1, m2, m3):
        pair = fold((m, jnp.zeros_like(m)), 0)
        sums.append(fold(pair, 1))
    corners = ((0, 0), (0, cols - 1), (rows - 1, 0), (rows - 1, cols - 1))

    def cell(ref, i, j):
        block = ref[i // 8 * 8 : i // 8 * 8 + 8, j // LANES * LANES : j // LANES * LANES + LANES]
        return block[i % 8 : i % 8 + 1, j % LANES : j % LANES + 1]

    values = [value[0:1, 0:1] for value, _ in sums] + [rest[0:1, 0:1] for _, rest in sums]
    values += [cell(r_ref, i, j) for i, j in corners]
    values += [cell(q_out, i, j) for i, j in corners]
    values += [cell(kx_ref, i, j) * keep_row for i, j in corners[2:]]
    values += [cell(ky_ref, i, j) * keep_col for i, j in corners[1::2]]
    lane = lane_ids((1, LANES))
    row = jnp.zeros((1, LANES), F32)
    for place, value in enumerate(values):
        row = jnp.where(lane == place, jnp.broadcast_to(value, (1, LANES)), row)
    table_out[...] = jnp.broadcast_to(row, table_out.shape)


def moments(flags, r, diag, kx, ky, r_up, r_down, r_left, r_right, k_up, k_left, devices):
    rows, cols = r.shape
    vmem = pl.BlockSpec(memory_space=pltpu.VMEM)
    cells = rows * cols
    return pl.pallas_call(
        moments_kernel,
        out_shape=[
            jax.ShapeDtypeStruct((rows, cols), F32),
            jax.ShapeDtypeStruct((rows, cols), F32),
            jax.ShapeDtypeStruct((devices, LANES), F32),
        ],
        in_specs=[pl.BlockSpec(memory_space=pltpu.SMEM)] + [vmem] * 10,
        out_specs=[vmem] * 3,
        scratch_shapes=[pltpu.VMEM((rows, LANES), F32)] * 5,
        compiler_params=pltpu.CompilerParams(vmem_limit_bytes=24 * 1024 * 1024),
        cost_estimate=pl.CostEstimate(flops=40 * cells, bytes_accessed=24 * cells, transcendentals=0),
        name="moments",
    )(flags, r, diag, kx, ky, r_up, r_down, r_left, r_right, k_up, k_left)


def split(a):
    high = a * 4097.0
    high = high - (high - a)
    return high, a - high


def product(a, b):
    p = a * b
    a1, a2 = split(a)
    b1, b2 = split(b)
    return p, ((a1 * b1 - p) + a1 * b2 + a2 * b1) + a2 * b2


def quotient(top, bottom):
    q = top[0] / bottom[0]
    p, error = product(q, bottom[0])
    rest = ((top[0] - p) - error + top[1] - q * bottom[1]) / bottom[0]
    return q, rest


def finish_kernel(col_count, where_ref, table_ref, prior, r, q, s, height_out, residual_out, coeff):
    step = pl.program_id(0)
    steps = pl.num_programs(0)
    rows, cols = r.shape

    @pl.when(step == 0)
    def _():
        turned = table_ref[...].T
        devices = turned.shape[1]
        field = [turned[i : i + 1, :] for i in range(20)]

        def at(index, down, right):
            shift = -(down * col_count + right)
            return pltpu.roll(jnp.broadcast_to(field[index], (8, devices)), shift % devices, axis=1)

        r_tl, r_tr, r_bl, r_br = 8, 9, 10, 11
        kx_l, kx_r, ky_t, ky_b = 16, 17, 18, 19
        extra = [
            (at(kx_l, -1, 0) * at(ky_b, -1, -1) + at(ky_t, 0, -1) * at(kx_r, -1, -1)) * at(r_br, -1, -1),
            (at(kx_r, -1, 0) * at(ky_b, -1, 0) + at(ky_t, 0, 0) * at(kx_l, -1, 1)) * at(r_bl, -1, 1),
            (at(kx_l, 0, 0) * at(ky_t, 1, -1) + at(ky_b, 0, -1) * at(kx_r, 0, -1)) * at(r_tr, 1, -1),
            (at(kx_r, 0, 0) * at(ky_t, 1, 0) + at(ky_b, 0, 0) * at(kx_l, 0, 1)) * at(r_tl, 1, 1),
        ]
        pairs = [
            [jnp.broadcast_to(field[i], (8, devices)), jnp.broadcast_to(field[4 + i], (8, devices))]
            for i in range(4)
        ]
        for corner in range(4):
            pairs[3][1] = pairs[3][1] + extra[corner] * field[12 + corner]
        m = [fold(tuple(pair), 1) for pair in pairs]
        m = [tuple(part[0:1, 0:1] for part in pair) for pair in m]
        x1, x2, x3 = (quotient(m[i + 1], m[i]) for i in range(3))
        gap_1 = (x2[0] - x1[0]) + (x2[1] - x1[1])
        gap_2 = (x3[0] - x2[0]) + (x3[1] - x2[1])
        alpha = 1.0 / x1[0]
        ratio = 1.0 + gap_1 / x1[0]
        alpha_1 = gap_1 / (x2[0] * gap_2)
        mine = lane_ids((8, devices)) == where_ref[0, 2]
        values = [alpha + alpha_1 * ratio, alpha_1 * alpha]
        for corner in range(4):
            own = jnp.sum(jnp.where(mine, extra[corner], 0.0), axis=1, keepdims=True)
            values.append(own[0:1, 0:1])
        for i, value in enumerate(values):
            coeff[i] = jnp.broadcast_to(value, (8, LANES))

    one, two = coeff[0][0:1, 0:1], coeff[1][0:1, 0:1]
    height_out[...] = prior[...] + (one * r[...] - two * q[...])
    residual_out[...] = r[...] - (one * q[...] - two * s[...])

    def mend(corner, i, j):
        place = (slice(i // 8 * 8, i // 8 * 8 + 8), slice(j // LANES * LANES, j // LANES * LANES + LANES))
        here = (row_ids((8, LANES)) == i % 8) & (lane_ids((8, LANES)) == j % LANES)
        residual_out[place] += jnp.where(here, coeff[1] * coeff[2 + corner], 0.0)

    @pl.when(step == 0)
    def _():
        mend(0, 0, 0)
        mend(1, 0, cols - 1)

    @pl.when(step == steps - 1)
    def _():
        mend(2, rows - 1, 0)
        mend(3, rows - 1, cols - 1)


def finish(where, table, prior, r, q, s, col_count):
    rows, cols = r.shape
    block = pl.BlockSpec((64, cols), lambda i: (i, 0))
    cells = rows * cols
    return pl.pallas_call(
        functools.partial(finish_kernel, col_count),
        grid=(rows // 64,),
        out_shape=[jax.ShapeDtypeStruct((rows, cols), F32)] * 2,
        in_specs=[
            pl.BlockSpec(memory_space=pltpu.SMEM),
            pl.BlockSpec(table.shape, lambda i: (0, 0)),
        ]
        + [block] * 4,
        out_specs=[block] * 2,
        scratch_shapes=[pltpu.VMEM((8, 8, LANES), F32)],
        compiler_params=pltpu.CompilerParams(vmem_limit_bytes=16 * 1024 * 1024),
        cost_estimate=pl.CostEstimate(flops=8 * cells, bytes_accessed=24 * cells, transcendentals=0),
        name="finish",
    )(where, table, prior, r, q, s)


def send(strip, axis, by):
    count = lax.axis_size(axis)
    return lax.ppermute(
        strip, axis, [(i, i + by) for i in range(count) if 0 <= i + by < count]
    )


def exchange(up, down, left, right):
    return (
        send(down, "row", 1), send(up, "row", -1), send(right, "col", 1), send(left, "col", -1),
    )


def shards(
    depth_tiles, conf_tiles, tile_owner, tile_offset, tile_count, prior, edge_rows, edge_cols
):
    row, col = lax.axis_index("row"), lax.axis_index("col")
    row_count, col_count = lax.axis_size("row"), lax.axis_size("col")
    flags = jnp.stack(
        [row == row_count - 1, col == col_count - 1, row * col_count + col]
    ).astype(jnp.int32)[None]
    early = exchange(*strips(prior, edge_rows, edge_cols))
    payload = pack(tile_owner, tile_offset, tile_count, depth_tiles[0], conf_tiles[0], col_count)
    got = lax.all_to_all(payload, "col", split_axis=0, concat_axis=0, tiled=True)
    flow, diag_0, prior_tiles = prepare(flags, prior, edge_rows, edge_cols, *early)
    r, diag, *edges = join(got, prior_tiles, flow, diag_0, edge_rows, edge_cols)
    late = exchange(*edges)
    q, s, table = moments(
        flags, r, diag, edge_rows, edge_cols, *late, early[0], early[2], row_count * col_count
    )
    table = lax.all_to_all(table, ("row", "col"), split_axis=0, concat_axis=0, tiled=True)
    return tuple(finish(flags, table, prior, r, q, s, col_count))


def solution(mesh):
    return jax.shard_map(
        shards,
        mesh=mesh,
        in_specs=(
            P("row", "col", None),
            P("row", "col", None),
            P("row", "col"),
            P("row", "col"),
            P("row", "col"),
            P("row", "col"),
            P("row", "col"),
            P("row", "col"),
        ),
        out_specs=(P("row", "col"), P("row", "col")),
        check_vma=False,
    )
```

time: 459 us -> 179 us (0.39)
  blocking collectives: 199 us -> 21.3 us
  local copies, waits for them, and re-layouts: 98.4 us -> 16.2 us
  Pallas kernels: 0 us -> 52.7 us
  other arithmetic: 48.6 us -> 0.08 us
  waiting for transfers between devices: 19.8 us -> 50.8 us
  starting transfers between devices: 59.6 us -> 34.7 us
  matrix products: 21.8 us -> 0 us
    psum x3 -> x0, blocking collectives: 199 us -> none  [the longest x2 131 us: squares(): return lax.psum(jnp.sum(residual * residual), ('row', 'col'))]
    reshape x7 -> x0, local copies, waits for them, and re-layouts: 55.6 us -> none  [the longest x2 19.6 us: to_tiles(): grid.reshape(grid_rows // tile_side, tile_side, grid_cols // tile_side, t...]
    pallas_call x0 -> x6, Pallas kernels: none -> 52.7 us  [the longest x1 13.8 us: prepare(): pl.pallas_call(prepare_kernel, out_shape=[jax.ShapeDtypeStruct((rows, col...]
    ppermute x14 -> x8, waiting for transfers between devices: 13.4 us -> 50.8 us  [send(): lax.ppermute(strip, axis, [(i, i + by) for i in range(count) if 0 <= i +...]
    add x3 -> x0, local copies, waits for them, and re-layouts: 27.4 us -> none  [make_operator(): diagonal = weight_sum + LAM + row_edge + row_above + col_edge + col_before]
    dot_general x3 -> x0, matrix products: 21.8 us -> none  [the longest x1 10 us: shards(): prior_at = jnp.dot(matches, prior_tiles, precision=lax.Precision.HIGHEST)]
    all_to_all x0 -> x1, blocking collectives: none -> 21.3 us  [shards(): lax.all_to_all(table, ('row', 'col'), split_axis=0, concat_axis=0, tiled=...]
    reduce_sum x5 -> x0, other arithmetic: 19.6 us -> none  [the longest x2 15.3 us: shards(): alpha = norm_now / lax.psum(jnp.sum(direction * image), ('row', 'col'))]
  transfers between devices with their start and end apart: 16 -> 9, of which waited for: 7 -> 2; matrix products, arithmetic and copies ran while one was open for 27% -> 0% of each run, Pallas kernels for 0% -> 9%
where the time goes in v1:
time: 179 us; the launch traced here: 177 us
  Pallas kernels  52.7 us (29%)
  waiting for transfers between devices  50.8 us (28%)
  starting transfers between devices  34.7 us (19%)
  blocking collectives  21.3 us (12%)
  local copies, waits for them, and re-layouts  16.2 us (9%)
    ppermute x8, waiting for transfers between devices, send(): lax.ppermute(strip, axis, [(i, i + by) for i in range(count) if 0 <= i +...  50.8 us
    ppermute x8, starting transfers between devices, send(): lax.ppermute(strip, axis, [(i, i + by) for i in range(count) if 0 <= i +...  26.1 us
    all_to_all x1, blocking collectives, shards(): lax.all_to_all(table, ('row', 'col'), split_axis=0, concat_axis=0, tiled=...  21.3 us
    unnamed x32, local copies, waits for them, and re-layouts  16.2 us
    pallas_call x1, Pallas kernels, prepare(): pl.pallas_call(prepare_kernel, out_shape=[jax.ShapeDtypeStruct((rows, col...  13.8 us
    pallas_call x1, Pallas kernels, moments(): pl.pallas_call(moments_kernel, out_shape=[jax.ShapeDtypeStruct((rows, col...  13.6 us
    pallas_call x1, Pallas kernels, join(): pl.pallas_call(join_kernel, grid=(1,), out_shape=[jax.ShapeDtypeStruct(s,...  12.9 us
    all_to_all x1, starting transfers between devices, shards(): lax.all_to_all(payload, 'col', split_axis=0, concat_axis=0, tiled=True)  8.64 us
  transfers between devices with their start and end apart: 9, of which 2 were waited for; matrix products, arithmetic and copies ran while one was open for 0% of the time, Pallas kernels for 9%

profile of v1, /device:TPU:1, one launch (start us, length us, event | category | flops | bytes accessed | tf_op | source)
XLA Modules:
  0.0 177.2 jit_solution(15875397581785217822)
XLA Ops:
  1.3 0.0 copy-start.12
  1.3 1.2 copy-done.12
  2.5 0.0 copy-start.13
  2.5 1.2 copy-done.13
  3.7 0.0 copy-start.14
  3.7 0.7 copy-done.14
  4.4 0.0 copy-start.15
  4.4 0.7 copy-done.15
  5.1 4.8 %pack.1 = bf16[16,1040,128]{2,1,0:T(8,128)(2,1)S(1)} custom-call(s32[1,512]{1,0:T(1,128)S(1)} %copy-done.14, s32[1,1]{1,0:T(1,128)S(6)} %copy.11.count_ref, s32[1,512]{1,0:T(1,128)S(1)} %copy-done.15, bf16[512,1024]{1,0:T(8,128)(2,1)S(1)} %bitcast.11, bf16[512,1024]{1,0:T(8,128)(2,1)S(1)} %bitcast.12), custom_call_target="tpu_custom_call" | custom-call | flops 1048576 | bytes 4194304 | tf_op jit(solution)/shard_map/pack/pallas_call | solution.py:133
  9.9 0.0 copy-start.6
  10.0 2.0 %copy-done.6 = bf16[16,1040,128]{2,1,0:T(8,128)(2,1)} copy-done((bf16[16,1040,128]{2,1,0:T(8,128)(2,1)}, bf16[16,1040,128]{2,1,0:T(8,128)(2,1)S(1)}, u32[]{:S(2)}) %copy-start.6) | copy-done | bytes 4259864
  12.0 8.6 %all-to-all-start = ((bf16[16,1040,128]{2,1,0:T(8,128)(2,1)}), bf16[16,1040,128]{2,1,0:T(8,128)(2,1)}, u32[]{:S(2)}, u32[]{:S(2)}) async-start(bf16[16,1040,128]{2,1,0:T(8,128)(2,1)} %copy-done.6), calls=%async_computation | async-start | bytes 8519680 | tf_op jit(solution)/shard_map/all_to_all | solution.py:698
  20.6 0.0 copy-start
  20.6 2.2 %strips.1 = (f32[1,1024]{1,0:T(1,128)}, f32[2,1024]{1,0:T(2,128)}, f32[1,512]{1,0:T(1,128)}, f32[2,512]{1,0:T(2,128)}) custom-call(f32[512,1024]{1,0:T(8,128)} %prior.3, f32[512,1024]{1,0:T(8,128)} %prior.3, f32[512,1024]{1,0:T(8,128)} %kx_ref.1, f32[512,1024]{1,0:T(8,128)} %prior.3, f32[512,1024]{1,0:T(8,128)} %prior.3, f32[512,1024]{1,0:T(8,128)} %ky_ref.1), custom_call_target="tpu_custom_call" | custom-call | tf_op jit(solution)/shard_map/strips/pallas_call | solution.py:178
  22.9 1.3 collective-permute-start.3
  24.1 2.9 %collective-permute-start.1 = (f32[1,1024]{1,0:T(1,128)}, f32[1,1024]{1,0:T(1,128)S(1)}, u32[]{:S(2)}, u32[]{:S(2)}) collective-permute-start(f32[1,1024]{1,0:T(1,128)} %get-tuple-element.19), channel_id=1, source_target_pairs={{16,0},{32,16},{48,32},{64,48},{80,64},{96,80},{112,96},{17,1},{33... | collective-permute-start | bytes 12296 | tf_op jit(solution)/shard_map/ppermute | solution.py:677
  27.0 4.3 %collective-permute-start.2 = (f32[2,512]{1,0:T(2,128)}, f32[2,512]{1,0:T(2,128)S(1)}, u32[]{:S(2)}, u32[]{:S(2)}) collective-permute-start(f32[2,512]{1,0:T(2,128)} %get-tuple-element.20), channel_id=1, source_target_pairs={{0,1},{1,2},{2,3},{3,4},{4,5},{5,6},{6,7},{7,8},{8,9},{9,10},{10,1... | collective-permute-start | bytes 12296 | tf_op jit(solution)/shard_map/ppermute | solution.py:677
  31.3 3.3 %collective-permute-start = (f32[2,1024]{1,0:T(2,128)}, f32[2,1024]{1,0:T(2,128)S(1)}, u32[]{:S(2)}, u32[]{:S(2)}) collective-permute-start(f32[2,1024]{1,0:T(2,128)} %get-tuple-element.18), channel_id=1, source_target_pairs={{0,16},{16,32},{32,48},{48,64},{64,80},{80,96},{96,112},{1,17},{17... | collective-permute-start | bytes 24584 | tf_op jit(solution)/shard_map/ppermute | solution.py:677
  34.6 0.1 add_bitcast_fusion.flags.where_ref
  34.7 47.6 %collective-permute-done.3.from_right = f32[1,512]{1,0:T(1,128)S(1)} collective-permute-done((f32[1,512]{1,0:T(1,128)}, f32[1,512]{1,0:T(1,128)S(1)}, u32[]{:S(2)}, u32[]{:S(2)}) %collective-permute-start.3) | collective-permute-done | bytes 2080 | tf_op jit(solution)/shard_map/ppermute | solution.py:677
  82.2 0.0 collective-permute-done.1.from_down
  82.2 0.0 collective-permute-done.2.from_left.k_left
  82.2 0.0 collective-permute-done.from_up.k_up
  82.3 0.0 copy-done
  82.3 0.0 copy-start.2
  82.3 1.6 copy-done.2
  83.9 0.0 copy-start.4
  83.9 1.6 copy-done.4
  85.4 13.8 %prepare.1 = (f32[512,1024]{1,0:T(8,128)S(1)}, f32[512,1024]{1,0:T(8,128)S(1)}, f32[4096,128]{1,0:T(8,128)S(1)}) custom-call(s32[1,3]{1,0:T(1,128)S(1)} %add_bitcast_fusion.flags.where_ref, f32[512,1024]{1,0:T(8,128)S(1)} %copy-done.4, f32[512,1024]{1,0:T(8,128)S(1)} %copy-done, f32[512,1024]{1,0:T(8,128)S(1)} %copy-done.2, ...), custom_call_target="tpu_custom_call" | custom-call | flops 10485760 | bytes 12582912 | tf_op jit(solution)/shard_map/prepare/pallas_call | solution.py:252
  99.2 0.0 copy-start.9
  99.2 1.3 copy-done.9
  100.5 0.0 copy-start.10
  100.5 1.4 copy-done.10
  101.9 0.0 copy-start.11
  101.9 1.3 copy-done.11
  103.2 0.0 all-to-all-done.got_hbm
  103.2 0.0 copy-start.1
  103.2 0.0 copy-start.3
  103.2 12.9 %join.1 = (f32[512,1024]{1,0:T(8,128)}, f32[512,1024]{1,0:T(8,128)}, f32[2,1024]{1,0:T(2,128)}, f32[2,1024]{1,0:T(2,128)}, f32[2,512]{1,0:T(2,128)}, /*index=5*/f32[2,512]{1,0:T(2,128)}) custom-call(bf16[16,1040,128]{2,1,0:T(8,128)(2,1)} %all-to-all-done.got_hbm, f32[4096,128]{1,0:T(8,128)} %copy-done.11, f32[512,1024]{1,0:T(8,128)} %copy-done.9, ...), custom_call_target="tpu_custom_call" | custom-call | flops 15728640 | bytes 12582912 | tf_op jit(solution)/shard_map/join/pallas_call | solution.py:418
  116.2 6.1 %collective-permute-start.4 = (f32[2,1024]{1,0:T(2,128)}, f32[2,1024]{1,0:T(2,128)S(1)}, u32[]{:S(2)}, u32[]{:S(2)}) collective-permute-start(f32[2,1024]{1,0:T(2,128)} %get-tuple-element.27), channel_id=1, source_target_pairs={{0,16},{16,32},{32,48},{48,64},{64,80},{80,96},{96,112},{1,17},{17... | collective-permute-start | bytes 24584 | tf_op jit(solution)/shard_map/ppermute | solution.py:677
  122.3 1.9 %collective-permute-start.5 = (f32[2,1024]{1,0:T(2,128)}, f32[2,1024]{1,0:T(2,128)S(1)}, u32[]{:S(2)}, u32[]{:S(2)}) collective-permute-start(f32[2,1024]{1,0:T(2,128)} %get-tuple-element.28), channel_id=1, source_target_pairs={{16,0},{32,16},{48,32},{64,48},{80,64},{96,80},{112,96},{17,1},{33... | collective-permute-start | bytes 24584 | tf_op jit(solution)/shard_map/ppermute | solution.py:677
  124.2 5.0 %collective-permute-start.6 = (f32[2,512]{1,0:T(2,128)}, f32[2,512]{1,0:T(2,128)S(1)}, u32[]{:S(2)}, u32[]{:S(2)}) collective-permute-start(f32[2,512]{1,0:T(2,128)} %get-tuple-element.29), channel_id=1, source_target_pairs={{0,1},{1,2},{2,3},{3,4},{4,5},{5,6},{6,7},{7,8},{8,9},{9,10},{10,1... | collective-permute-start | bytes 12296 | tf_op jit(solution)/shard_map/ppermute | solution.py:677
  129.3 1.3 collective-permute-start.7
  130.6 0.0 collective-permute-done.6.r_left
  130.6 3.3 %collective-permute-done.7.r_right = f32[2,512]{1,0:T(2,128)S(1)} collective-permute-done((f32[2,512]{1,0:T(2,128)}, f32[2,512]{1,0:T(2,128)S(1)}, u32[]{:S(2)}, u32[]{:S(2)}) %collective-permute-start.7) | collective-permute-done | bytes 4128 | tf_op jit(solution)/shard_map/ppermute | solution.py:677
  133.8 0.0 collective-permute-done.4.r_up
  133.8 0.0 collective-permute-done.5.r_down
  133.8 0.0 copy-done.1
  133.8 0.0 copy-done.3
  133.8 0.0 copy-start.7
  133.9 1.6 copy-done.7
  135.4 0.0 copy-start.8
  135.4 1.6 copy-done.8
  137.0 0.0 copy-start.5
  137.0 13.6 %moments.1 = (f32[512,1024]{1,0:T(8,128)S(1)}, f32[512,1024]{1,0:T(8,128)S(1)}, f32[128,128]{1,0:T(8,128)S(1)}) custom-call(s32[1,3]{1,0:T(1,128)S(1)} %add_bitcast_fusion.flags.where_ref, f32[512,1024]{1,0:T(8,128)S(1)} %copy-done.7, f32[512,1024]{1,0:T(8,128)S(1)} %copy-done.8, f32[512,1024]{1,0:T(8,128)S(1)} %copy-done.1, f32[512,1024]{1,0:T(8,128)S(1)} %copy-done.3, ...), custom_call_target="tpu_custom_call" | custom-call | flops 20971520 | bytes 12582912 | tf_op jit(solution)/shard_map/moments/pallas_call | solution.py:553
  150.6 21.3 %all_to_all.16 = f32[128,1,128]{2,1,0:T(1,128)S(1)} all-to-all(f32[128,1,128]{2,1,0:T(1,128)S(1)} %bitcast.14), channel_id=1, replica_groups=mesh['row'=8,'col'=16] {'row','col'}, dimensions={0} | all-to-all | bytes 131072 | tf_op jit(solution)/shard_map/all_to_all | solution.py:705
  171.9 0.0 copy-done.5
  171.9 5.4 %finish.1 = (f32[512,1024]{1,0:T(8,128)}, f32[512,1024]{1,0:T(8,128)}) custom-call(s32[1,3]{1,0:T(1,128)S(1)} %add_bitcast_fusion.flags.where_ref, f32[128,128]{1,0:T(8,128)S(1)} %bitcast.13, f32[512,1024]{1,0:T(8,128)S(1)} %copy-done.5, f32[512,1024]{1,0:T(8,128)S(1)} %copy-done.7, f32[512,1024]{1,0:T(8,128)S(1)} %get-tuple-element.32.q, ...), custom_call_target="tpu_custom_call" | custom-call | flops 4194304 | bytes 12582912 | tf_op jit(solution)/shard_map/finish/pallas_call | solution.py:658
Async XLA Ops:
  1.3 1.2 copy-start.12
  2.5 1.2 copy-start.13
  3.7 0.7 copy-start.14
  4.4 0.7 copy-start.15
  9.9 2.0 %copy-start.6 = (bf16[16,1040,128]{2,1,0:T(8,128)(2,1)}, bf16[16,1040,128]{2,1,0:T(8,128)(2,1)S(1)}, u32[]{:S(2)}) copy-start(bf16[16,1040,128]{2,1,0:T(8,128)(2,1)S(1)} %pack.1) | copy-start | bytes 12779524
  12.0 91.3 %all-to-all-start = ((bf16[16,1040,128]{2,1,0:T(8,128)(2,1)}), bf16[16,1040,128]{2,1,0:T(8,128)(2,1)}, u32[]{:S(2)}, u32[]{:S(2)}) async-start(bf16[16,1040,128]{2,1,0:T(8,128)(2,1)} %copy-done.6), calls=%async_computation | async-start | bytes 8519680 | tf_op jit(solution)/shard_map/all_to_all | solution.py:698
  20.6 61.6 %copy-start = (f32[512,1024]{1,0:T(8,128)S(1)}, f32[512,1024]{1,0:T(8,128)}, u32[]{:S(2)}) copy-start(f32[512,1024]{1,0:T(8,128)} %kx_ref.1) | copy-start | bytes 6291460
  22.9 59.4 %collective-permute-start.3 = (f32[1,512]{1,0:T(1,128)}, f32[1,512]{1,0:T(1,128)S(1)}, u32[]{:S(2)}, u32[]{:S(2)}) collective-permute-start(f32[1,512]{1,0:T(1,128)} %get-tuple-element.21), channel_id=1, source_target_pairs={{1,0},{2,1},{3,2},{4,3},{5,4},{6,5},{7,6},{8,7},{9,8},{10,9},{11,1... | collective-permute-start | bytes 6152 | tf_op jit(solution)/shard_map/ppermute | solution.py:677
  24.1 58.1 %collective-permute-start.1 = (f32[1,1024]{1,0:T(1,128)}, f32[1,1024]{1,0:T(1,128)S(1)}, u32[]{:S(2)}, u32[]{:S(2)}) collective-permute-start(f32[1,1024]{1,0:T(1,128)} %get-tuple-element.19), channel_id=1, source_target_pairs={{16,0},{32,16},{48,32},{64,48},{80,64},{96,80},{112,96},{17,1},{33... | collective-permute-start | bytes 12296 | tf_op jit(solution)/shard_map/ppermute | solution.py:677
  27.0 55.2 %collective-permute-start.2 = (f32[2,512]{1,0:T(2,128)}, f32[2,512]{1,0:T(2,128)S(1)}, u32[]{:S(2)}, u32[]{:S(2)}) collective-permute-start(f32[2,512]{1,0:T(2,128)} %get-tuple-element.20), channel_id=1, source_target_pairs={{0,1},{1,2},{2,3},{3,4},{4,5},{5,6},{6,7},{7,8},{8,9},{9,10},{10,1... | collective-permute-start | bytes 12296 | tf_op jit(solution)/shard_map/ppermute | solution.py:677
  31.3 51.0 %collective-permute-start = (f32[2,1024]{1,0:T(2,128)}, f32[2,1024]{1,0:T(2,128)S(1)}, u32[]{:S(2)}, u32[]{:S(2)}) collective-permute-start(f32[2,1024]{1,0:T(2,128)} %get-tuple-element.18), channel_id=1, source_target_pairs={{0,16},{16,32},{32,48},{48,64},{64,80},{80,96},{96,112},{1,17},{17... | collective-permute-start | bytes 24584 | tf_op jit(solution)/shard_map/ppermute | solution.py:677
  82.3 1.6 copy-start.2
  83.9 1.6 copy-start.4
  99.2 1.3 copy-start.9
  100.5 1.4 copy-start.10
  101.9 1.3 copy-start.11
  103.2 30.6 %copy-start.1 = (f32[512,1024]{1,0:T(8,128)S(1)}, f32[512,1024]{1,0:T(8,128)}, u32[]{:S(2)}) copy-start(f32[512,1024]{1,0:T(8,128)} %kx_ref.1) | copy-start | bytes 6291460
  103.2 30.6 %copy-start.3 = (f32[512,1024]{1,0:T(8,128)S(1)}, f32[512,1024]{1,0:T(8,128)}, u32[]{:S(2)}) copy-start(f32[512,1024]{1,0:T(8,128)} %ky_ref.1) | copy-start | bytes 6291460
  116.2 17.6 %collective-permute-start.4 = (f32[2,1024]{1,0:T(2,128)}, f32[2,1024]{1,0:T(2,128)S(1)}, u32[]{:S(2)}, u32[]{:S(2)}) collective-permute-start(f32[2,1024]{1,0:T(2,128)} %get-tuple-element.27), channel_id=1, source_target_pairs={{0,16},{16,32},{32,48},{48,64},{64,80},{80,96},{96,112},{1,17},{17... | collective-permute-start | bytes 24584 | tf_op jit(solution)/shard_map/ppermute | solution.py:677
  122.3 11.5 %collective-permute-start.5 = (f32[2,1024]{1,0:T(2,128)}, f32[2,1024]{1,0:T(2,128)S(1)}, u32[]{:S(2)}, u32[]{:S(2)}) collective-permute-start(f32[2,1024]{1,0:T(2,128)} %get-tuple-element.28), channel_id=1, source_target_pairs={{16,0},{32,16},{48,32},{64,48},{80,64},{96,80},{112,96},{17,1},{33... | collective-permute-start | bytes 24584 | tf_op jit(solution)/shard_map/ppermute | solution.py:677
  124.2 6.3 %collective-permute-start.6 = (f32[2,512]{1,0:T(2,128)}, f32[2,512]{1,0:T(2,128)S(1)}, u32[]{:S(2)}, u32[]{:S(2)}) collective-permute-start(f32[2,512]{1,0:T(2,128)} %get-tuple-element.29), channel_id=1, source_target_pairs={{0,1},{1,2},{2,3},{3,4},{4,5},{5,6},{6,7},{7,8},{8,9},{9,10},{10,1... | collective-permute-start | bytes 12296 | tf_op jit(solution)/shard_map/ppermute | solution.py:677
  129.3 4.6 %collective-permute-start.7 = (f32[2,512]{1,0:T(2,128)}, f32[2,512]{1,0:T(2,128)S(1)}, u32[]{:S(2)}, u32[]{:S(2)}) collective-permute-start(f32[2,512]{1,0:T(2,128)} %get-tuple-element.30), channel_id=1, source_target_pairs={{1,0},{2,1},{3,2},{4,3},{5,4},{6,5},{7,6},{8,7},{9,8},{10,9},{11,1... | collective-permute-start | bytes 12296 | tf_op jit(solution)/shard_map/ppermute | solution.py:677
  133.8 1.6 copy-start.7
  135.4 1.6 copy-start.8
  137.0 34.8 %copy-start.5 = (f32[512,1024]{1,0:T(8,128)S(1)}, f32[512,1024]{1,0:T(8,128)}, u32[]{:S(2)}) copy-start(f32[512,1024]{1,0:T(8,128)} %prior.3) | copy-start | bytes 6291460

commit v2 on v0

v2 whole, which is shorter than its diff:
```python
import functools

import jax
import jax.numpy as jnp
from jax import lax
from jax.experimental import pallas as pl
from jax.experimental.pallas import tpu as pltpu
from jax.sharding import PartitionSpec as P

TS = 32
GROUPS = 8
LAM = 0.05
HUBER = 0.5
META = 16
LANES = 128
PAD = 8
F32 = jnp.float32
SMALL_VMEM = 20 * 1024 * 1024


def lane_ids(shape):
    return lax.broadcasted_iota(jnp.int32, shape, len(shape) - 1)


def row_ids(shape):
    return lax.broadcasted_iota(jnp.int32, shape, len(shape) - 2)


def cols_up(parts, after):
    rolled = [pltpu.roll(x, LANES - 1, axis=1) for x in parts] + [after]
    last = lane_ids(parts[0].shape) == LANES - 1
    return [jnp.where(last, rolled[b + 1], rolled[b]) for b in range(len(parts))]


def cols_down(parts, before):
    rolled = [before] + [pltpu.roll(x, 1, axis=1) for x in parts]
    first = lane_ids(parts[0].shape) == 0
    return [jnp.where(first, rolled[b], rolled[b + 1]) for b in range(len(parts))]


def side_columns(first, last):
    shape = (LANES, first.shape[1])
    rows = row_ids(shape)
    return jnp.where(rows == 0, first, jnp.where(rows == LANES - 1, last, 0.0)).T


def at_row(i, shift=0):
    if shift:
        return pl.ds(PAD + 8 * i + shift, 8)
    return pl.ds(pl.multiple_of(PAD + 8 * i, 8), 8)


def swap_blocks(four):
    lane = lane_ids(four[0].shape)
    low_half = lane < 64
    even = (lane & 32) == 0
    half = [None] * 4
    for q in range(2):
        a, b = four[q], four[q + 2]
        half[q] = jnp.where(low_half, a, pltpu.roll(b, 64, axis=1))
        half[q + 2] = jnp.where(low_half, pltpu.roll(a, 64, axis=1), b)
    out = [None] * 4
    for q in (0, 2):
        a, b = half[q], half[q + 1]
        out[q] = jnp.where(even, a, pltpu.roll(b, 32, axis=1))
        out[q + 1] = jnp.where(even, pltpu.roll(a, 96, axis=1), b)
    return out


def pack_kernel(owner_ref, count_ref, offset_ref, depth, conf, out, scratch):
    slots = out.shape[0]
    run = depth.shape[0] // GROUPS
    chunks = depth.shape[1] // LANES
    cells = run * chunks
    blank = jnp.zeros((META, LANES), jnp.bfloat16)
    for s in range(slots):
        out[s, 2 * cells :, :] = blank
    rows = row_ids((META, LANES))
    count = count_ref[0, 0]
    for pair in range(GROUPS // 2):
        offsets = jnp.broadcast_to(offset_ref[:, pair * LANES : (pair + 1) * LANES], (META, LANES))
        high = (offsets >> 4).astype(F32)
        low = (offsets & 15).astype(F32)
        for side in range(2):
            g = 2 * pair + side
            if side:
                high, low = pltpu.roll(high, run, axis=1), pltpu.roll(low, run, axis=1)
            live = jnp.clip(count - g * run, 0, run).astype(F32)
            meta = jnp.where(rows == 0, high, jnp.where(rows == 1, low, jnp.where(rows == 2, live, 0.0)))
            out[owner_ref[0, g * run], 2 * cells :, :] = meta.astype(jnp.bfloat16)

    def one_run(g, carry):
        slot = owner_ref[0, g * run]
        for which, source in enumerate((depth, conf)):
            for m in range(run // 16):
                buffer = scratch.at[which * (run // 16) + m]
                block = source[pl.ds(pl.multiple_of(g * run + 16 * m, 16), 16), :].astype(F32)
                if which:
                    tile = row_ids(block.shape) + (g * run + 16 * m)
                    block = jnp.where(tile < count, block * HUBER, 0.0)
                for c in range(chunks):
                    buffer[pl.ds(c, 16, stride=chunks), :] = block[:, c * LANES : (c + 1) * LANES]
                first = which * cells + m * 16 * chunks
                out[slot, first : first + 16 * chunks, :] = buffer[...].astype(jnp.bfloat16)
        return carry

    lax.fori_loop(0, GROUPS, one_run, 0)


def pack(owners, offsets, count, depth, conf, slots):
    tiles, cells = depth.shape
    run = tiles // GROUPS
    rows = 2 * run * (cells // LANES) + META
    vmem = pl.BlockSpec(memory_space=pltpu.VMEM)
    smem = pl.BlockSpec(memory_space=pltpu.SMEM)
    return pl.pallas_call(
        pack_kernel,
        out_shape=jax.ShapeDtypeStruct((slots, rows, LANES), jnp.bfloat16),
        in_specs=[smem, smem, vmem, vmem, vmem],
        out_specs=vmem,
        scratch_shapes=[pltpu.VMEM((2 * run // 16, 16 * (cells // LANES), LANES), F32)],
        compiler_params=pltpu.CompilerParams(vmem_limit_bytes=SMALL_VMEM),
        cost_estimate=pl.CostEstimate(flops=1 << 20, bytes_accessed=4 << 20, transcendentals=0),
        name="pack",
    )(owners, count, offsets, depth, conf)


def strips_kernel(top, bottom, kx_bottom, left, right, ky_right, up_out, down_out, left_out, right_out):
    up_out[...] = top[0:1, :]
    down_out[0:1, :] = bottom[7:8, :]
    down_out[1:2, :] = kx_bottom[7:8, :]
    lane = lane_ids(left.shape)
    left_out[...] = left[...].T[0:1, :]
    both = jnp.where(lane == LANES - 1, right[...], pltpu.roll(ky_right[...], LANES - 1, axis=1))
    turned = both.T
    right_out[0:1, :] = turned[LANES - 1 : LANES, :]
    right_out[1:2, :] = turned[LANES - 2 : LANES - 1, :]


def strips(prior, kx, ky):
    rows, cols = prior.shape
    last_rows = pl.BlockSpec((8, cols), lambda i: (rows // 8 - 1, 0))
    last_cols = pl.BlockSpec((rows, LANES), lambda i: (0, cols // LANES - 1))
    whole = lambda shape: pl.BlockSpec(shape, lambda i: (0, 0))
    shapes = ((1, cols), (2, cols), (1, rows), (2, rows))
    return pl.pallas_call(
        strips_kernel,
        grid=(1,),
        out_shape=[jax.ShapeDtypeStruct(s, F32) for s in shapes],
        in_specs=[
            whole((8, cols)), last_rows, last_rows, whole((rows, LANES)), last_cols, last_cols,
        ],
        out_specs=[whole(s) for s in shapes],
        name="strips",
    )(prior, prior, kx, prior, prior, ky)


BATCH = 16
UF = 4
US = 16
UM = 8


def join_kernel(
    flags, got, prior_in, kx_in, ky_in, from_up, from_down, from_left, from_right,
    r_out, diag_out, kx, ky, up_out, down_out, left_out, right_out,
    prior, table_v, table, tiles, weights, pulls, side_p, left_k, table_sem,
):
    slots, rows_in = got.shape[0], got.shape[1]
    cells = (rows_in - META) // 2
    blocks, rows = diag_out.shape[0], diag_out.shape[1]
    steps = rows // 8
    for s in range(slots):
        fields = got[s, 2 * cells :, :].astype(F32)
        target = fields[0:1, :] * 128.0 + fields[1:2, :] * 8.0
        table_v[s, 0:1, :] = target.astype(jnp.int32)
        table_v[s, 1:2, :] = fields[2:3, :].astype(jnp.int32)
    table_copy = pltpu.make_async_copy(table_v, table, table_sem)
    table_copy.start()

    zero = jnp.zeros((TS, LANES), F32)

    def clear(i, carry):
        part = pl.ds(pl.multiple_of(i * TS, TS), TS)
        weights[part, :] = zero
        pulls[part, :] = zero
        return carry

    lax.fori_loop(0, rows * blocks // TS, clear, 0)
    side_p[...] = side_columns(from_left[0:1, :], from_right[...])
    left_k[...] = side_columns(from_left[1:2, :], from_left[1:2, :])
    for b in range(blocks):
        lanes = slice(b * LANES, (b + 1) * LANES)
        prior[b, PAD - 1 : PAD, :] = from_up[0:1, lanes]
        kx[b, PAD - 1 : PAD, :] = from_up[1:2, lanes]
        prior[b, PAD + rows : PAD + rows + 1, :] = from_down[0:1, lanes]
        r_out[b, PAD - 1 : PAD, :] = jnp.zeros((1, LANES), F32)
        r_out[b, PAD + rows : PAD + rows + 1, :] = jnp.zeros((1, LANES), F32)
    def tile_rows(strip, b):
        first = (strip * (blocks * LANES // TS) + 4 * b) * 8
        return [pl.ds(pl.multiple_of(first + 8 * q, 8), 8) for q in range(4)]

    def grid_rows(pad, strip, a):
        return pl.ds(pad + TS * strip + a, 8, stride=4)

    def to_tiles(strip, carry):
        base = pl.multiple_of(TS * strip, TS)
        rows_here = pl.ds(base, TS)
        padded = pl.ds(pl.multiple_of(PAD + base, 8), TS)
        for b in range(blocks):
            lanes = slice(b * LANES, (b + 1) * LANES)
            prior[b, padded, :] = prior_in[rows_here, lanes]
            kx[b, padded, :] = kx_in[rows_here, lanes]
            ky[b, rows_here, :] = ky_in[rows_here, lanes]
        for b in range(blocks):
            four = swap_blocks([prior[b, grid_rows(PAD, strip, a), :] for a in range(4)])
            for place, part in zip(tile_rows(strip, b), four):
                tiles[place, :] = part
        return carry

    lax.fori_loop(0, rows // TS, to_tiles, 0)
    table_copy.wait()

    def one_slot(slot, carry):
        live = table[slot, 1, 0]

        def batch(step, carry):
            first = step * BATCH
            places, terms = [], []
            for pair in range(BATCH // 2):
                at = pl.multiple_of((first + 2 * pair) * 8, 16)
                depths = got[slot, pl.ds(at, 16), :].astype(F32)
                confs = got[slot, pl.ds(cells + at, 16), :].astype(F32)
                for side in range(2):
                    tile = first + 2 * pair + side
                    place = pl.ds(pl.multiple_of(table[slot, 0, tile], 8), 8)
                    error = depths[8 * side : 8 * side + 8] - tiles[place, :]
                    weight = confs[8 * side : 8 * side + 8] / jnp.maximum(jnp.abs(error), HUBER)
                    places.append(place)
                    terms.append((weight, weight * error))
            for place, (weight, pull) in zip(places, terms):
                weights[place, :] += weight
                pulls[place, :] += pull
            return carry

        return lax.fori_loop(0, (live + BATCH - 1) // BATCH, batch, carry)

    lax.fori_loop(0, slots, one_slot, 0)
    @pl.when(flags[0, 0] == 1)
    def _():
        for b in range(blocks):
            kx[b, PAD + rows - 1 : PAD + rows, :] = jnp.zeros((1, LANES), F32)

    @pl.when(flags[0, 1] == 1)
    def _():
        edge = ky[blocks - 1]
        ky[blocks - 1] = jnp.where(lane_ids(edge.shape) == LANES - 1, 0.0, edge)

    def to_grid(strip, carry):
        for b in range(blocks):
            places = tile_rows(strip, b)
            for total, out, pad in ((weights, diag_out, 0), (pulls, r_out, PAD)):
                for a, part in enumerate(swap_blocks([total[place, :] for place in places])):
                    out[b, grid_rows(pad, strip, a), :] = part
        return carry

    lax.fori_loop(0, rows // TS, to_grid, 0)

    def flows(i, carry):
        here, above, below = at_row(i), at_row(i, -1), at_row(i, 1)
        part = pl.ds(pl.multiple_of(8 * i, 8), 8)
        p = [prior[b, here, :] for b in range(blocks)]
        h = [ky[b, part, :] for b in range(blocks)]
        p_right = cols_up(p, side_p[part, :])
        p_left = cols_down(p, side_p[part, :])
        h_left = cols_down(h, left_k[part, :])
        for b in range(blocks):
            k, k_up = kx[b, here, :], kx[b, above, :]
            down_flow = k * (prior[b, below, :] - p[b])
            up_flow = k_up * (p[b] - prior[b, above, :])
            side_flow = h[b] * (p_right[b] - p[b]) - h_left[b] * (p[b] - p_left[b])
            r_out[b, here, :] += (down_flow - up_flow) + side_flow
            diag_out[b, part, :] += LAM + (k + k_up) + (h[b] + h_left[b])
        return carry

    lax.fori_loop(0, steps, flows, 0, unroll=UF)

    zeros = jnp.zeros((8, LANES), F32)
    for i, out, row in ((0, up_out, 0), (steps - 1, down_out, 7)):
        image = operate(r_out, diag_out, kx, ky, i, zeros, zeros)
        for b in range(blocks):
            lanes = slice(b * LANES, (b + 1) * LANES)
            out[0:1, lanes] = r_out[b, at_row(i), :][row : row + 1, :]
            out[1:2, lanes] = image[b][row : row + 1, :]
    lane = lane_ids((8, LANES))

    def sides(i, carry):
        here = at_row(i)
        part = pl.ds(pl.multiple_of(8 * i, 8), 8)
        for b, edge, sign, target in ((0, 0, 1, side_p), (blocks - 1, LANES - 1, -1, left_k)):
            field = r_out[b, here, :]
            if edge:
                across = pltpu.roll(ky[b, part, :] * field, 1, axis=1)
            else:
                across = ky[b, part, :] * pltpu.roll(field, LANES - 1, axis=1)
            image = diag_out[b, part, :] * field - across - vertical(r_out, kx, b, i)
            target[part, :] = jnp.where(lane == edge, image, pltpu.roll(field, sign % LANES, axis=1))
        return carry

    lax.fori_loop(0, steps, sides, 0, unroll=US)
    turned = side_p[...].T
    left_out[0:1, :] = turned[1:2, :]
    left_out[1:2, :] = turned[0:1, :]
    right_out[...] = left_k[...].T[LANES - 2 :, :]


def join(flags, got, prior, kx, ky, from_up, from_down, from_left, from_right):
    rows, cols = prior.shape
    cells = rows * cols
    blocks = cols // LANES
    slots = got.shape[0]
    vmem = pl.BlockSpec(memory_space=pltpu.VMEM)
    padded, plain = (blocks, rows + 2 * PAD, LANES), (blocks, rows, LANES)
    shapes = (padded, plain, padded, plain, (2, cols), (2, cols), (2, rows), (2, rows))
    in_tiles = pltpu.VMEM((cells // LANES, LANES), F32)
    return pl.pallas_call(
        join_kernel,
        out_shape=[jax.ShapeDtypeStruct(s, F32) for s in shapes],
        in_specs=[pl.BlockSpec(memory_space=pltpu.SMEM)] + [vmem] * 8,
        out_specs=[vmem] * len(shapes),
        scratch_shapes=[
            pltpu.VMEM(padded, F32),
            pltpu.VMEM((slots, 8, LANES), jnp.int32),
            pltpu.SMEM((slots, 8, LANES), jnp.int32),
            in_tiles,
            in_tiles,
            in_tiles,
            pltpu.VMEM((rows, LANES), F32),
            pltpu.VMEM((rows, LANES), F32),
            pltpu.SemaphoreType.DMA,
        ],
        compiler_params=pltpu.CompilerParams(vmem_limit_bytes=SMALL_VMEM),
        cost_estimate=pl.CostEstimate(flops=30 * cells, bytes_accessed=24 * cells, transcendentals=0),
        name="join",
    )(flags, got, prior, kx, ky, from_up, from_down, from_left, from_right)


def vertical(field, kx, b, i):
    here, above, below = at_row(i), at_row(i, -1), at_row(i, 1)
    return kx[b, here, :] * field[b, below, :] + kx[b, above, :] * field[b, above, :]


def operate(field, diag, kx, ky, i, entering, after):
    blocks = diag.shape[0]
    part = pl.ds(8 * i, 8) if isinstance(i, int) else pl.ds(pl.multiple_of(8 * i, 8), 8)
    x = [field[b, at_row(i), :] for b in range(blocks)]
    h = [ky[b, part, :] for b in range(blocks)]
    right = cols_up(x, after)
    left = cols_down([h[b] * x[b] for b in range(blocks)], entering)
    return [
        (diag[b, part, :] * x[b] - vertical(field, kx, b, i)) - (h[b] * right[b] + left[b])
        for b in range(blocks)
    ]


def add_pair(total, other):
    (a, rest_a), (b, rest_b) = total, other
    s = a + b
    back = s - a
    error = (a - (s - back)) + (b - back)
    return s, rest_a + rest_b + error


def fold(pair, axis):
    size = pair[0].shape[axis] // 2
    while size:
        other = tuple(pltpu.roll(part, size, axis=axis) for part in pair)
        pair = add_pair(pair, other)
        size //= 2
    return pair


def moments_kernel(
    r_in, diag, kx, ky, r_up, r_down, r_left, r_right, k_left, own_left, own_right, own_ky,
    r, q, s, table_out, side_r, side_q,
):
    blocks, rows = diag.shape[0], diag.shape[1]
    steps = rows // 8
    last = blocks - 1
    k = k_left[1:2, :]
    side_r[...] = side_columns(k * r_left[0:1, :], r_right[0:1, :])
    side_q[...] = side_columns(
        k * (r_left[1:2, :] - k * own_left[0:1, :]),
        r_right[1:2, :] - own_ky[1:2, :] * own_right[0:1, :],
    )
    top, low = slice(PAD - 1, PAD), slice(PAD + rows, PAD + rows + 1)
    for b in range(blocks):
        lanes = slice(b * LANES, (b + 1) * LANES)
        r[b, top, :] = r_up[0:1, lanes]
        r[b, low, :] = r_down[0:1, lanes]
        q[b, top, :] = r_up[1:2, lanes] - kx[b, top, :] * r[b, PAD : PAD + 1, :]
        final = slice(PAD + rows - 1, PAD + rows)
        q[b, low, :] = r_down[1:2, lanes] - kx[b, final, :] * r[b, final, :]

    def folded(parts):
        while len(parts) > 1:
            parts = [a + b for a, b in zip(parts[::2], parts[1::2])]
        return parts[0]

    def products(left, right):
        return folded([a * b for a, b in zip(left, right)])

    def first(i, carry):
        m0, m1, m2 = carry
        part = pl.ds(pl.multiple_of(8 * i, 8), 8)
        image = operate(r, diag, kx, ky, i, side_r[part, :], side_r[part, :])
        field = [r[b, at_row(i), :] for b in range(blocks)]
        for b in range(blocks):
            q[b, at_row(i), :] = image[b]
        return (
            m0 + products(field, field), m1 + products(field, image), m2 + products(image, image),
        )

    zero = jnp.zeros((8, LANES), F32)
    m0, m1, m2 = lax.fori_loop(0, steps, first, (zero, zero, zero), unroll=UM)

    def second(i, m3):
        part = pl.ds(pl.multiple_of(8 * i, 8), 8)
        image = operate(q, diag, kx, ky, i, side_q[part, :], side_q[part, :])
        for b in range(blocks):
            s[b, part, :] = image[b]
        return m3 + products([q[b, at_row(i), :] for b in range(blocks)], image)

    m3 = lax.fori_loop(0, steps, second, zero, unroll=UM)

    sums = []
    for m in (m0, m1, m2, m3):
        pair = fold((m, jnp.zeros_like(m)), 0)
        sums.append(fold(pair, 1))
    corners = ((0, 0), (last, 0), (0, rows - 1), (last, rows - 1))

    def cell(ref, corner, pad=PAD):
        b, i = corner
        j = LANES - 1 if b else 0
        first = (pad + i) // 8 * 8
        return ref[b, first : first + 8, :][(pad + i) % 8 : (pad + i) % 8 + 1, j : j + 1]

    values = [value[0:1, 0:1] for value, _ in sums] + [rest[0:1, 0:1] for _, rest in sums]
    values += [cell(r, corner) for corner in corners]
    values += [cell(q, corner) for corner in corners]
    values += [cell(kx, corner) for corner in corners[2:]]
    values += [cell(ky, corner, 0) for corner in corners[1::2]]
    lane = lane_ids((1, LANES))
    row = jnp.zeros((1, LANES), F32)
    for place, value in enumerate(values):
        row = jnp.where(lane == place, jnp.broadcast_to(value, (1, LANES)), row)
    table_out[...] = jnp.broadcast_to(row, table_out.shape)


def moments(devices, r, diag, *others):
    blocks, rows, _ = diag.shape
    vmem = pl.BlockSpec(memory_space=pltpu.VMEM)
    cells = blocks * rows * LANES
    return pl.pallas_call(
        moments_kernel,
        out_shape=[
            jax.ShapeDtypeStruct(r.shape, F32),
            jax.ShapeDtypeStruct(r.shape, F32),
            jax.ShapeDtypeStruct(diag.shape, F32),
            jax.ShapeDtypeStruct((devices, LANES), F32),
        ],
        in_specs=[vmem] * (2 + len(others)),
        out_specs=[vmem] * 4,
        scratch_shapes=[pltpu.VMEM((rows, LANES), F32)] * 2,
        input_output_aliases={0: 0},
        compiler_params=pltpu.CompilerParams(vmem_limit_bytes=SMALL_VMEM),
        cost_estimate=pl.CostEstimate(flops=40 * cells, bytes_accessed=24 * cells, transcendentals=0),
        name="moments",
    )(r, diag, *others)


def split(a):
    high = a * 4097.0
    high = high - (high - a)
    return high, a - high


def product(a, b):
    p = a * b
    a1, a2 = split(a)
    b1, b2 = split(b)
    return p, ((a1 * b1 - p) + a1 * b2 + a2 * b1) + a2 * b2


def quotient(top, bottom):
    q = top[0] / bottom[0]
    p, error = product(q, bottom[0])
    rest = ((top[0] - p) - error + top[1] - q * bottom[1]) / bottom[0]
    return q, rest


def finish_kernel(
    col_count, where_ref, table_ref, prior, r, q, s, height_hbm, residual_hbm,
    height, residual, coeff, sems,
):
    blocks, rows = s.shape[0], s.shape[1]
    turned = table_ref[...].T
    devices = turned.shape[1]
    field = [turned[i : i + 1, :] for i in range(20)]

    def at(index, down, right):
        shift = -(down * col_count + right)
        return pltpu.roll(jnp.broadcast_to(field[index], (8, devices)), shift % devices, axis=1)

    r_tl, r_tr, r_bl, r_br = 8, 9, 10, 11
    kx_l, kx_r, ky_t, ky_b = 16, 17, 18, 19
    extra = [
        (at(kx_l, -1, 0) * at(ky_b, -1, -1) + at(ky_t, 0, -1) * at(kx_r, -1, -1)) * at(r_br, -1, -1),
        (at(kx_r, -1, 0) * at(ky_b, -1, 0) + at(ky_t, 0, 0) * at(kx_l, -1, 1)) * at(r_bl, -1, 1),
        (at(kx_l, 0, 0) * at(ky_t, 1, -1) + at(ky_b, 0, -1) * at(kx_r, 0, -1)) * at(r_tr, 1, -1),
        (at(kx_r, 0, 0) * at(ky_t, 1, 0) + at(ky_b, 0, 0) * at(kx_l, 0, 1)) * at(r_tl, 1, 1),
    ]
    pairs = [
        [jnp.broadcast_to(field[i], (8, devices)), jnp.broadcast_to(field[4 + i], (8, devices))]
        for i in range(4)
    ]
    for corner in range(4):
        pairs[3][1] = pairs[3][1] + extra[corner] * field[12 + corner]
    m = [fold(tuple(pair), 1) for pair in pairs]
    m = [tuple(part[0:1, 0:1] for part in pair) for pair in m]
    x1, x2, x3 = (quotient(m[i + 1], m[i]) for i in range(3))
    gap_1 = (x2[0] - x1[0]) + (x2[1] - x1[1])
    gap_2 = (x3[0] - x2[0]) + (x3[1] - x2[1])
    alpha = 1.0 / x1[0]
    ratio = 1.0 + gap_1 / x1[0]
    alpha_1 = gap_1 / (x2[0] * gap_2)
    mine = lane_ids((8, devices)) == where_ref[0, 2]
    values = [alpha + alpha_1 * ratio, alpha_1 * alpha]
    for corner in range(4):
        own = jnp.sum(jnp.where(mine, extra[corner], 0.0), axis=1, keepdims=True)
        values.append(own[0:1, 0:1])
    for i, value in enumerate(values):
        coeff[i] = jnp.broadcast_to(value, (8, LANES))

    one, two = coeff[0][0:1, 0:1], coeff[1][0:1, 0:1]

    def mend(corner, b, i):
        here = (row_ids((8, LANES)) == i % 8) & (
            lane_ids((8, LANES)) == (LANES - 1 if b else 0)
        )
        residual[b, i // 8 * 8 : i // 8 * 8 + 8, :] += jnp.where(
            here, coeff[1] * coeff[2 + corner], 0.0
        )

    copies = []
    for b in range(blocks):

        def step(i, carry, b=b):
            part = pl.ds(pl.multiple_of(8 * i, 8), 8)
            here = at_row(i)
            x, y = r[b, here, :], q[b, here, :]
            height[b, part, :] = prior[part, b * LANES : (b + 1) * LANES] + (one * x - two * y)
            residual[b, part, :] = x - (one * y - two * s[b, part, :])
            return carry

        lax.fori_loop(0, rows // 8, step, 0, unroll=8)
        if b == 0:
            mend(0, b, 0)
            mend(2, b, rows - 1)
        if b == blocks - 1:
            mend(1, b, 0)
            mend(3, b, rows - 1)
        for which, (source, target) in enumerate(((height, height_hbm), (residual, residual_hbm))):
            copy = pltpu.make_async_copy(
                source.at[b], target.at[:, pl.ds(b * LANES, LANES)], sems.at[which, b]
            )
            copy.start()
            copies.append(copy)
    for copy in copies:
        copy.wait()


def finish(where, table, prior, r, q, s, col_count):
    blocks, rows, _ = s.shape
    cells = rows * blocks * LANES
    vmem = pl.BlockSpec(memory_space=pltpu.VMEM)
    return pl.pallas_call(
        functools.partial(finish_kernel, col_count),
        out_shape=[jax.ShapeDtypeStruct((rows, blocks * LANES), F32)] * 2,
        in_specs=[pl.BlockSpec(memory_space=pltpu.SMEM)] + [vmem] * 5,
        out_specs=[pl.BlockSpec(memory_space=pltpu.HBM)] * 2,
        scratch_shapes=[
            pltpu.VMEM(s.shape, F32),
            pltpu.VMEM(s.shape, F32),
            pltpu.VMEM((8, 8, LANES), F32),
            pltpu.SemaphoreType.DMA((2, blocks)),
        ],
        compiler_params=pltpu.CompilerParams(vmem_limit_bytes=SMALL_VMEM),
        cost_estimate=pl.CostEstimate(flops=8 * cells, bytes_accessed=24 * cells, transcendentals=0),
        name="finish",
    )(where, table, prior, r, q, s)


def send(strip, axis, by):
    count = lax.axis_size(axis)
    return lax.ppermute(
        strip, axis, [(i, i + by) for i in range(count) if 0 <= i + by < count]
    )


def exchange(up, down, left, right):
    return (
        send(down, "row", 1), send(up, "row", -1), send(right, "col", 1), send(left, "col", -1),
    )


def shards(
    depth_tiles, conf_tiles, tile_owner, tile_offset, tile_count, prior, edge_rows, edge_cols
):
    row, col = lax.axis_index("row"), lax.axis_index("col")
    row_count, col_count = lax.axis_size("row"), lax.axis_size("col")
    flags = jnp.stack(
        [row == row_count - 1, col == col_count - 1, row * col_count + col]
    ).astype(jnp.int32)[None]
    own = strips(prior, edge_rows, edge_cols)
    early = exchange(*own)
    payload = pack(tile_owner, tile_offset, tile_count, depth_tiles[0], conf_tiles[0], col_count)
    payload, early, flags = lax.optimization_barrier((payload, early, flags))
    got = lax.all_to_all(payload, "col", split_axis=0, concat_axis=0, tiled=True)
    r, diag, kx, ky, *edges = join(flags, got, prior, edge_rows, edge_cols, *early)
    late = exchange(*edges)
    r, q, s, table = moments(
        row_count * col_count, r, diag, kx, ky, *late, early[2], edges[2], edges[3], own[3]
    )
    table = lax.all_to_all(table, ("row", "col"), split_axis=0, concat_axis=0, tiled=True)
    return tuple(finish(flags, table, prior, r, q, s, col_count))


def solution(mesh):
    return jax.shard_map(
        shards,
        mesh=mesh,
        in_specs=(
            P("row", "col", None),
            P("row", "col", None),
            P("row", "col"),
            P("row", "col"),
            P("row", "col"),
            P("row", "col"),
            P("row", "col"),
            P("row", "col"),
        ),
        out_specs=(P("row", "col"), P("row", "col")),
        check_vma=False,
    )
```

time: 459 us -> 139 us (0.30); the launches traced: 453 us -> 138 us
  blocking collectives: 199 us -> 81.3 us
  local copies, waits for them, and re-layouts: 98.4 us -> 0.04 us
  other arithmetic: 48.6 us -> 0.08 us
  starting transfers between devices: 59.6 us -> 26 us
  Pallas kernels: 0 us -> 25.8 us
  matrix products: 21.8 us -> 0 us
  waiting for transfers between devices: 19.8 us -> 3.06 us
    psum x3 -> x0, blocking collectives: 199 us -> none  [the longest x2 131 us: squares(): return lax.psum(jnp.sum(residual * residual), ('row', 'col'))]
    all_to_all x0 -> x2, blocking collectives: none -> 81.3 us  [the longest x1 62.8 us: shards(): lax.all_to_all(payload, 'col', split_axis=0, concat_axis=0, tiled=True)]
    reshape x7 -> x0, local copies, waits for them, and re-layouts: 55.6 us -> none  [the longest x2 19.6 us: to_tiles(): grid.reshape(grid_rows // tile_side, tile_side, grid_cols // tile_side, t...]
    add x3 -> x0, local copies, waits for them, and re-layouts: 27.4 us -> none  [make_operator(): diagonal = weight_sum + LAM + row_edge + row_above + col_edge + col_before]
    pallas_call x0 -> x5, Pallas kernels: none -> 25.8 us  [the longest x1 13.4 us: join(): pl.pallas_call(join_kernel, out_shape=[jax.ShapeDtypeStruct(s, F32) for s...]
    dot_general x3 -> x0, matrix products: 21.8 us -> none  [the longest x1 10 us: shards(): prior_at = jnp.dot(matches, prior_tiles, precision=lax.Precision.HIGHEST)]
    reduce_sum x5 -> x0, other arithmetic: 19.6 us -> none  [the longest x2 15.3 us: shards(): alpha = norm_now / lax.psum(jnp.sum(direction * image), ('row', 'col'))]
    sub x3 -> x0, other arithmetic: 18.8 us -> none  [the longest x1 11.8 us: shards(): residual = right_side - operate(prior)]
  transfers between devices with their start and end apart: 16 -> 8, of which waited for: 7 -> 1; matrix products, arithmetic and copies ran while one was open for 27% -> 0% of each run, Pallas kernels for 0% -> 1%
where the time goes in v2:
time: 139 us; the launch traced here: 138 us
  blocking collectives  81.3 us (58%)
  starting transfers between devices  26 us (19%)
  Pallas kernels  25.8 us (19%)
  waiting for transfers between devices  3.06 us (2%)
  between operations  1.52 us (1%)
    all_to_all x1, blocking collectives, shards(): lax.all_to_all(payload, 'col', split_axis=0, concat_axis=0, tiled=True)  62.8 us
    ppermute x8, starting transfers between devices, send(): lax.ppermute(strip, axis, [(i, i + by) for i in range(count) if 0 <= i +...  26 us
    all_to_all x1, blocking collectives, shards(): lax.all_to_all(table, ('row', 'col'), split_axis=0, concat_axis=0, tiled=...  18.6 us
    pallas_call x1, Pallas kernels, join(): pl.pallas_call(join_kernel, out_shape=[jax.ShapeDtypeStruct(s, F32) for s...  13.4 us
    pallas_call x1, Pallas kernels, moments(): pl.pallas_call(moments_kernel, out_shape=[jax.ShapeDtypeStruct(r.shape, F...  4.9 us
    pallas_call x1, Pallas kernels, finish(): pl.pallas_call(functools.partial(finish_kernel, col_count), out_shape=[ja...  3.74 us
    ppermute x8, waiting for transfers between devices, send(): lax.ppermute(strip, axis, [(i, i + by) for i in range(count) if 0 <= i +...  3.06 us
  transfers between devices with their start and end apart: 8, of which 1 were waited for; matrix products, arithmetic and copies ran while one was open for 0% of the time, Pallas kernels for 1%

profile of v2, /device:TPU:1, one launch (start us, length us, event | category | flops | bytes accessed | tf_op | source)
XLA Modules:
  0.0 137.9 jit_solution(15335504950724709906)
XLA Ops:
  0.6 0.0 copy-start.7
  0.6 0.0 copy-start.6
  0.7 0.0 copy-start.4
  0.7 0.0 copy-start.3
  0.7 2.2 %strips.1 = (f32[1,1024]{1,0:T(1,128)}, f32[2,1024]{1,0:T(2,128)}, f32[1,512]{1,0:T(1,128)}, f32[2,512]{1,0:T(2,128)}) custom-call(f32[512,1024]{1,0:T(8,128)} %prior.1, f32[512,1024]{1,0:T(8,128)} %prior.1, f32[512,1024]{1,0:T(8,128)} %kx_in.1, f32[512,1024]{1,0:T(8,128)} %prior.1, f32[512,1024]{1,0:T(8,128)} %prior.1, f32[512,1024]{1,0:T(8,128)} %ky_in.1), custom_call_target="tpu_custom_call" | custom-call | tf_op jit(solution)/shard_map/strips/pallas_call | solution.py:146
  2.9 1.3 collective-permute-start.3
  4.2 3.3 %collective-permute-start.1 = (f32[1,1024]{1,0:T(1,128)}, f32[1,1024]{1,0:T(1,128)S(1)}, u32[]{:S(2)}, u32[]{:S(2)}) collective-permute-start(f32[1,1024]{1,0:T(1,128)} %get-tuple-element.25), channel_id=1, source_target_pairs={{16,0},{32,16},{48,32},{64,48},{80,64},{96,80},{112,96},{17,1},{33... | collective-permute-start | bytes 12296 | tf_op jit(solution)/shard_map/ppermute | solution.py:606
  7.5 4.3 %collective-permute-start.2 = (f32[2,512]{1,0:T(2,128)}, f32[2,512]{1,0:T(2,128)S(1)}, u32[]{:S(2)}, u32[]{:S(2)}) collective-permute-start(f32[2,512]{1,0:T(2,128)} %get-tuple-element.26.own_ky), channel_id=1, source_target_pairs={{0,1},{1,2},{2,3},{3,4},{4,5},{5,6},{6,7},{7,8},{8,9},{9,10},{10,1... | collective-permute-start | bytes 12296 | tf_op jit(solution)/shard_map/ppermute | solution.py:606
  11.8 3.4 %collective-permute-start = (f32[2,1024]{1,0:T(2,128)}, f32[2,1024]{1,0:T(2,128)S(1)}, u32[]{:S(2)}, u32[]{:S(2)}) collective-permute-start(f32[2,1024]{1,0:T(2,128)} %get-tuple-element.24), channel_id=1, source_target_pairs={{0,16},{16,32},{32,48},{48,64},{64,80},{80,96},{96,112},{1,17},{17... | collective-permute-start | bytes 24584 | tf_op jit(solution)/shard_map/ppermute | solution.py:606
  15.2 0.1 add_bitcast_fusion.flags.where_ref
  15.9 0.0 copy-done.7
  15.9 0.0 copy-done.6
  15.9 0.0 copy-done.4
  15.9 0.0 copy-done.3
  15.9 1.6 %pack.1 = bf16[16,1040,128]{2,1,0:T(8,128)(2,1)S(1)} custom-call(s32[1,512]{1,0:T(1,128)S(1)} %copy-done.6, s32[1,1]{1,0:T(1,128)S(6)} %copy.13.count_ref, s32[1,512]{1,0:T(1,128)S(1)} %copy-done.7, bf16[512,1024]{1,0:T(8,128)(2,1)S(1)} %bitcast.11, bf16[512,1024]{1,0:T(8,128)(2,1)S(1)} %bitcast.12), custom_call_target="tpu_custom_call" | custom-call | flops 1048576 | bytes 4194304 | tf_op jit(solution)/shard_map/pack/pallas_call | solution.py:116
  17.5 0.0 copy-start
  17.6 0.0 copy-start.1
  17.6 0.0 copy-start.2
  17.6 0.0 collective-permute-done.3.from_right
  17.6 0.0 collective-permute-done.1.from_down
  17.6 0.0 collective-permute-done.2.from_left.k_left
  17.6 0.0 collective-permute-done.from_up
  17.6 62.8 %all_to_all.16.got = bf16[16,1040,128]{2,1,0:T(8,128)(2,1)S(1)} all-to-all(bf16[16,1040,128]{2,1,0:T(8,128)(2,1)S(1)} %pack.1), channel_id=1, replica_groups=mesh['row'=8,'col'=16] {'col'}, dimensions={0} | all-to-all | bytes 8519680 | tf_op jit(solution)/shard_map/all_to_all | solution.py:629
  80.4 0.0 copy-done
  80.4 0.0 copy-done.1
  80.4 0.0 copy-done.2
  80.4 0.0 copy-start.5
  80.4 13.4 %join.1 = (f32[8,528,128]{2,1,0:T(8,128)S(1)}, f32[8,512,128]{2,1,0:T(8,128)S(1)}, f32[8,528,128]{2,1,0:T(8,128)S(1)}, f32[8,512,128]{2,1,0:T(8,128)S(1)}, f32[2...) custom-call(s32[1,3]{1,0:T(1,128)S(1)} %add_bitcast_fusion.flags.where_ref, ...), custom_call_target="tpu_custom_call" | custom-call | flops 15728640 | bytes 12582912 | tf_op jit(solution)/shard_map/join/pallas_call | solution.py:326
  93.8 2.7 %collective-permute-start.4 = (f32[2,1024]{1,0:T(2,128)S(1)}, f32[2,1024]{1,0:T(2,128)S(1)}, u32[]{:S(2)}, u32[]{:S(2)}) collective-permute-start(f32[2,1024]{1,0:T(2,128)S(1)} %get-tuple-element.38), channel_id=1, source_target_pairs={{0,16},{16,32},{32,48},{48,64},{64,80},{80,96},{96,112},{1,17},{17... | collective-permute-start | bytes 24584 | tf_op jit(solution)/shard_map/ppermute | solution.py:606
  96.5 1.9 %collective-permute-start.5 = (f32[2,1024]{1,0:T(2,128)S(1)}, f32[2,1024]{1,0:T(2,128)S(1)}, u32[]{:S(2)}, u32[]{:S(2)}) collective-permute-start(f32[2,1024]{1,0:T(2,128)S(1)} %get-tuple-element.39), channel_id=1, source_target_pairs={{16,0},{32,16},{48,32},{64,48},{80,64},{96,80},{112,96},{17,1},{33... | collective-permute-start | bytes 24584 | tf_op jit(solution)/shard_map/ppermute | solution.py:606
  98.4 7.9 %collective-permute-start.6 = (f32[2,512]{1,0:T(2,128)S(1)}, f32[2,512]{1,0:T(2,128)S(1)}, u32[]{:S(2)}, u32[]{:S(2)}) collective-permute-start(f32[2,512]{1,0:T(2,128)S(1)} %get-tuple-element.40.own_right), channel_id=1, source_target_pairs={{0,1},{1,2},{2,3},{3,4},{4,5},{5,6},{6,7},{7,8},{8,9},{9,10},{10,1... | collective-permute-start | bytes 12296 | tf_op jit(solution)/shard_map/ppermute | solution.py:606
  106.3 1.3 collective-permute-start.7
  107.6 0.0 collective-permute-done.6.r_left
  107.7 3.0 %collective-permute-done.7.r_right = f32[2,512]{1,0:T(2,128)S(1)} collective-permute-done((f32[2,512]{1,0:T(2,128)S(1)}, f32[2,512]{1,0:T(2,128)S(1)}, u32[]{:S(2)}, u32[]{:S(2)}) %collective-permute-start.7) | collective-permute-done | bytes 4128 | tf_op jit(solution)/shard_map/ppermute | solution.py:606
  110.7 0.0 collective-permute-done.4.r_up
  110.7 0.0 collective-permute-done.5.r_down
  110.7 0.0 copy-done.5
  110.7 4.9 %moments.1 = (f32[8,528,128]{2,1,0:T(8,128)S(1)}, f32[8,528,128]{2,1,0:T(8,128)S(1)}, f32[8,512,128]{2,1,0:T(8,128)S(1)}, f32[128,128]{1,0:T(8,128)S(1)}) custom-call(f32[8,528,128]{2,1,0:T(8,128)S(1)} %get-tuple-element.34.r_in, f32[8,512,128]{2,1,0:T(8,128)S(1)} %get-tuple-element.35.diag, ...), custom_call_target="tpu_custom_call", output_to_operand_aliasing={{0}: (0, {})} | custom-call | flops 20971520 | bytes 12582912 | tf_op jit(solution)/shard_map/moments/pallas_call | solution.py:464
  115.6 18.6 %all_to_all.17 = f32[128,1,128]{2,1,0:T(1,128)S(1)} all-to-all(f32[128,1,128]{2,1,0:T(1,128)S(1)} %bitcast.14), channel_id=1, replica_groups=mesh['row'=8,'col'=16] {'row','col'}, dimensions={0} | all-to-all | bytes 131072 | tf_op jit(solution)/shard_map/all_to_all | solution.py:635
  134.2 3.7 %finish.1 = (f32[512,1024]{1,0:T(8,128)}, f32[512,1024]{1,0:T(8,128)}) custom-call(s32[1,3]{1,0:T(1,128)S(1)} %add_bitcast_fusion.flags.where_ref, f32[128,128]{1,0:T(8,128)S(1)} %bitcast.13, f32[512,1024]{1,0:T(8,128)S(1)} %copy-done, f32[8,528,128]{2,1,0:T(8,128)S(1)} %get-tuple-element.43.r, f32[8,528,128]{2,1,0:T(8,128)S(1)} %get-tuple-element.44.q, ...), custom_call_target="tpu_custom_call" | custom-call | flops 4194304 | bytes 12582912 | tf_op jit(solution)/shard_map/finish/pallas_call | solution.py:587
Async XLA Ops:
  0.6 15.3 %copy-start.7 = (s32[1,512]{1,0:T(1,128)S(1)}, s32[1,512]{1,0:T(1,128)}, u32[]{:S(2)}) copy-start(s32[1,512]{1,0:T(1,128)} %offset_ref.1) | copy-start | bytes 6148
  0.6 15.3 %copy-start.6 = (s32[1,512]{1,0:T(1,128)S(1)}, s32[1,512]{1,0:T(1,128)}, u32[]{:S(2)}) copy-start(s32[1,512]{1,0:T(1,128)} %owner_ref.1) | copy-start | bytes 6148
  0.7 15.3 %copy-start.4 = (bf16[1,512,1024]{2,1,0:T(8,128)(2,1)S(1)}, bf16[1,512,1024]{2,1,0:T(8,128)(2,1)}, u32[]{:S(2)}) copy-start(bf16[1,512,1024]{2,1,0:T(8,128)(2,1)} %param.9) | copy-start | bytes 3145732
  0.7 15.3 %copy-start.3 = (bf16[1,512,1024]{2,1,0:T(8,128)(2,1)S(1)}, bf16[1,512,1024]{2,1,0:T(8,128)(2,1)}, u32[]{:S(2)}) copy-start(bf16[1,512,1024]{2,1,0:T(8,128)(2,1)} %param.8) | copy-start | bytes 3145732
  2.9 14.7 %collective-permute-start.3 = (f32[1,512]{1,0:T(1,128)}, f32[1,512]{1,0:T(1,128)S(1)}, u32[]{:S(2)}, u32[]{:S(2)}) collective-permute-start(f32[1,512]{1,0:T(1,128)} %get-tuple-element.27), channel_id=1, source_target_pairs={{1,0},{2,1},{3,2},{4,3},{5,4},{6,5},{7,6},{8,7},{9,8},{10,9},{11,1... | collective-permute-start | bytes 6152 | tf_op jit(solution)/shard_map/ppermute | solution.py:606
  4.2 13.4 %collective-permute-start.1 = (f32[1,1024]{1,0:T(1,128)}, f32[1,1024]{1,0:T(1,128)S(1)}, u32[]{:S(2)}, u32[]{:S(2)}) collective-permute-start(f32[1,1024]{1,0:T(1,128)} %get-tuple-element.25), channel_id=1, source_target_pairs={{16,0},{32,16},{48,32},{64,48},{80,64},{96,80},{112,96},{17,1},{33... | collective-permute-start | bytes 12296 | tf_op jit(solution)/shard_map/ppermute | solution.py:606
  7.5 10.1 %collective-permute-start.2 = (f32[2,512]{1,0:T(2,128)}, f32[2,512]{1,0:T(2,128)S(1)}, u32[]{:S(2)}, u32[]{:S(2)}) collective-permute-start(f32[2,512]{1,0:T(2,128)} %get-tuple-element.26.own_ky), channel_id=1, source_target_pairs={{0,1},{1,2},{2,3},{3,4},{4,5},{5,6},{6,7},{7,8},{8,9},{9,10},{10,1... | collective-permute-start | bytes 12296 | tf_op jit(solution)/shard_map/ppermute | solution.py:606
  11.8 5.8 %collective-permute-start = (f32[2,1024]{1,0:T(2,128)}, f32[2,1024]{1,0:T(2,128)S(1)}, u32[]{:S(2)}, u32[]{:S(2)}) collective-permute-start(f32[2,1024]{1,0:T(2,128)} %get-tuple-element.24), channel_id=1, source_target_pairs={{0,16},{16,32},{32,48},{48,64},{64,80},{80,96},{96,112},{1,17},{17... | collective-permute-start | bytes 24584 | tf_op jit(solution)/shard_map/ppermute | solution.py:606
  17.5 62.9 %copy-start = (f32[512,1024]{1,0:T(8,128)S(1)}, f32[512,1024]{1,0:T(8,128)}, u32[]{:S(2)}) copy-start(f32[512,1024]{1,0:T(8,128)} %prior.1) | copy-start | bytes 6291460
  17.6 62.9 %copy-start.1 = (f32[512,1024]{1,0:T(8,128)S(1)}, f32[512,1024]{1,0:T(8,128)}, u32[]{:S(2)}) copy-start(f32[512,1024]{1,0:T(8,128)} %kx_in.1) | copy-start | bytes 6291460
  17.6 62.9 %copy-start.2 = (f32[512,1024]{1,0:T(8,128)S(1)}, f32[512,1024]{1,0:T(8,128)}, u32[]{:S(2)}) copy-start(f32[512,1024]{1,0:T(8,128)} %ky_in.1) | copy-start | bytes 6291460
  80.4 30.3 %copy-start.5 = (f32[2,512]{1,0:T(2,128)S(1)}, f32[2,512]{1,0:T(2,128)}, u32[]{:S(2)}) copy-start(f32[2,512]{1,0:T(2,128)} %get-tuple-element.26.own_ky) | copy-start | bytes 12292
  93.8 16.9 %collective-permute-start.4 = (f32[2,1024]{1,0:T(2,128)S(1)}, f32[2,1024]{1,0:T(2,128)S(1)}, u32[]{:S(2)}, u32[]{:S(2)}) collective-permute-start(f32[2,1024]{1,0:T(2,128)S(1)} %get-tuple-element.38), channel_id=1, source_target_pairs={{0,16},{16,32},{32,48},{48,64},{64,80},{80,96},{96,112},{1,17},{17... | collective-permute-start | bytes 24584 | tf_op jit(solution)/shard_map/ppermute | solution.py:606
  96.5 14.2 %collective-permute-start.5 = (f32[2,1024]{1,0:T(2,128)S(1)}, f32[2,1024]{1,0:T(2,128)S(1)}, u32[]{:S(2)}, u32[]{:S(2)}) collective-permute-start(f32[2,1024]{1,0:T(2,128)S(1)} %get-tuple-element.39), channel_id=1, source_target_pairs={{16,0},{32,16},{48,32},{64,48},{80,64},{96,80},{112,96},{17,1},{33... | collective-permute-start | bytes 24584 | tf_op jit(solution)/shard_map/ppermute | solution.py:606
  98.4 9.2 %collective-permute-start.6 = (f32[2,512]{1,0:T(2,128)S(1)}, f32[2,512]{1,0:T(2,128)S(1)}, u32[]{:S(2)}, u32[]{:S(2)}) collective-permute-start(f32[2,512]{1,0:T(2,128)S(1)} %get-tuple-element.40.own_right), channel_id=1, source_target_pairs={{0,1},{1,2},{2,3},{3,4},{4,5},{5,6},{6,7},{7,8},{8,9},{9,10},{10,1... | collective-permute-start | bytes 12296 | tf_op jit(solution)/shard_map/ppermute | solution.py:606
  106.3 4.4 %collective-permute-start.7 = (f32[2,512]{1,0:T(2,128)S(1)}, f32[2,512]{1,0:T(2,128)S(1)}, u32[]{:S(2)}, u32[]{:S(2)}) collective-permute-start(f32[2,512]{1,0:T(2,128)S(1)} %get-tuple-element.41.own_left), channel_id=1, source_target_pairs={{1,0},{2,1},{3,2},{4,3},{5,4},{6,5},{7,6},{8,7},{9,8},{10,9},{11,1... | collective-permute-start | bytes 12296 | tf_op jit(solution)/shard_map/ppermute | solution.py:606

commit v3 on v2

--- a/solution.py
+++ b/solution.py
@@ -15,7 +15,7 @@
 LANES = 128
 PAD = 8
 F32 = jnp.float32
-SMALL_VMEM = 20 * 1024 * 1024
+SMALL_VMEM = 16 * 1024 * 1024
 
 
 def lane_ids(shape):
@@ -125,19 +125,21 @@
     )(owners, count, offsets, depth, conf)
 
 
-def strips_kernel(top, bottom, kx_bottom, left, right, ky_right, up_out, down_out, left_out, right_out):
+def strips_kernel(
+    flags, top, bottom, kx_bottom, left, right, ky_right, up_out, down_out, left_out, right_out
+):
     up_out[...] = top[0:1, :]
     down_out[0:1, :] = bottom[7:8, :]
-    down_out[1:2, :] = kx_bottom[7:8, :]
+    down_out[1:2, :] = jnp.where(flags[0, 0] == 1, 0.0, kx_bottom[7:8, :])
     lane = lane_ids(left.shape)
     left_out[...] = left[...].T[0:1, :]
     both = jnp.where(lane == LANES - 1, right[...], pltpu.roll(ky_right[...], LANES - 1, axis=1))
     turned = both.T
     right_out[0:1, :] = turned[LANES - 1 : LANES, :]
-    right_out[1:2, :] = turned[LANES - 2 : LANES - 1, :]
-
-
-def strips(prior, kx, ky):
+    right_out[1:2, :] = jnp.where(flags[0, 1] == 1, 0.0, turned[LANES - 2 : LANES - 1, :])
+
+
+def strips(flags, prior, kx, ky):
     rows, cols = prior.shape
     last_rows = pl.BlockSpec((8, cols), lambda i: (rows // 8 - 1, 0))
     last_cols = pl.BlockSpec((rows, LANES), lambda i: (0, cols // LANES - 1))
@@ -148,23 +150,64 @@
         grid=(1,),
         out_shape=[jax.ShapeDtypeStruct(s, F32) for s in shapes],
         in_specs=[
-            whole((8, cols)), last_rows, last_rows, whole((rows, LANES)), last_cols, last_cols,
+            pl.BlockSpec(memory_space=pltpu.SMEM), whole((8, cols)), last_rows, last_rows, whole((rows, LANES)), last_cols, last_cols,
         ],
         out_specs=[whole(s) for s in shapes],
         name="strips",
-    )(prior, prior, kx, prior, prior, ky)
+    )(flags, prior, prior, kx, prior, prior, ky)
 
 
 BATCH = 16
 UF = 4
+UO = 8
 US = 16
 UM = 8
 
 
+def tile_rows(strip, b, blocks):
+    first = (strip * (blocks * LANES // TS) + 4 * b) * 8
+    return [pl.ds(pl.multiple_of(first + 8 * q, 8), 8) for q in range(4)]
+
+
+def grid_rows(pad, strip, a):
+    return pl.ds(pad + TS * strip + a, 8, stride=4)
+
+
+def to_grid(weights, pulls, diag, r, strip, chosen):
+    for b in chosen:
+        places = tile_rows(strip, b, diag.shape[0])
+        for total, out, pad in ((weights, diag, 0), (pulls, r, PAD)):
+            for a, part in enumerate(swap_blocks([total[place, :] for place in places])):
+                out[b, grid_rows(pad, strip, a), :] = part
+
+
+def add_flows(r, diag, prior, kx, ky, side_p, left_k, i, chosen):
+    last = diag.shape[0] - 1
+    here, above, below = at_row(i), at_row(i, -1), at_row(i, 1)
+    part = pl.ds(pl.multiple_of(8 * i, 8), 8)
+    near = sorted({n for b in chosen for n in (b - 1, b, b + 1) if 0 <= n <= last})
+    p = {b: prior[b, here, :] for b in near}
+    h = {b: ky[b, part, :] for b in near}
+    lane = lane_ids((8, LANES))
+    up = {b: pltpu.roll(p[b], LANES - 1, axis=1) for b in near}
+    down = {b: pltpu.roll(p[b], 1, axis=1) for b in near}
+    h_down = {b: pltpu.roll(h[b], 1, axis=1) for b in near}
+    for b in chosen:
+        p_right = jnp.where(lane == LANES - 1, up[b + 1] if b < last else side_p[part, :], up[b])
+        p_left = jnp.where(lane == 0, down[b - 1] if b else side_p[part, :], down[b])
+        h_left = jnp.where(lane == 0, h_down[b - 1] if b else left_k[part, :], h_down[b])
+        k, k_up = kx[b, here, :], kx[b, above, :]
+        down_flow = k * (prior[b, below, :] - p[b])
+        up_flow = k_up * (p[b] - prior[b, above, :])
+        side_flow = h[b] * (p_right - p[b]) - h_left * (p[b] - p_left)
+        r[b, here, :] += (down_flow - up_flow) + side_flow
+        diag[b, part, :] += LAM + (k + k_up) + (h[b] + h_left)
+
+
 def join_kernel(
     flags, got, prior_in, kx_in, ky_in, from_up, from_down, from_left, from_right,
-    r_out, diag_out, kx, ky, up_out, down_out, left_out, right_out,
-    prior, table_v, table, tiles, weights, pulls, side_p, left_k, table_sem,
+    r_out, diag_out, prior, kx, ky, weights, pulls, up_out, down_out, left_out, right_out,
+    table_v, table, tiles, side_p, left_k, table_sem,
 ):
     slots, rows_in = got.shape[0], got.shape[1]
     cells = (rows_in - META) // 2
@@ -196,13 +239,6 @@
         prior[b, PAD + rows : PAD + rows + 1, :] = from_down[0:1, lanes]
         r_out[b, PAD - 1 : PAD, :] = jnp.zeros((1, LANES), F32)
         r_out[b, PAD + rows : PAD + rows + 1, :] = jnp.zeros((1, LANES), F32)
-    def tile_rows(strip, b):
-        first = (strip * (blocks * LANES // TS) + 4 * b) * 8
-        return [pl.ds(pl.multiple_of(first + 8 * q, 8), 8) for q in range(4)]
-
-    def grid_rows(pad, strip, a):
-        return pl.ds(pad + TS * strip + a, 8, stride=4)
-
     def to_tiles(strip, carry):
         base = pl.multiple_of(TS * strip, TS)
         rows_here = pl.ds(base, TS)
@@ -214,7 +250,7 @@
             ky[b, rows_here, :] = ky_in[rows_here, lanes]
         for b in range(blocks):
             four = swap_blocks([prior[b, grid_rows(PAD, strip, a), :] for a in range(4)])
-            for place, part in zip(tile_rows(strip, b), four):
+            for place, part in zip(tile_rows(strip, b, blocks), four):
                 tiles[place, :] = part
         return carry
 
@@ -256,34 +292,31 @@
         edge = ky[blocks - 1]
         ky[blocks - 1] = jnp.where(lane_ids(edge.shape) == LANES - 1, 0.0, edge)
 
-    def to_grid(strip, carry):
-        for b in range(blocks):
-            places = tile_rows(strip, b)
-            for total, out, pad in ((weights, diag_out, 0), (pulls, r_out, PAD)):
-                for a, part in enumerate(swap_blocks([total[place, :] for place in places])):
-                    out[b, grid_rows(pad, strip, a), :] = part
-        return carry
-
-    lax.fori_loop(0, rows // TS, to_grid, 0)
-
-    def flows(i, carry):
-        here, above, below = at_row(i), at_row(i, -1), at_row(i, 1)
-        part = pl.ds(pl.multiple_of(8 * i, 8), 8)
-        p = [prior[b, here, :] for b in range(blocks)]
-        h = [ky[b, part, :] for b in range(blocks)]
-        p_right = cols_up(p, side_p[part, :])
-        p_left = cols_down(p, side_p[part, :])
-        h_left = cols_down(h, left_k[part, :])
-        for b in range(blocks):
-            k, k_up = kx[b, here, :], kx[b, above, :]
-            down_flow = k * (prior[b, below, :] - p[b])
-            up_flow = k_up * (p[b] - prior[b, above, :])
-            side_flow = h[b] * (p_right[b] - p[b]) - h_left[b] * (p[b] - p_left[b])
-            r_out[b, here, :] += (down_flow - up_flow) + side_flow
-            diag_out[b, part, :] += LAM + (k + k_up) + (h[b] + h_left[b])
-        return carry
-
-    lax.fori_loop(0, steps, flows, 0, unroll=UF)
+    last = blocks - 1
+
+    def outer(pair, carry):
+        for strip in (2 * pair, 2 * pair + 1):
+            to_grid(weights, pulls, diag_out, r_out, strip, (0, last))
+        return carry
+
+    def ends(n, carry):
+        to_grid(weights, pulls, diag_out, r_out, n * (rows // TS - 1), range(1, last))
+        return carry
+
+    lax.fori_loop(0, rows // TS // 2, outer, 0)
+    lax.fori_loop(0, 2, ends, 0)
+
+    def outer_flows(i, carry):
+        add_flows(r_out, diag_out, prior, kx, ky, side_p, left_k, i, (0, last))
+        return carry
+
+    def end_flows(n, carry):
+        i = n * (steps - 1)
+        add_flows(r_out, diag_out, prior, kx, ky, side_p, left_k, i, range(1, last))
+        return carry
+
+    lax.fori_loop(0, steps, outer_flows, 0, unroll=UO)
+    lax.fori_loop(0, 2, end_flows, 0)
 
     zeros = jnp.zeros((8, LANES), F32)
     for i, out, row in ((0, up_out, 0), (steps - 1, down_out, 7)):
@@ -321,20 +354,17 @@
     slots = got.shape[0]
     vmem = pl.BlockSpec(memory_space=pltpu.VMEM)
     padded, plain = (blocks, rows + 2 * PAD, LANES), (blocks, rows, LANES)
-    shapes = (padded, plain, padded, plain, (2, cols), (2, cols), (2, rows), (2, rows))
-    in_tiles = pltpu.VMEM((cells // LANES, LANES), F32)
+    in_tiles = (cells // LANES, LANES)
+    shapes = (padded, plain, padded, padded, plain, in_tiles, in_tiles, (2, cols), (2, cols), (2, rows), (2, rows))
     return pl.pallas_call(
         join_kernel,
         out_shape=[jax.ShapeDtypeStruct(s, F32) for s in shapes],
         in_specs=[pl.BlockSpec(memory_space=pltpu.SMEM)] + [vmem] * 8,
         out_specs=[vmem] * len(shapes),
         scratch_shapes=[
-            pltpu.VMEM(padded, F32),
             pltpu.VMEM((slots, 8, LANES), jnp.int32),
             pltpu.SMEM((slots, 8, LANES), jnp.int32),
-            in_tiles,
-            in_tiles,
-            in_tiles,
+            pltpu.VMEM(in_tiles, F32),
             pltpu.VMEM((rows, LANES), F32),
             pltpu.VMEM((rows, LANES), F32),
             pltpu.SemaphoreType.DMA,
@@ -343,6 +373,36 @@
         cost_estimate=pl.CostEstimate(flops=30 * cells, bytes_accessed=24 * cells, transcendentals=0),
         name="join",
     )(flags, got, prior, kx, ky, from_up, from_down, from_left, from_right)
+
+
+def fill_kernel(weights, pulls, prior, kx, ky, r_in, diag_in, r, diag):
+    blocks, rows = diag.shape[0], diag.shape[1]
+    inner = range(1, blocks - 1)
+
+    def grid_step(strip, carry):
+        to_grid(weights, pulls, diag, r, strip, inner)
+        return carry
+
+    def flow_step(i, carry):
+        add_flows(r, diag, prior, kx, ky, None, None, i, inner)
+        return carry
+
+    lax.fori_loop(0, rows // TS, grid_step, 0)
+    lax.fori_loop(0, rows // 8, flow_step, 0, unroll=UF)
+
+
+def fill(weights, pulls, prior, kx, ky, r, diag):
+    vmem = pl.BlockSpec(memory_space=pltpu.VMEM)
+    return pl.pallas_call(
+        fill_kernel,
+        out_shape=[jax.ShapeDtypeStruct(x.shape, F32) for x in (r, diag)],
+        in_specs=[vmem] * 7,
+        out_specs=[vmem] * 2,
+        input_output_aliases={5: 0, 6: 1},
+        compiler_params=pltpu.CompilerParams(vmem_limit_bytes=SMALL_VMEM),
+        cost_estimate=pl.CostEstimate(flops=1 << 25, bytes_accessed=16 << 20, transcendentals=0),
+        name="fill",
+    )(weights, pulls, prior, kx, ky, r, diag)
 
 
 def vertical(field, kx, b, i):
@@ -603,9 +663,7 @@
 
 def send(strip, axis, by):
     count = lax.axis_size(axis)
-    return lax.ppermute(
-        strip, axis, [(i, i + by) for i in range(count) if 0 <= i + by < count]
-    )
+    return lax.ppermute(strip, axis, [(i, (i + by) % count) for i in range(count)])
 
 
 def exchange(up, down, left, right):
@@ -622,13 +680,16 @@
     flags = jnp.stack(
         [row == row_count - 1, col == col_count - 1, row * col_count + col]
     ).astype(jnp.int32)[None]
-    own = strips(prior, edge_rows, edge_cols)
+    own = strips(flags, prior, edge_rows, edge_cols)
     early = exchange(*own)
     payload = pack(tile_owner, tile_offset, tile_count, depth_tiles[0], conf_tiles[0], col_count)
     payload, early, flags = lax.optimization_barrier((payload, early, flags))
     got = lax.all_to_all(payload, "col", split_axis=0, concat_axis=0, tiled=True)
-    r, diag, kx, ky, *edges = join(flags, got, prior, edge_rows, edge_cols, *early)
+    r, diag, blocked, kx, ky, weights, pulls, *edges = join(
+        flags, got, prior, edge_rows, edge_cols, *early
+    )
     late = exchange(*edges)
+    r, diag = fill(weights, pulls, blocked, kx, ky, r, diag)
     r, q, s, table = moments(
         row_count * col_count, r, diag, kx, ky, *late, early[2], edges[2], edges[3], own[3]
     )

time: 139 us -> 123 us (0.88)
  blocking collectives: 81.3 us -> 67.6 us
  Pallas kernels: 25.8 us -> 33.2 us
  starting transfers between devices: 26 us -> 20.2 us
  waiting for transfers between devices: 3.06 us -> 0.02 us
    all_to_all x1, blocking collectives: 62.8 us -> 52.9 us  [shards(): lax.all_to_all(payload, 'col', split_axis=0, concat_axis=0, tiled=True)]
    ppermute x8, starting transfers between devices: 26 us -> 20.2 us  [send(): lax.ppermute(strip, axis, [(i, (i + by) % count) for i in range(count)])]
    pallas_call x0 -> x1, Pallas kernels: none -> 5.81 us  [fill(): pl.pallas_call(fill_kernel, out_shape=[jax.ShapeDtypeStruct(x.shape, F32)...]
    all_to_all x1, blocking collectives: 18.6 us -> 14.7 us  [shards(): lax.all_to_all(table, ('row', 'col'), split_axis=0, concat_axis=0, tiled=...]
    ppermute x8, waiting for transfers between devices: 3.06 us -> 0.02 us  [send(): lax.ppermute(strip, axis, [(i, (i + by) % count) for i in range(count)])]
    pallas_call x1, Pallas kernels: 13.4 us -> 15.1 us  [join(): pl.pallas_call(join_kernel, out_shape=[jax.ShapeDtypeStruct(s, F32) for s...]
  transfers between devices with their start and end apart: 8 -> 8, of which waited for: 1 -> 0; matrix products, arithmetic and copies ran while one was open for 0% -> 0% of each run, Pallas kernels for 1% -> 6%
where the time goes in v3:
time: 123 us
  blocking collectives  67.6 us (55%)
  Pallas kernels  33.2 us (27%)
  starting transfers between devices  20.2 us (16%)
  between operations  1.47 us (1%)
    all_to_all x1, blocking collectives, shards(): lax.all_to_all(payload, 'col', split_axis=0, concat_axis=0, tiled=True)  52.9 us
    ppermute x8, starting transfers between devices, send(): lax.ppermute(strip, axis, [(i, (i + by) % count) for i in range(count)])  20.2 us
    pallas_call x1, Pallas kernels, join(): pl.pallas_call(join_kernel, out_shape=[jax.ShapeDtypeStruct(s, F32) for s...  15.1 us
    all_to_all x1, blocking collectives, shards(): lax.all_to_all(table, ('row', 'col'), split_axis=0, concat_axis=0, tiled=...  14.7 us
    pallas_call x1, Pallas kernels, fill(): pl.pallas_call(fill_kernel, out_shape=[jax.ShapeDtypeStruct(x.shape, F32)...  5.81 us
    pallas_call x1, Pallas kernels, moments(): pl.pallas_call(moments_kernel, out_shape=[jax.ShapeDtypeStruct(r.shape, F...  4.75 us
    pallas_call x1, Pallas kernels, finish(): pl.pallas_call(functools.partial(finish_kernel, col_count), out_shape=[ja...  3.75 us
  transfers between devices with their start and end apart: 8, of which 0 were waited for; matrix products, arithmetic and copies ran while one was open for 0% of the time, Pallas kernels for 6%

profile of v3, /device:TPU:1, one launch (start us, length us, event | category | flops | bytes accessed | tf_op | source)
XLA Modules:
  0.0 123.2 jit_solution(2675096460168820190)
XLA Ops:
  0.6 0.6 add_bitcast_fusion.flags.where_ref
  1.3 0.0 copy-start.3
  1.3 0.0 copy-start.4
  1.3 0.0 copy-start.7
  1.3 0.0 copy-start.8
  1.3 2.2 %strips.1 = (f32[1,1024]{1,0:T(1,128)}, f32[2,1024]{1,0:T(2,128)}, f32[1,512]{1,0:T(1,128)}, f32[2,512]{1,0:T(2,128)}) custom-call(s32[1,3]{1,0:T(1,128)} %add_bitcast_fusion.flags.where_ref, f32[512,1024]{1,0:T(8,128)} %prior.1, f32[512,1024]{1,0:T(8,128)} %prior.1, f32[512,1024]{1,0:T(8,128)} %kx_in.1, f32[512,1024]{1,0:T(8,128)} %prior.1, ...), custom_call_target="tpu_custom_call" | custom-call | tf_op jit(solution)/shard_map/strips/pallas_call | solution.py:148
  3.5 2.6 %collective-permute-start = (f32[2,1024]{1,0:T(2,128)}, f32[2,1024]{1,0:T(2,128)S(1)}, u32[]{:S(2)}, u32[]{:S(2)}) collective-permute-start(f32[2,1024]{1,0:T(2,128)} %get-tuple-element.29), channel_id=1, source_target_pairs={{0,16},{16,32},{32,48},{48,64},{64,80},{80,96},{96,112},{112,0},{1... | collective-permute-start | bytes 24584 | tf_op jit(solution)/shard_map/ppermute | solution.py:666
  6.1 0.0 collective-permute-start.1
  6.1 1.3 %collective-permute-start.2 = (f32[2,512]{1,0:T(2,128)}, f32[2,512]{1,0:T(2,128)S(1)}, u32[]{:S(2)}, u32[]{:S(2)}) collective-permute-start(f32[2,512]{1,0:T(2,128)} %get-tuple-element.31.own_ky), channel_id=1, source_target_pairs={{0,1},{1,2},{2,3},{3,4},{4,5},{5,6},{6,7},{7,8},{8,9},{9,10},{10,1... | collective-permute-start | bytes 12296 | tf_op jit(solution)/shard_map/ppermute | solution.py:666
  7.4 4.9 %collective-permute-start.3 = (f32[1,512]{1,0:T(1,128)}, f32[1,512]{1,0:T(1,128)S(1)}, u32[]{:S(2)}, u32[]{:S(2)}) collective-permute-start(f32[1,512]{1,0:T(1,128)} %get-tuple-element.32), channel_id=1, source_target_pairs={{0,15},{1,0},{2,1},{3,2},{4,3},{5,4},{6,5},{7,6},{8,7},{9,8},{10,9... | collective-permute-start | bytes 6152 | tf_op jit(solution)/shard_map/ppermute | solution.py:666
  13.0 0.0 copy-done.3
  13.0 0.0 copy-done.4
  13.0 0.0 copy-done.7
  13.0 0.0 copy-done.8
  13.0 1.6 %pack.1 = bf16[16,1040,128]{2,1,0:T(8,128)(2,1)S(1)} custom-call(s32[1,512]{1,0:T(1,128)S(1)} %copy-done.7, s32[1,1]{1,0:T(1,128)S(6)} %copy.17.count_ref, s32[1,512]{1,0:T(1,128)S(1)} %copy-done.8, bf16[512,1024]{1,0:T(8,128)(2,1)S(1)} %bitcast.11, bf16[512,1024]{1,0:T(8,128)(2,1)S(1)} %bitcast.12), custom_call_target="tpu_custom_call" | custom-call | flops 1048576 | bytes 4194304 | tf_op jit(solution)/shard_map/pack/pallas_call | solution.py:116
  14.6 0.0 copy-start
  14.6 0.0 copy-start.1
  14.6 0.0 copy-start.2
  14.6 0.0 copy-start.5
  14.6 0.0 collective-permute-done.3.from_right
  14.7 0.0 collective-permute-done.1.from_down
  14.7 0.0 collective-permute-done.2.from_left.k_left
  14.7 0.0 collective-permute-done.from_up
  14.7 52.9 %all_to_all.16.got = bf16[16,1040,128]{2,1,0:T(8,128)(2,1)S(1)} all-to-all(bf16[16,1040,128]{2,1,0:T(8,128)(2,1)S(1)} %pack.1), channel_id=1, replica_groups=mesh['row'=8,'col'=16] {'col'}, dimensions={0} | all-to-all | bytes 8519680 | tf_op jit(solution)/shard_map/all_to_all | solution.py:687
  67.6 0.0 copy-done
  67.6 0.0 copy-done.1
  67.6 0.0 copy-done.2
  67.6 0.0 copy-done.5
  67.6 15.1 %join.1 = (f32[8,528,128]{2,1,0:T(8,128)S(1)}, f32[8,512,128]{2,1,0:T(8,128)S(1)}, f32[8,528,128]{2,1,0:T(8,128)S(1)}, f32[8,528,128]{2,1,0:T(8,128)S(1)}, f32[8...) custom-call(s32[1,3]{1,0:T(1,128)S(1)} %copy-done.5, ...), custom_call_target="tpu_custom_call" | custom-call | flops 15728640 | bytes 12582912 | tf_op jit(solution)/shard_map/join/pallas_call | solution.py:359
  82.7 6.6 %collective-permute-start.4 = (f32[2,1024]{1,0:T(2,128)S(1)}, f32[2,1024]{1,0:T(2,128)S(1)}, u32[]{:S(2)}, u32[]{:S(2)}) collective-permute-start(f32[2,1024]{1,0:T(2,128)S(1)} %get-tuple-element.48), channel_id=1, source_target_pairs={{0,16},{16,32},{32,48},{48,64},{64,80},{80,96},{96,112},{112,0},{1... | collective-permute-start | bytes 24584 | tf_op jit(solution)/shard_map/ppermute | solution.py:666
  89.3 0.0 collective-permute-start.5
  89.3 0.3 collective-permute-start.6
  89.6 4.5 %collective-permute-start.7 = (f32[2,512]{1,0:T(2,128)S(1)}, f32[2,512]{1,0:T(2,128)S(1)}, u32[]{:S(2)}, u32[]{:S(2)}) collective-permute-start(f32[2,512]{1,0:T(2,128)S(1)} %get-tuple-element.51.own_left), channel_id=1, source_target_pairs={{0,15},{1,0},{2,1},{3,2},{4,3},{5,4},{6,5},{7,6},{8,7},{9,8},{10,9... | collective-permute-start | bytes 12296 | tf_op jit(solution)/shard_map/ppermute | solution.py:666
  94.1 0.0 copy-start.6
  94.1 5.8 %fill.1 = (f32[8,528,128]{2,1,0:T(8,128)S(1)}, f32[8,512,128]{2,1,0:T(8,128)S(1)}) custom-call(f32[4096,128]{1,0:T(8,128)S(1)} %get-tuple-element.39.weights, f32[4096,128]{1,0:T(8,128)S(1)} %get-tuple-element.40.pulls, f32[8,528,128]{2,1,0:T(8,128)S(1)} %get-tuple-element.41.prior, ...), custom_call_target="tpu_custom_call", output_to_operand_aliasing={{0}: (5, {}), {1}: (6, {})} | custom-call | flops 33554432 | bytes 16777216 | tf_op jit(solution)/shard_map/fill/pallas_call | solution.py:396
  99.9 0.0 collective-permute-done.6.r_left
  99.9 0.0 collective-permute-done.7.r_right
  100.0 0.0 collective-permute-done.4.r_up
  100.0 0.0 collective-permute-done.5.r_down
  100.0 0.0 copy-done.6
  100.0 4.8 %moments.1 = (f32[8,528,128]{2,1,0:T(8,128)S(1)}, f32[8,528,128]{2,1,0:T(8,128)S(1)}, f32[8,512,128]{2,1,0:T(8,128)S(1)}, f32[128,128]{1,0:T(8,128)S(1)}) custom-call(f32[8,528,128]{2,1,0:T(8,128)S(1)} %get-tuple-element.46.r_in, f32[8,512,128]{2,1,0:T(8,128)S(1)} %get-tuple-element.47.diag, ...), custom_call_target="tpu_custom_call", output_to_operand_aliasing={{0}: (0, {})} | custom-call | flops 20971520 | bytes 12582912 | tf_op jit(solution)/shard_map/moments/pallas_call | solution.py:524
  104.7 14.7 %all_to_all.17 = f32[128,1,128]{2,1,0:T(1,128)S(1)} all-to-all(f32[128,1,128]{2,1,0:T(1,128)S(1)} %bitcast.14), channel_id=1, replica_groups=mesh['row'=8,'col'=16] {'row','col'}, dimensions={0} | all-to-all | bytes 131072 | tf_op jit(solution)/shard_map/all_to_all | solution.py:696
  119.4 3.7 %finish.1 = (f32[512,1024]{1,0:T(8,128)}, f32[512,1024]{1,0:T(8,128)}) custom-call(s32[1,3]{1,0:T(1,128)S(1)} %copy-done.5, f32[128,128]{1,0:T(8,128)S(1)} %bitcast.13, f32[512,1024]{1,0:T(8,128)S(1)} %copy-done, f32[8,528,128]{2,1,0:T(8,128)S(1)} %get-tuple-element.53.r, f32[8,528,128]{2,1,0:T(8,128)S(1)} %get-tuple-element.54.q, ...), custom_call_target="tpu_custom_call" | custom-call | flops 4194304 | bytes 12582912 | tf_op jit(solution)/shard_map/finish/pallas_call | solution.py:647
Async XLA Ops:
  1.3 11.7 %copy-start.3 = (bf16[1,512,1024]{2,1,0:T(8,128)(2,1)S(1)}, bf16[1,512,1024]{2,1,0:T(8,128)(2,1)}, u32[]{:S(2)}) copy-start(bf16[1,512,1024]{2,1,0:T(8,128)(2,1)} %param.8) | copy-start | bytes 3145732
  1.3 11.7 %copy-start.4 = (bf16[1,512,1024]{2,1,0:T(8,128)(2,1)S(1)}, bf16[1,512,1024]{2,1,0:T(8,128)(2,1)}, u32[]{:S(2)}) copy-start(bf16[1,512,1024]{2,1,0:T(8,128)(2,1)} %param.9) | copy-start | bytes 3145732
  1.3 11.7 %copy-start.7 = (s32[1,512]{1,0:T(1,128)S(1)}, s32[1,512]{1,0:T(1,128)}, u32[]{:S(2)}) copy-start(s32[1,512]{1,0:T(1,128)} %owner_ref.1) | copy-start | bytes 6148
  1.3 11.7 %copy-start.8 = (s32[1,512]{1,0:T(1,128)S(1)}, s32[1,512]{1,0:T(1,128)}, u32[]{:S(2)}) copy-start(s32[1,512]{1,0:T(1,128)} %offset_ref.1) | copy-start | bytes 6148
  3.5 11.2 %collective-permute-start = (f32[2,1024]{1,0:T(2,128)}, f32[2,1024]{1,0:T(2,128)S(1)}, u32[]{:S(2)}, u32[]{:S(2)}) collective-permute-start(f32[2,1024]{1,0:T(2,128)} %get-tuple-element.29), channel_id=1, source_target_pairs={{0,16},{16,32},{32,48},{48,64},{64,80},{80,96},{96,112},{112,0},{1... | collective-permute-start | bytes 24584 | tf_op jit(solution)/shard_map/ppermute | solution.py:666
  6.1 8.6 %collective-permute-start.1 = (f32[1,1024]{1,0:T(1,128)}, f32[1,1024]{1,0:T(1,128)S(1)}, u32[]{:S(2)}, u32[]{:S(2)}) collective-permute-start(f32[1,1024]{1,0:T(1,128)} %get-tuple-element.30), channel_id=1, source_target_pairs={{0,112},{16,0},{32,16},{48,32},{64,48},{80,64},{96,80},{112,96},{1... | collective-permute-start | bytes 12296 | tf_op jit(solution)/shard_map/ppermute | solution.py:666
  6.1 8.6 %collective-permute-start.2 = (f32[2,512]{1,0:T(2,128)}, f32[2,512]{1,0:T(2,128)S(1)}, u32[]{:S(2)}, u32[]{:S(2)}) collective-permute-start(f32[2,512]{1,0:T(2,128)} %get-tuple-element.31.own_ky), channel_id=1, source_target_pairs={{0,1},{1,2},{2,3},{3,4},{4,5},{5,6},{6,7},{7,8},{8,9},{9,10},{10,1... | collective-permute-start | bytes 12296 | tf_op jit(solution)/shard_map/ppermute | solution.py:666
  7.4 7.3 %collective-permute-start.3 = (f32[1,512]{1,0:T(1,128)}, f32[1,512]{1,0:T(1,128)S(1)}, u32[]{:S(2)}, u32[]{:S(2)}) collective-permute-start(f32[1,512]{1,0:T(1,128)} %get-tuple-element.32), channel_id=1, source_target_pairs={{0,15},{1,0},{2,1},{3,2},{4,3},{5,4},{6,5},{7,6},{8,7},{9,8},{10,9... | collective-permute-start | bytes 6152 | tf_op jit(solution)/shard_map/ppermute | solution.py:666
  14.6 53.0 %copy-start = (f32[512,1024]{1,0:T(8,128)S(1)}, f32[512,1024]{1,0:T(8,128)}, u32[]{:S(2)}) copy-start(f32[512,1024]{1,0:T(8,128)} %prior.1) | copy-start | bytes 6291460
  14.6 53.0 %copy-start.1 = (f32[512,1024]{1,0:T(8,128)S(1)}, f32[512,1024]{1,0:T(8,128)}, u32[]{:S(2)}) copy-start(f32[512,1024]{1,0:T(8,128)} %kx_in.1) | copy-start | bytes 6291460
  14.6 53.0 %copy-start.2 = (f32[512,1024]{1,0:T(8,128)S(1)}, f32[512,1024]{1,0:T(8,128)}, u32[]{:S(2)}) copy-start(f32[512,1024]{1,0:T(8,128)} %ky_in.1) | copy-start | bytes 6291460
  14.6 53.0 %copy-start.5 = (s32[1,3]{1,0:T(1,128)S(1)}, s32[1,3]{1,0:T(1,128)}, u32[]{:S(2)}) copy-start(s32[1,3]{1,0:T(1,128)} %add_bitcast_fusion.flags.where_ref) | copy-start | bytes 40
  82.7 17.2 %collective-permute-start.4 = (f32[2,1024]{1,0:T(2,128)S(1)}, f32[2,1024]{1,0:T(2,128)S(1)}, u32[]{:S(2)}, u32[]{:S(2)}) collective-permute-start(f32[2,1024]{1,0:T(2,128)S(1)} %get-tuple-element.48), channel_id=1, source_target_pairs={{0,16},{16,32},{32,48},{48,64},{64,80},{80,96},{96,112},{112,0},{1... | collective-permute-start | bytes 24584 | tf_op jit(solution)/shard_map/ppermute | solution.py:666
  89.3 10.6 %collective-permute-start.5 = (f32[2,1024]{1,0:T(2,128)S(1)}, f32[2,1024]{1,0:T(2,128)S(1)}, u32[]{:S(2)}, u32[]{:S(2)}) collective-permute-start(f32[2,1024]{1,0:T(2,128)S(1)} %get-tuple-element.49), channel_id=1, source_target_pairs={{0,112},{16,0},{32,16},{48,32},{64,48},{80,64},{96,80},{112,96},{1... | collective-permute-start | bytes 24584 | tf_op jit(solution)/shard_map/ppermute | solution.py:666
  89.3 10.6 %collective-permute-start.6 = (f32[2,512]{1,0:T(2,128)S(1)}, f32[2,512]{1,0:T(2,128)S(1)}, u32[]{:S(2)}, u32[]{:S(2)}) collective-permute-start(f32[2,512]{1,0:T(2,128)S(1)} %get-tuple-element.50.own_right), channel_id=1, source_target_pairs={{0,1},{1,2},{2,3},{3,4},{4,5},{5,6},{6,7},{7,8},{8,9},{9,10},{10,1... | collective-permute-start | bytes 12296 | tf_op jit(solution)/shard_map/ppermute | solution.py:666
  89.6 10.3 %collective-permute-start.7 = (f32[2,512]{1,0:T(2,128)S(1)}, f32[2,512]{1,0:T(2,128)S(1)}, u32[]{:S(2)}, u32[]{:S(2)}) collective-permute-start(f32[2,512]{1,0:T(2,128)S(1)} %get-tuple-element.51.own_left), channel_id=1, source_target_pairs={{0,15},{1,0},{2,1},{3,2},{4,3},{5,4},{6,5},{7,6},{8,7},{9,8},{10,9... | collective-permute-start | bytes 12296 | tf_op jit(solution)/shard_map/ppermute | solution.py:666
  94.1 5.9 %copy-start.6 = (f32[2,512]{1,0:T(2,128)S(1)}, f32[2,512]{1,0:T(2,128)}, u32[]{:S(2)}) copy-start(f32[2,512]{1,0:T(2,128)} %get-tuple-element.31.own_ky) | copy-start | bytes 12292

commit v4 on v3

--- a/solution.py
+++ b/solution.py
@@ -1,5 +1,3 @@
-import functools
-
 import jax
 import jax.numpy as jnp
 from jax import lax
@@ -16,6 +14,10 @@
 PAD = 8
 F32 = jnp.float32
 SMALL_VMEM = 16 * 1024 * 1024
+
+
+def is_last(axis):
+    return lax.axis_index(axis) == lax.axis_size(axis) - 1
 
 
 def lane_ids(shape):
@@ -126,20 +128,20 @@
 
 
 def strips_kernel(
-    flags, top, bottom, kx_bottom, left, right, ky_right, up_out, down_out, left_out, right_out
+    top, bottom, kx_bottom, left, right, ky_right, up_out, down_out, left_out, right_out
 ):
     up_out[...] = top[0:1, :]
     down_out[0:1, :] = bottom[7:8, :]
-    down_out[1:2, :] = jnp.where(flags[0, 0] == 1, 0.0, kx_bottom[7:8, :])
+    down_out[1:2, :] = jnp.where(is_last("row"), 0.0, kx_bottom[7:8, :])
     lane = lane_ids(left.shape)
-    left_out[...] = left[...].T[0:1, :]
     both = jnp.where(lane == LANES - 1, right[...], pltpu.roll(ky_right[...], LANES - 1, axis=1))
-    turned = both.T
+    turned = jnp.where(lane == 0, left[...], both).T
+    left_out[...] = turned[0:1, :]
     right_out[0:1, :] = turned[LANES - 1 : LANES, :]
-    right_out[1:2, :] = jnp.where(flags[0, 1] == 1, 0.0, turned[LANES - 2 : LANES - 1, :])
-
-
-def strips(flags, prior, kx, ky):
+    right_out[1:2, :] = jnp.where(is_last("col"), 0.0, turned[LANES - 2 : LANES - 1, :])
+
+
+def strips(prior, kx, ky):
     rows, cols = prior.shape
     last_rows = pl.BlockSpec((8, cols), lambda i: (rows // 8 - 1, 0))
     last_cols = pl.BlockSpec((rows, LANES), lambda i: (0, cols // LANES - 1))
@@ -150,23 +152,71 @@
         grid=(1,),
         out_shape=[jax.ShapeDtypeStruct(s, F32) for s in shapes],
         in_specs=[
-            pl.BlockSpec(memory_space=pltpu.SMEM), whole((8, cols)), last_rows, last_rows, whole((rows, LANES)), last_cols, last_cols,
+            whole((8, cols)), last_rows, last_rows, whole((rows, LANES)), last_cols, last_cols,
         ],
         out_specs=[whole(s) for s in shapes],
         name="strips",
-    )(flags, prior, prior, kx, prior, prior, ky)
+    )(prior, prior, kx, prior, prior, ky)
+
+
+def arrange_kernel(prior_in, kx_in, ky_in, tiles, prior, kx, ky):
+    blocks, rows = ky.shape[0], ky.shape[1]
+
+    def one_strip(strip, carry):
+        base = pl.multiple_of(TS * strip, TS)
+        here = pl.ds(base, TS)
+        padded = pl.ds(pl.multiple_of(PAD + base, 8), TS)
+        for b in range(blocks):
+            lanes = slice(b * LANES, (b + 1) * LANES)
+            prior[b, padded, :] = prior_in[here, lanes]
+            kx[b, padded, :] = kx_in[here, lanes]
+            ky[b, here, :] = ky_in[here, lanes]
+        for b in range(blocks):
+            four = swap_blocks([prior[b, grid_rows(PAD, strip, a), :] for a in range(4)])
+            for place, part in zip(tiles_of(strip, b, blocks), four):
+                tiles[place] = part
+        return carry
+
+    lax.fori_loop(0, rows // TS, one_strip, 0, unroll=2)
+
+    @pl.when(is_last("row"))
+    def _():
+        for b in range(blocks):
+            kx[b, PAD + rows - 1 : PAD + rows, :] = jnp.zeros((1, LANES), F32)
+
+    @pl.when(is_last("col"))
+    def _():
+        edge = ky[blocks - 1]
+        ky[blocks - 1] = jnp.where(lane_ids(edge.shape) == LANES - 1, 0.0, edge)
+
+
+def arrange(prior, kx, ky):
+    rows, cols = prior.shape
+    blocks = cols // LANES
+    vmem = pl.BlockSpec(memory_space=pltpu.VMEM)
+    padded, plain = (blocks, rows + 2 * PAD, LANES), (blocks, rows, LANES)
+    shapes = ((rows * cols // (8 * LANES), 8, LANES), padded, padded, plain)
+    return pl.pallas_call(
+        arrange_kernel,
+        out_shape=[jax.ShapeDtypeStruct(s, F32) for s in shapes],
+        in_specs=[vmem] * 3,
+        out_specs=[vmem] * 4,
+        compiler_params=pltpu.CompilerParams(vmem_limit_bytes=SMALL_VMEM),
+        cost_estimate=pl.CostEstimate(flops=1 << 22, bytes_accessed=14 << 20, transcendentals=0),
+        name="arrange",
+    )(prior, kx, ky)
 
 
 BATCH = 16
 UF = 4
-UO = 8
+UO = 16
 US = 16
 UM = 8
 
 
-def tile_rows(strip, b, blocks):
-    first = (strip * (blocks * LANES // TS) + 4 * b) * 8
-    return [pl.ds(pl.multiple_of(first + 8 * q, 8), 8) for q in range(4)]
+def tiles_of(strip, b, blocks):
+    first = strip * (blocks * LANES // TS) + 4 * b
+    return [first + q for q in range(4)]
 
 
 def grid_rows(pad, strip, a):
@@ -175,9 +225,9 @@
 
 def to_grid(weights, pulls, diag, r, strip, chosen):
     for b in chosen:
-        places = tile_rows(strip, b, diag.shape[0])
+        places = tiles_of(strip, b, diag.shape[0])
         for total, out, pad in ((weights, diag, 0), (pulls, r, PAD)):
-            for a, part in enumerate(swap_blocks([total[place, :] for place in places])):
+            for a, part in enumerate(swap_blocks([total[place] for place in places])):
                 out[b, grid_rows(pad, strip, a), :] = part
 
 
@@ -205,9 +255,9 @@
 
 
 def join_kernel(
-    flags, got, prior_in, kx_in, ky_in, from_up, from_down, from_left, from_right,
-    r_out, diag_out, prior, kx, ky, weights, pulls, up_out, down_out, left_out, right_out,
-    table_v, table, tiles, side_p, left_k, table_sem,
+    got, tiles, prior_in, kx_in, ky, from_up, from_down, from_left, from_right,
+    r_out, diag_out, prior, kx, weights, pulls, up_out, down_out, left_out, right_out,
+    table_v, table, side_p, left_k, table_sem,
 ):
     slots, rows_in = got.shape[0], got.shape[1]
     cells = (rows_in - META) // 2
@@ -215,21 +265,20 @@
     steps = rows // 8
     for s in range(slots):
         fields = got[s, 2 * cells :, :].astype(F32)
-        target = fields[0:1, :] * 128.0 + fields[1:2, :] * 8.0
+        target = fields[0:1, :] * 16.0 + fields[1:2, :]
         table_v[s, 0:1, :] = target.astype(jnp.int32)
         table_v[s, 1:2, :] = fields[2:3, :].astype(jnp.int32)
     table_copy = pltpu.make_async_copy(table_v, table, table_sem)
     table_copy.start()
 
-    zero = jnp.zeros((TS, LANES), F32)
+    zero = jnp.zeros((8, LANES), F32)
 
     def clear(i, carry):
-        part = pl.ds(pl.multiple_of(i * TS, TS), TS)
-        weights[part, :] = zero
-        pulls[part, :] = zero
-        return carry
-
-    lax.fori_loop(0, rows * blocks // TS, clear, 0)
+        weights[i] = zero
+        pulls[i] = zero
+        return carry
+
+    lax.fori_loop(0, tiles.shape[0], clear, 0, unroll=8)
     side_p[...] = side_columns(from_left[0:1, :], from_right[...])
     left_k[...] = side_columns(from_left[1:2, :], from_left[1:2, :])
     for b in range(blocks):
@@ -239,22 +288,6 @@
         prior[b, PAD + rows : PAD + rows + 1, :] = from_down[0:1, lanes]
         r_out[b, PAD - 1 : PAD, :] = jnp.zeros((1, LANES), F32)
         r_out[b, PAD + rows : PAD + rows + 1, :] = jnp.zeros((1, LANES), F32)
-    def to_tiles(strip, carry):
-        base = pl.multiple_of(TS * strip, TS)
-        rows_here = pl.ds(base, TS)
-        padded = pl.ds(pl.multiple_of(PAD + base, 8), TS)
-        for b in range(blocks):
-            lanes = slice(b * LANES, (b + 1) * LANES)
-            prior[b, padded, :] = prior_in[rows_here, lanes]
-            kx[b, padded, :] = kx_in[rows_here, lanes]
-            ky[b, rows_here, :] = ky_in[rows_here, lanes]
-        for b in range(blocks):
-            four = swap_blocks([prior[b, grid_rows(PAD, strip, a), :] for a in range(4)])
-            for place, part in zip(tile_rows(strip, b, blocks), four):
-                tiles[place, :] = part
-        return carry
-
-    lax.fori_loop(0, rows // TS, to_tiles, 0)
     table_copy.wait()
 
     def one_slot(slot, carry):
@@ -269,29 +302,19 @@
                 confs = got[slot, pl.ds(cells + at, 16), :].astype(F32)
                 for side in range(2):
                     tile = first + 2 * pair + side
-                    place = pl.ds(pl.multiple_of(table[slot, 0, tile], 8), 8)
-                    error = depths[8 * side : 8 * side + 8] - tiles[place, :]
+                    place = table[slot, 0, tile]
+                    error = depths[8 * side : 8 * side + 8] - tiles[place]
                     weight = confs[8 * side : 8 * side + 8] / jnp.maximum(jnp.abs(error), HUBER)
                     places.append(place)
                     terms.append((weight, weight * error))
             for place, (weight, pull) in zip(places, terms):
-                weights[place, :] += weight
-                pulls[place, :] += pull
+                weights[place] += weight
+                pulls[place] += pull
             return carry
 
         return lax.fori_loop(0, (live + BATCH - 1) // BATCH, batch, carry)
 
     lax.fori_loop(0, slots, one_slot, 0)
-    @pl.when(flags[0, 0] == 1)
-    def _():
-        for b in range(blocks):
-            kx[b, PAD + rows - 1 : PAD + rows, :] = jnp.zeros((1, LANES), F32)
-
-    @pl.when(flags[0, 1] == 1)
-    def _():
-        edge = ky[blocks - 1]
-        ky[blocks - 1] = jnp.where(lane_ids(edge.shape) == LANES - 1, 0.0, edge)
-
     last = blocks - 1
 
     def outer(pair, carry):
@@ -330,49 +353,52 @@
     def sides(i, carry):
         here = at_row(i)
         part = pl.ds(pl.multiple_of(8 * i, 8), 8)
-        for b, edge, sign, target in ((0, 0, 1, side_p), (blocks - 1, LANES - 1, -1, left_k)):
+        edges = []
+        for b, edge, sign in ((0, 0, 1), (blocks - 1, LANES - 1, -1)):
             field = r_out[b, here, :]
             if edge:
                 across = pltpu.roll(ky[b, part, :] * field, 1, axis=1)
             else:
                 across = ky[b, part, :] * pltpu.roll(field, LANES - 1, axis=1)
             image = diag_out[b, part, :] * field - across - vertical(r_out, kx, b, i)
-            target[part, :] = jnp.where(lane == edge, image, pltpu.roll(field, sign % LANES, axis=1))
+            edges.append(
+                jnp.where(lane == edge, image, pltpu.roll(field, sign % LANES, axis=1))
+            )
+        side_p[part, :] = jnp.where(lane < LANES // 2, edges[0], edges[1])
         return carry
 
     lax.fori_loop(0, steps, sides, 0, unroll=US)
     turned = side_p[...].T
     left_out[0:1, :] = turned[1:2, :]
     left_out[1:2, :] = turned[0:1, :]
-    right_out[...] = left_k[...].T[LANES - 2 :, :]
-
-
-def join(flags, got, prior, kx, ky, from_up, from_down, from_left, from_right):
-    rows, cols = prior.shape
-    cells = rows * cols
-    blocks = cols // LANES
+    right_out[...] = turned[LANES - 2 :, :]
+
+
+def join(got, tiles, prior, kx, ky, from_up, from_down, from_left, from_right):
+    blocks, rows, _ = ky.shape
+    cols = blocks * LANES
     slots = got.shape[0]
     vmem = pl.BlockSpec(memory_space=pltpu.VMEM)
-    padded, plain = (blocks, rows + 2 * PAD, LANES), (blocks, rows, LANES)
-    in_tiles = (cells // LANES, LANES)
-    shapes = (padded, plain, padded, padded, plain, in_tiles, in_tiles, (2, cols), (2, cols), (2, rows), (2, rows))
+    strip_shapes = ((2, cols), (2, cols), (2, rows), (2, rows))
+    shapes = (prior.shape, ky.shape, prior.shape, kx.shape, tiles.shape, tiles.shape) + strip_shapes
+    cells = rows * cols
     return pl.pallas_call(
         join_kernel,
         out_shape=[jax.ShapeDtypeStruct(s, F32) for s in shapes],
-        in_specs=[pl.BlockSpec(memory_space=pltpu.SMEM)] + [vmem] * 8,
+        in_specs=[vmem] * 9,
         out_specs=[vmem] * len(shapes),
         scratch_shapes=[
             pltpu.VMEM((slots, 8, LANES), jnp.int32),
             pltpu.SMEM((slots, 8, LANES), jnp.int32),
-            pltpu.VMEM(in_tiles, F32),
             pltpu.VMEM((rows, LANES), F32),
             pltpu.VMEM((rows, LANES), F32),
             pltpu.SemaphoreType.DMA,
         ],
+        input_output_aliases={2: 2, 3: 3},
         compiler_params=pltpu.CompilerParams(vmem_limit_bytes=SMALL_VMEM),
         cost_estimate=pl.CostEstimate(flops=30 * cells, bytes_accessed=24 * cells, transcendentals=0),
         name="join",
-    )(flags, got, prior, kx, ky, from_up, from_down, from_left, from_right)
+    )(got, tiles, prior, kx, ky, from_up, from_down, from_left, from_right)
 
 
 def fill_kernel(weights, pulls, prior, kx, ky, r_in, diag_in, r, diag):
@@ -495,8 +521,7 @@
 
     sums = []
     for m in (m0, m1, m2, m3):
-        pair = fold((m, jnp.zeros_like(m)), 0)
-        sums.append(fold(pair, 1))
+        sums.append(fold(fold((m, jnp.zeros_like(m)), 0), 1))
     corners = ((0, 0), (last, 0), (0, rows - 1), (last, rows - 1))
 
     def cell(ref, corner, pad=PAD):
@@ -560,7 +585,7 @@
 
 
 def finish_kernel(
-    col_count, where_ref, table_ref, prior, r, q, s, height_hbm, residual_hbm,
+    table_ref, prior, r, q, s, height_hbm, residual_hbm,
     height, residual, coeff, sems,
 ):
     blocks, rows = s.shape[0], s.shape[1]
@@ -569,7 +594,7 @@
     field = [turned[i : i + 1, :] for i in range(20)]
 
     def at(index, down, right):
-        shift = -(down * col_count + right)
+        shift = -(down * lax.axis_size("col") + right)
         return pltpu.roll(jnp.broadcast_to(field[index], (8, devices)), shift % devices, axis=1)
 
     r_tl, r_tr, r_bl, r_br = 8, 9, 10, 11
@@ -580,21 +605,24 @@
         (at(kx_l, 0, 0) * at(ky_t, 1, -1) + at(ky_b, 0, -1) * at(kx_r, 0, -1)) * at(r_tr, 1, -1),
         (at(kx_r, 0, 0) * at(ky_t, 1, 0) + at(ky_b, 0, 0) * at(kx_l, 0, 1)) * at(r_tl, 1, 1),
     ]
-    pairs = [
-        [jnp.broadcast_to(field[i], (8, devices)), jnp.broadcast_to(field[4 + i], (8, devices))]
-        for i in range(4)
+    rows_of = [(table_ref[8 * n : 8 * n + 8, :], 0.0) for n in range(devices // 8)]
+    while len(rows_of) > 1:
+        rows_of = [add_pair(a, b) for a, b in zip(rows_of[::2], rows_of[1::2])]
+    total, rest = fold(rows_of[0], 0)
+    m = [
+        (total[0:1, i : i + 1], rest[0:1, i : i + 1] + total[0:1, 4 + i : 5 + i]) for i in range(4)
     ]
-    for corner in range(4):
-        pairs[3][1] = pairs[3][1] + extra[corner] * field[12 + corner]
-    m = [fold(tuple(pair), 1) for pair in pairs]
-    m = [tuple(part[0:1, 0:1] for part in pair) for pair in m]
+    mended = sum(extra[corner] * field[12 + corner] for corner in range(4))
+    mended = jnp.sum(mended, axis=1, keepdims=True)[0:1, :]
+    m[3] = (m[3][0], m[3][1] + mended)
     x1, x2, x3 = (quotient(m[i + 1], m[i]) for i in range(3))
     gap_1 = (x2[0] - x1[0]) + (x2[1] - x1[1])
     gap_2 = (x3[0] - x2[0]) + (x3[1] - x2[1])
     alpha = 1.0 / x1[0]
     ratio = 1.0 + gap_1 / x1[0]
     alpha_1 = gap_1 / (x2[0] * gap_2)
-    mine = lane_ids((8, devices)) == where_ref[0, 2]
+    place = lax.axis_index("row") * lax.axis_size("col") + lax.axis_index("col")
+    mine = lane_ids((8, devices)) == place
     values = [alpha + alpha_1 * ratio, alpha_1 * alpha]
     for corner in range(4):
         own = jnp.sum(jnp.where(mine, extra[corner], 0.0), axis=1, keepdims=True)
@@ -640,14 +668,14 @@
         copy.wait()
 
 
-def finish(where, table, prior, r, q, s, col_count):
+def finish(table, prior, r, q, s):
     blocks, rows, _ = s.shape
     cells = rows * blocks * LANES
     vmem = pl.BlockSpec(memory_space=pltpu.VMEM)
     return pl.pallas_call(
-        functools.partial(finish_kernel, col_count),
+        finish_kernel,
         out_shape=[jax.ShapeDtypeStruct((rows, blocks * LANES), F32)] * 2,
-        in_specs=[pl.BlockSpec(memory_space=pltpu.SMEM)] + [vmem] * 5,
+        in_specs=[vmem] * 5,
         out_specs=[pl.BlockSpec(memory_space=pltpu.HBM)] * 2,
         scratch_shapes=[
             pltpu.VMEM(s.shape, F32),
@@ -658,7 +686,7 @@
         compiler_params=pltpu.CompilerParams(vmem_limit_bytes=SMALL_VMEM),
         cost_estimate=pl.CostEstimate(flops=8 * cells, bytes_accessed=24 * cells, transcendentals=0),
         name="finish",
-    )(where, table, prior, r, q, s)
+    )(table, prior, r, q, s)
 
 
 def send(strip, axis, by):
@@ -675,26 +703,22 @@
 def shards(
     depth_tiles, conf_tiles, tile_owner, tile_offset, tile_count, prior, edge_rows, edge_cols
 ):
-    row, col = lax.axis_index("row"), lax.axis_index("col")
     row_count, col_count = lax.axis_size("row"), lax.axis_size("col")
-    flags = jnp.stack(
-        [row == row_count - 1, col == col_count - 1, row * col_count + col]
-    ).astype(jnp.int32)[None]
-    own = strips(flags, prior, edge_rows, edge_cols)
+    own = strips(prior, edge_rows, edge_cols)
     early = exchange(*own)
     payload = pack(tile_owner, tile_offset, tile_count, depth_tiles[0], conf_tiles[0], col_count)
-    payload, early, flags = lax.optimization_barrier((payload, early, flags))
+    arranged = arrange(prior, edge_rows, edge_cols)
+    payload, early, arranged = lax.optimization_barrier((payload, early, arranged))
     got = lax.all_to_all(payload, "col", split_axis=0, concat_axis=0, tiled=True)
-    r, diag, blocked, kx, ky, weights, pulls, *edges = join(
-        flags, got, prior, edge_rows, edge_cols, *early
-    )
+    ky = arranged[3]
+    r, diag, blocked, kx, weights, pulls, *edges = join(got, *arranged, *early)
     late = exchange(*edges)
     r, diag = fill(weights, pulls, blocked, kx, ky, r, diag)
     r, q, s, table = moments(
         row_count * col_count, r, diag, kx, ky, *late, early[2], edges[2], edges[3], own[3]
     )
     table = lax.all_to_all(table, ("row", "col"), split_axis=0, concat_axis=0, tiled=True)
-    return tuple(finish(flags, table, prior, r, q, s, col_count))
+    return tuple(finish(table, prior, r, q, s))
 
 
 def solution(mesh):

time: 123 us -> 119 us (0.967)
  Pallas kernels: 33.2 us -> 25.4 us
  starting transfers between devices: 20.2 us -> 24.2 us
  blocking collectives: 67.6 us -> 66 us
    pallas_call x1, Pallas kernels: 15.1 us -> 5.7 us  [join(): pl.pallas_call(join_kernel, out_shape=[jax.ShapeDtypeStruct(s, F32) for s...]
    ppermute x8, starting transfers between devices: 20.2 us -> 24.2 us  [send(): lax.ppermute(strip, axis, [(i, (i + by) % count) for i in range(count)])]
    pallas_call x1 -> x2, Pallas kernels: 3.75 us -> 5.36 us  [the longest x1 3.03 us: finish(): pl.pallas_call(finish_kernel, out_shape=[jax.ShapeDtypeStruct((rows, bloc...]
  transfers between devices with their start and end apart: 8 -> 8, of which waited for: 0 -> 0; matrix products, arithmetic and copies ran while one was open for 0% -> 0% of each run, Pallas kernels for 6% -> 8%
where the time goes in v4:
time: 119 us; the launch traced here: 118 us
  blocking collectives  66 us (55%)
  Pallas kernels  25.4 us (21%)
  starting transfers between devices  24.2 us (20%)
  between operations  1.49 us (1%)
  local copies, waits for them, and re-layouts  1.26 us (1%)
    all_to_all x1, blocking collectives, shards(): lax.all_to_all(payload, 'col', split_axis=0, concat_axis=0, tiled=True)  52.2 us
    ppermute x8, starting transfers between devices, send(): lax.ppermute(strip, axis, [(i, (i + by) % count) for i in range(count)])  24.2 us
    all_to_all x1, blocking collectives, shards(): lax.all_to_all(table, ('row', 'col'), split_axis=0, concat_axis=0, tiled=...  13.8 us
    pallas_call x1, Pallas kernels, fill(): pl.pallas_call(fill_kernel, out_shape=[jax.ShapeDtypeStruct(x.shape, F32)...  5.73 us
    pallas_call x1, Pallas kernels, join(): pl.pallas_call(join_kernel, out_shape=[jax.ShapeDtypeStruct(s, F32) for s...  5.7 us
    pallas_call x1, Pallas kernels, moments(): pl.pallas_call(moments_kernel, out_shape=[jax.ShapeDtypeStruct(r.shape, F...  4.83 us
    pallas_call x1, Pallas kernels, finish(): pl.pallas_call(finish_kernel, out_shape=[jax.ShapeDtypeStruct((rows, bloc...  3.03 us
  transfers between devices with their start and end apart: 8, of which 0 were waited for; matrix products, arithmetic and copies ran while one was open for 0% of the time, Pallas kernels for 8%

profile of v4, /device:TPU:1, one launch (start us, length us, event | category | flops | bytes accessed | tf_op | source)
XLA Modules:
  0.0 118.3 jit_solution(16043159969352071437)
XLA Ops:
  0.6 0.0 copy-start.7
  0.6 0.0 copy-start.6
  0.7 0.0 copy-start.4
  0.7 0.0 copy-start.3
  0.7 2.1 %strips.1 = (f32[1,1024]{1,0:T(1,128)}, f32[2,1024]{1,0:T(2,128)}, f32[1,512]{1,0:T(1,128)}, f32[2,512]{1,0:T(2,128)}) custom-call(f32[512,1024]{1,0:T(8,128)} %prior.1, f32[512,1024]{1,0:T(8,128)} %prior.1, f32[512,1024]{1,0:T(8,128)} %kx_in.1, f32[512,1024]{1,0:T(8,128)} %prior.1, f32[512,1024]{1,0:T(8,128)} %prior.1, f32[512,1024]{1,0:T(8,128)} %ky_in.1), custom_call_target="tpu_custom_call" | custom-call | tf_op jit(solution)/shard_map/strips/pallas_call | solution.py:150
  2.8 2.6 %collective-permute-start = (f32[2,1024]{1,0:T(2,128)}, f32[2,1024]{1,0:T(2,128)S(1)}, u32[]{:S(2)}, u32[]{:S(2)}) collective-permute-start(f32[2,1024]{1,0:T(2,128)} %get-tuple-element.35), channel_id=1, source_target_pairs={{0,16},{16,32},{32,48},{48,64},{64,80},{80,96},{96,112},{112,0},{1... | collective-permute-start | bytes 24584 | tf_op jit(solution)/shard_map/ppermute | solution.py:694
  5.4 0.0 collective-permute-start.1
  5.4 1.3 %collective-permute-start.2 = (f32[2,512]{1,0:T(2,128)}, f32[2,512]{1,0:T(2,128)S(1)}, u32[]{:S(2)}, u32[]{:S(2)}) collective-permute-start(f32[2,512]{1,0:T(2,128)} %get-tuple-element.37.own_ky), channel_id=1, source_target_pairs={{0,1},{1,2},{2,3},{3,4},{4,5},{5,6},{6,7},{7,8},{8,9},{9,10},{10,1... | collective-permute-start | bytes 12296 | tf_op jit(solution)/shard_map/ppermute | solution.py:694
  6.7 4.9 %collective-permute-start.3 = (f32[1,512]{1,0:T(1,128)}, f32[1,512]{1,0:T(1,128)S(1)}, u32[]{:S(2)}, u32[]{:S(2)}) collective-permute-start(f32[1,512]{1,0:T(1,128)} %get-tuple-element.38), channel_id=1, source_target_pairs={{0,15},{1,0},{2,1},{3,2},{4,3},{5,4},{6,5},{7,6},{8,7},{9,8},{10,9... | collective-permute-start | bytes 6152 | tf_op jit(solution)/shard_map/ppermute | solution.py:694
  12.3 0.0 copy-done.7
  12.3 0.0 copy-done.6
  12.3 0.0 copy-done.4
  12.3 0.0 copy-done.3
  12.3 0.0 copy-start
  12.3 0.0 copy-start.1
  12.3 0.0 copy-start.2
  12.4 1.6 %pack.1 = bf16[16,1040,128]{2,1,0:T(8,128)(2,1)S(1)} custom-call(s32[1,512]{1,0:T(1,128)S(1)} %copy-done.6, s32[1,1]{1,0:T(1,128)S(6)} %copy.21.count_ref, s32[1,512]{1,0:T(1,128)S(1)} %copy-done.7, bf16[512,1024]{1,0:T(8,128)(2,1)S(1)} %bitcast.6, bf16[512,1024]{1,0:T(8,128)(2,1)S(1)} %bitcast.7), custom_call_target="tpu_custom_call" | custom-call | flops 1048576 | bytes 4194304 | tf_op jit(solution)/shard_map/pack/pallas_call | solution.py:118
  14.0 0.0 copy-done
  14.0 0.6 copy-done.1
  14.5 0.6 copy-done.2
  15.2 2.3 %arrange.1 = (f32[512,8,128]{2,1,0:T(8,128)S(1)}, f32[8,528,128]{2,1,0:T(8,128)S(1)}, f32[8,528,128]{2,1,0:T(8,128)S(1)}, f32[8,512,128]{2,1,0:T(8,128)S(1)}) custom-call(f32[512,1024]{1,0:T(8,128)S(1)} %copy-done, f32[512,1024]{1,0:T(8,128)S(1)} %copy-done.1, f32[512,1024]{1,0:T(8,128)S(1)} %copy-done.2), custom_call_target="tpu_custom_call" | custom-call | flops 4194304 | bytes 14680064 | tf_op jit(solution)/shard_map/arrange/pallas_call | solution.py:199
  17.5 0.0 collective-permute-done.3.from_right
  17.5 0.0 collective-permute-done.1.from_down
  17.5 0.0 collective-permute-done.2.from_left.k_left
  17.6 0.0 collective-permute-done.from_up
  17.6 52.2 %all_to_all.16.got = bf16[16,1040,128]{2,1,0:T(8,128)(2,1)S(1)} all-to-all(bf16[16,1040,128]{2,1,0:T(8,128)(2,1)S(1)} %pack.1), channel_id=1, replica_groups=mesh['row'=8,'col'=16] {'col'}, dimensions={0} | all-to-all | bytes 8519680 | tf_op jit(solution)/shard_map/all_to_all | solution.py:712
  69.7 5.7 %join.1 = (f32[8,528,128]{2,1,0:T(8,128)S(1)}, f32[8,512,128]{2,1,0:T(8,128)S(1)}, f32[8,528,128]{2,1,0:T(8,128)S(1)}, f32[8,528,128]{2,1,0:T(8,128)S(1)}, f32[5...) custom-call(bf16[16,1040,128]{2,1,0:T(8,128)(2,1)S(1)} %all_to_all.1, ...), custom_call_target="tpu_custom_call", output_to_operand_aliasing={{2}: (2, {}), {3}: (3, {})} | custom-call | flops 15728640 | bytes 12582912 | tf_op jit(solution)/shard_map/join/pallas_call | solution.py:385
  75.4 10.6 %collective-permute-start.4 = (f32[2,1024]{1,0:T(2,128)S(1)}, f32[2,1024]{1,0:T(2,128)S(1)}, u32[]{:S(2)}, u32[]{:S(2)}) collective-permute-start(f32[2,1024]{1,0:T(2,128)S(1)} %get-tuple-element.60), channel_id=1, source_target_pairs={{0,16},{16,32},{32,48},{48,64},{64,80},{80,96},{96,112},{112,0},{1... | collective-permute-start | bytes 24584 | tf_op jit(solution)/shard_map/ppermute | solution.py:694
  86.0 0.0 collective-permute-start.5
  86.0 0.0 collective-permute-start.6
  86.0 4.8 %collective-permute-start.7 = (f32[2,512]{1,0:T(2,128)S(1)}, f32[2,512]{1,0:T(2,128)S(1)}, u32[]{:S(2)}, u32[]{:S(2)}) collective-permute-start(f32[2,512]{1,0:T(2,128)S(1)} %get-tuple-element.63.own_left), channel_id=1, source_target_pairs={{0,15},{1,0},{2,1},{3,2},{4,3},{5,4},{6,5},{7,6},{8,7},{9,8},{10,9... | collective-permute-start | bytes 12296 | tf_op jit(solution)/shard_map/ppermute | solution.py:694
  90.8 0.0 copy-start.5
  90.8 5.7 %fill.1 = (f32[8,528,128]{2,1,0:T(8,128)S(1)}, f32[8,512,128]{2,1,0:T(8,128)S(1)}) custom-call(f32[512,8,128]{2,1,0:T(8,128)S(1)} %get-tuple-element.52.weights, f32[512,8,128]{2,1,0:T(8,128)S(1)} %get-tuple-element.53.pulls, f32[8,528,128]{2,1,0:T(8,128)S(1)} %get-tuple-element.54.prior, ...), custom_call_target="tpu_custom_call", output_to_operand_aliasing={{0}: (5, {}), {1}: (6, {})} | custom-call | flops 33554432 | bytes 16777216 | tf_op jit(solution)/shard_map/fill/pallas_call | solution.py:422
  96.6 0.0 collective-permute-done.6.r_left
  96.6 0.0 collective-permute-done.7.r_right
  96.6 0.0 collective-permute-done.4.r_up
  96.6 0.0 collective-permute-done.5.r_down
  96.6 0.0 copy-done.5
  96.6 4.8 %moments.1 = (f32[8,528,128]{2,1,0:T(8,128)S(1)}, f32[8,528,128]{2,1,0:T(8,128)S(1)}, f32[8,512,128]{2,1,0:T(8,128)S(1)}, f32[128,128]{1,0:T(8,128)S(1)}) custom-call(f32[8,528,128]{2,1,0:T(8,128)S(1)} %get-tuple-element.58.r_in, f32[8,512,128]{2,1,0:T(8,128)S(1)} %get-tuple-element.59.diag, ...), custom_call_target="tpu_custom_call", output_to_operand_aliasing={{0}: (0, {})} | custom-call | flops 20971520 | bytes 12582912 | tf_op jit(solution)/shard_map/moments/pallas_call | solution.py:549
  101.5 13.8 %all_to_all.17 = f32[128,1,128]{2,1,0:T(1,128)S(1)} all-to-all(f32[128,1,128]{2,1,0:T(1,128)S(1)} %bitcast.9), channel_id=1, replica_groups=mesh['row'=8,'col'=16] {'row','col'}, dimensions={0} | all-to-all | bytes 131072 | tf_op jit(solution)/shard_map/all_to_all | solution.py:720
  115.2 3.0 %finish.1 = (f32[512,1024]{1,0:T(8,128)}, f32[512,1024]{1,0:T(8,128)}) custom-call(f32[128,128]{1,0:T(8,128)S(1)} %bitcast.8, f32[512,1024]{1,0:T(8,128)S(1)} %copy-done, f32[8,528,128]{2,1,0:T(8,128)S(1)} %get-tuple-element.65.r, f32[8,528,128]{2,1,0:T(8,128)S(1)} %get-tuple-element.66.q, f32[8,512,128]{2,1,0:T(8,128)S(1)} %get-tuple-element.67.s), custom_call_target="tpu_custom_call" | custom-call | flops 4194304 | bytes 12582912 | tf_op jit(solution)/shard_map/finish/pallas_call | solution.py:675
Async XLA Ops:
  0.6 11.6 %copy-start.7 = (s32[1,512]{1,0:T(1,128)S(1)}, s32[1,512]{1,0:T(1,128)}, u32[]{:S(2)}) copy-start(s32[1,512]{1,0:T(1,128)} %offset_ref.1) | copy-start | bytes 6148
  0.6 11.6 %copy-start.6 = (s32[1,512]{1,0:T(1,128)S(1)}, s32[1,512]{1,0:T(1,128)}, u32[]{:S(2)}) copy-start(s32[1,512]{1,0:T(1,128)} %owner_ref.1) | copy-start | bytes 6148
  0.7 11.6 %copy-start.4 = (bf16[1,512,1024]{2,1,0:T(8,128)(2,1)S(1)}, bf16[1,512,1024]{2,1,0:T(8,128)(2,1)}, u32[]{:S(2)}) copy-start(bf16[1,512,1024]{2,1,0:T(8,128)(2,1)} %param.9) | copy-start | bytes 3145732
  0.7 11.6 %copy-start.3 = (bf16[1,512,1024]{2,1,0:T(8,128)(2,1)S(1)}, bf16[1,512,1024]{2,1,0:T(8,128)(2,1)}, u32[]{:S(2)}) copy-start(bf16[1,512,1024]{2,1,0:T(8,128)(2,1)} %param.8) | copy-start | bytes 3145732
  2.8 14.7 %collective-permute-start = (f32[2,1024]{1,0:T(2,128)}, f32[2,1024]{1,0:T(2,128)S(1)}, u32[]{:S(2)}, u32[]{:S(2)}) collective-permute-start(f32[2,1024]{1,0:T(2,128)} %get-tuple-element.35), channel_id=1, source_target_pairs={{0,16},{16,32},{32,48},{48,64},{64,80},{80,96},{96,112},{112,0},{1... | collective-permute-start | bytes 24584 | tf_op jit(solution)/shard_map/ppermute | solution.py:694
  5.4 12.1 %collective-permute-start.1 = (f32[1,1024]{1,0:T(1,128)}, f32[1,1024]{1,0:T(1,128)S(1)}, u32[]{:S(2)}, u32[]{:S(2)}) collective-permute-start(f32[1,1024]{1,0:T(1,128)} %get-tuple-element.36), channel_id=1, source_target_pairs={{0,112},{16,0},{32,16},{48,32},{64,48},{80,64},{96,80},{112,96},{1... | collective-permute-start | bytes 12296 | tf_op jit(solution)/shard_map/ppermute | solution.py:694
  5.4 12.1 %collective-permute-start.2 = (f32[2,512]{1,0:T(2,128)}, f32[2,512]{1,0:T(2,128)S(1)}, u32[]{:S(2)}, u32[]{:S(2)}) collective-permute-start(f32[2,512]{1,0:T(2,128)} %get-tuple-element.37.own_ky), channel_id=1, source_target_pairs={{0,1},{1,2},{2,3},{3,4},{4,5},{5,6},{6,7},{7,8},{8,9},{9,10},{10,1... | collective-permute-start | bytes 12296 | tf_op jit(solution)/shard_map/ppermute | solution.py:694
  6.7 10.8 %collective-permute-start.3 = (f32[1,512]{1,0:T(1,128)}, f32[1,512]{1,0:T(1,128)S(1)}, u32[]{:S(2)}, u32[]{:S(2)}) collective-permute-start(f32[1,512]{1,0:T(1,128)} %get-tuple-element.38), channel_id=1, source_target_pairs={{0,15},{1,0},{2,1},{3,2},{4,3},{5,4},{6,5},{7,6},{8,7},{9,8},{10,9... | collective-permute-start | bytes 6152 | tf_op jit(solution)/shard_map/ppermute | solution.py:694
  12.3 1.6 %copy-start = (f32[512,1024]{1,0:T(8,128)S(1)}, f32[512,1024]{1,0:T(8,128)}, u32[]{:S(2)}) copy-start(f32[512,1024]{1,0:T(8,128)} %prior.1) | copy-start | bytes 6291460
  12.3 2.2 %copy-start.1 = (f32[512,1024]{1,0:T(8,128)S(1)}, f32[512,1024]{1,0:T(8,128)}, u32[]{:S(2)}) copy-start(f32[512,1024]{1,0:T(8,128)} %kx_in.1) | copy-start | bytes 6291460
  12.3 2.8 %copy-start.2 = (f32[512,1024]{1,0:T(8,128)S(1)}, f32[512,1024]{1,0:T(8,128)}, u32[]{:S(2)}) copy-start(f32[512,1024]{1,0:T(8,128)} %ky_in.1) | copy-start | bytes 6291460
  75.4 21.1 %collective-permute-start.4 = (f32[2,1024]{1,0:T(2,128)S(1)}, f32[2,1024]{1,0:T(2,128)S(1)}, u32[]{:S(2)}, u32[]{:S(2)}) collective-permute-start(f32[2,1024]{1,0:T(2,128)S(1)} %get-tuple-element.60), channel_id=1, source_target_pairs={{0,16},{16,32},{32,48},{48,64},{64,80},{80,96},{96,112},{112,0},{1... | collective-permute-start | bytes 24584 | tf_op jit(solution)/shard_map/ppermute | solution.py:694
  86.0 10.6 %collective-permute-start.5 = (f32[2,1024]{1,0:T(2,128)S(1)}, f32[2,1024]{1,0:T(2,128)S(1)}, u32[]{:S(2)}, u32[]{:S(2)}) collective-permute-start(f32[2,1024]{1,0:T(2,128)S(1)} %get-tuple-element.61), channel_id=1, source_target_pairs={{0,112},{16,0},{32,16},{48,32},{64,48},{80,64},{96,80},{112,96},{1... | collective-permute-start | bytes 24584 | tf_op jit(solution)/shard_map/ppermute | solution.py:694
  86.0 10.5 %collective-permute-start.6 = (f32[2,512]{1,0:T(2,128)S(1)}, f32[2,512]{1,0:T(2,128)S(1)}, u32[]{:S(2)}, u32[]{:S(2)}) collective-permute-start(f32[2,512]{1,0:T(2,128)S(1)} %get-tuple-element.62.own_right), channel_id=1, source_target_pairs={{0,1},{1,2},{2,3},{3,4},{4,5},{5,6},{6,7},{7,8},{8,9},{9,10},{10,1... | collective-permute-start | bytes 12296 | tf_op jit(solution)/shard_map/ppermute | solution.py:694
  86.0 10.5 %collective-permute-start.7 = (f32[2,512]{1,0:T(2,128)S(1)}, f32[2,512]{1,0:T(2,128)S(1)}, u32[]{:S(2)}, u32[]{:S(2)}) collective-permute-start(f32[2,512]{1,0:T(2,128)S(1)} %get-tuple-element.63.own_left), channel_id=1, source_target_pairs={{0,15},{1,0},{2,1},{3,2},{4,3},{5,4},{6,5},{7,6},{8,7},{9,8},{10,9... | collective-permute-start | bytes 12296 | tf_op jit(solution)/shard_map/ppermute | solution.py:694
  90.8 5.8 %copy-start.5 = (f32[2,512]{1,0:T(2,128)S(1)}, f32[2,512]{1,0:T(2,128)}, u32[]{:S(2)}) copy-start(f32[2,512]{1,0:T(2,128)} %get-tuple-element.37.own_ky) | copy-start | bytes 12292

commit v5 on v4

--- a/solution.py
+++ b/solution.py
@@ -44,6 +44,13 @@
     shape = (LANES, first.shape[1])
     rows = row_ids(shape)
     return jnp.where(rows == 0, first, jnp.where(rows == LANES - 1, last, 0.0)).T
+
+
+def right_edges(ky, part, b):
+    edges = ky[part, b * LANES : (b + 1) * LANES]
+    if (b + 1) * LANES < ky.shape[1]:
+        return edges
+    return jnp.where(is_last("col") & (lane_ids(edges.shape) == LANES - 1), 0.0, edges)
 
 
 def at_row(i, shift=0):
@@ -154,13 +161,14 @@
         in_specs=[
             whole((8, cols)), last_rows, last_rows, whole((rows, LANES)), last_cols, last_cols,
         ],
-        out_specs=[whole(s) for s in shapes],
+        out_specs=[pl.BlockSpec(memory_space=pltpu.VMEM)] * 4,
         name="strips",
     )(prior, prior, kx, prior, prior, ky)
 
 
-def arrange_kernel(prior_in, kx_in, ky_in, tiles, prior, kx, ky):
-    blocks, rows = ky.shape[0], ky.shape[1]
+def arrange_kernel(prior_in, kx_in, tiles, prior, kx):
+    rows, cols = prior_in.shape
+    blocks = cols // LANES
 
     def one_strip(strip, carry):
         base = pl.multiple_of(TS * strip, TS)
@@ -170,7 +178,6 @@
             lanes = slice(b * LANES, (b + 1) * LANES)
             prior[b, padded, :] = prior_in[here, lanes]
             kx[b, padded, :] = kx_in[here, lanes]
-            ky[b, here, :] = ky_in[here, lanes]
         for b in range(blocks):
             four = swap_blocks([prior[b, grid_rows(PAD, strip, a), :] for a in range(4)])
             for place, part in zip(tiles_of(strip, b, blocks), four):
@@ -184,34 +191,29 @@
         for b in range(blocks):
             kx[b, PAD + rows - 1 : PAD + rows, :] = jnp.zeros((1, LANES), F32)
 
-    @pl.when(is_last("col"))
-    def _():
-        edge = ky[blocks - 1]
-        ky[blocks - 1] = jnp.where(lane_ids(edge.shape) == LANES - 1, 0.0, edge)
-
-
-def arrange(prior, kx, ky):
+
+def arrange(prior, kx):
     rows, cols = prior.shape
     blocks = cols // LANES
     vmem = pl.BlockSpec(memory_space=pltpu.VMEM)
-    padded, plain = (blocks, rows + 2 * PAD, LANES), (blocks, rows, LANES)
-    shapes = ((rows * cols // (8 * LANES), 8, LANES), padded, padded, plain)
+    padded = (blocks, rows + 2 * PAD, LANES)
+    shapes = ((rows * cols // (8 * LANES), 8, LANES), padded, padded)
     return pl.pallas_call(
         arrange_kernel,
         out_shape=[jax.ShapeDtypeStruct(s, F32) for s in shapes],
-        in_specs=[vmem] * 3,
-        out_specs=[vmem] * 4,
+        in_specs=[vmem] * 2,
+        out_specs=[vmem] * 3,
         compiler_params=pltpu.CompilerParams(vmem_limit_bytes=SMALL_VMEM),
         cost_estimate=pl.CostEstimate(flops=1 << 22, bytes_accessed=14 << 20, transcendentals=0),
         name="arrange",
-    )(prior, kx, ky)
-
-
-BATCH = 16
-UF = 4
+    )(prior, kx)
+
+
+BATCH = 32
+UF = 16
 UO = 16
-US = 16
-UM = 8
+US = 32
+UM = 16
 
 
 def tiles_of(strip, b, blocks):
@@ -237,7 +239,7 @@
     part = pl.ds(pl.multiple_of(8 * i, 8), 8)
     near = sorted({n for b in chosen for n in (b - 1, b, b + 1) if 0 <= n <= last})
     p = {b: prior[b, here, :] for b in near}
-    h = {b: ky[b, part, :] for b in near}
+    h = {b: right_edges(ky, part, b) for b in near}
     lane = lane_ids((8, LANES))
     up = {b: pltpu.roll(p[b], LANES - 1, axis=1) for b in near}
     down = {b: pltpu.roll(p[b], 1, axis=1) for b in near}
@@ -265,8 +267,9 @@
     steps = rows // 8
     for s in range(slots):
         fields = got[s, 2 * cells :, :].astype(F32)
-        target = fields[0:1, :] * 16.0 + fields[1:2, :]
-        table_v[s, 0:1, :] = target.astype(jnp.int32)
+        target = jnp.broadcast_to(fields[0:1, :] * 16.0 + fields[1:2, :], (8, LANES))
+        target = target + 1024.0 * pltpu.roll(target, LANES - 1, axis=1)
+        table_v[s, 0:1, :] = target[0:1, :].astype(jnp.int32)
         table_v[s, 1:2, :] = fields[2:3, :].astype(jnp.int32)
     table_copy = pltpu.make_async_copy(table_v, table, table_sem)
     table_copy.start()
@@ -300,9 +303,9 @@
                 at = pl.multiple_of((first + 2 * pair) * 8, 16)
                 depths = got[slot, pl.ds(at, 16), :].astype(F32)
                 confs = got[slot, pl.ds(cells + at, 16), :].astype(F32)
+                word = table[slot, 0, first + 2 * pair]
                 for side in range(2):
-                    tile = first + 2 * pair + side
-                    place = table[slot, 0, tile]
+                    place = word >> 10 if side else word & 1023
                     error = depths[8 * side : 8 * side + 8] - tiles[place]
                     weight = confs[8 * side : 8 * side + 8] / jnp.maximum(jnp.abs(error), HUBER)
                     places.append(place)
@@ -317,16 +320,16 @@
     lax.fori_loop(0, slots, one_slot, 0)
     last = blocks - 1
 
-    def outer(pair, carry):
-        for strip in (2 * pair, 2 * pair + 1):
-            to_grid(weights, pulls, diag_out, r_out, strip, (0, last))
+    def outer(four, carry):
+        for n in range(4):
+            to_grid(weights, pulls, diag_out, r_out, 4 * four + n, (0, last))
         return carry
 
     def ends(n, carry):
         to_grid(weights, pulls, diag_out, r_out, n * (rows // TS - 1), range(1, last))
         return carry
 
-    lax.fori_loop(0, rows // TS // 2, outer, 0)
+    lax.fori_loop(0, rows // TS // 4, outer, 0)
     lax.fori_loop(0, 2, ends, 0)
 
     def outer_flows(i, carry):
@@ -357,9 +360,9 @@
         for b, edge, sign in ((0, 0, 1), (blocks - 1, LANES - 1, -1)):
             field = r_out[b, here, :]
             if edge:
-                across = pltpu.roll(ky[b, part, :] * field, 1, axis=1)
+                across = pltpu.roll(right_edges(ky, part, b) * field, 1, axis=1)
             else:
-                across = ky[b, part, :] * pltpu.roll(field, LANES - 1, axis=1)
+                across = right_edges(ky, part, b) * pltpu.roll(field, LANES - 1, axis=1)
             image = diag_out[b, part, :] * field - across - vertical(r_out, kx, b, i)
             edges.append(
                 jnp.where(lane == edge, image, pltpu.roll(field, sign % LANES, axis=1))
@@ -375,12 +378,12 @@
 
 
 def join(got, tiles, prior, kx, ky, from_up, from_down, from_left, from_right):
-    blocks, rows, _ = ky.shape
-    cols = blocks * LANES
+    rows, cols = ky.shape
+    blocks = cols // LANES
     slots = got.shape[0]
     vmem = pl.BlockSpec(memory_space=pltpu.VMEM)
     strip_shapes = ((2, cols), (2, cols), (2, rows), (2, rows))
-    shapes = (prior.shape, ky.shape, prior.shape, kx.shape, tiles.shape, tiles.shape) + strip_shapes
+    shapes = (prior.shape, (blocks, rows, LANES), prior.shape, kx.shape, tiles.shape, tiles.shape) + strip_shapes
     cells = rows * cols
     return pl.pallas_call(
         join_kernel,
@@ -440,7 +443,7 @@
     blocks = diag.shape[0]
     part = pl.ds(8 * i, 8) if isinstance(i, int) else pl.ds(pl.multiple_of(8 * i, 8), 8)
     x = [field[b, at_row(i), :] for b in range(blocks)]
-    h = [ky[b, part, :] for b in range(blocks)]
+    h = [right_edges(ky, part, b) for b in range(blocks)]
     right = cols_up(x, after)
     left = cols_down([h[b] * x[b] for b in range(blocks)], entering)
     return [
@@ -534,7 +537,9 @@
     values += [cell(r, corner) for corner in corners]
     values += [cell(q, corner) for corner in corners]
     values += [cell(kx, corner) for corner in corners[2:]]
-    values += [cell(ky, corner, 0) for corner in corners[1::2]]
+    for _, i in corners[1::2]:
+        part = slice(i // 8 * 8, i // 8 * 8 + 8)
+        values.append(right_edges(ky, part, last)[i % 8 : i % 8 + 1, LANES - 1 :])
     lane = lane_ids((1, LANES))
     row = jnp.zeros((1, LANES), F32)
     for place, value in enumerate(values):
@@ -707,15 +712,14 @@
     own = strips(prior, edge_rows, edge_cols)
     early = exchange(*own)
     payload = pack(tile_owner, tile_offset, tile_count, depth_tiles[0], conf_tiles[0], col_count)
-    arranged = arrange(prior, edge_rows, edge_cols)
+    arranged = arrange(prior, edge_rows)
     payload, early, arranged = lax.optimization_barrier((payload, early, arranged))
     got = lax.all_to_all(payload, "col", split_axis=0, concat_axis=0, tiled=True)
-    ky = arranged[3]
-    r, diag, blocked, kx, weights, pulls, *edges = join(got, *arranged, *early)
+    r, diag, blocked, kx, weights, pulls, *edges = join(got, *arranged, edge_cols, *early)
     late = exchange(*edges)
-    r, diag = fill(weights, pulls, blocked, kx, ky, r, diag)
+    r, diag = fill(weights, pulls, blocked, kx, edge_cols, r, diag)
     r, q, s, table = moments(
-        row_count * col_count, r, diag, kx, ky, *late, early[2], edges[2], edges[3], own[3]
+        row_count * col_count, r, diag, kx, edge_cols, *late, early[2], edges[2], edges[3], own[3]
     )
     table = lax.all_to_all(table, ("row", "col"), split_axis=0, concat_axis=0, tiled=True)
     return tuple(finish(table, prior, r, q, s))

time: 119 us -> 117 us (0.983)
  starting transfers between devices: 24.2 us -> 15.4 us
  blocking collectives: 66 us -> 70.7 us
  Pallas kernels: 25.4 us -> 29.1 us
    ppermute x8, starting transfers between devices: 24.2 us -> 15.4 us  [send(): lax.ppermute(strip, axis, [(i, (i + by) % count) for i in range(count)])]
    pallas_call x1, Pallas kernels: 5.7 us -> 10.7 us  [join(): pl.pallas_call(join_kernel, out_shape=[jax.ShapeDtypeStruct(s, F32) for s...]
    all_to_all x1, blocking collectives: 13.8 us -> 18.4 us  [shards(): lax.all_to_all(table, ('row', 'col'), split_axis=0, concat_axis=0, tiled=...]
  transfers between devices with their start and end apart: 8 -> 8, of which waited for: 0 -> 0; matrix products, arithmetic and copies ran while one was open for 0% -> 0% of each run, Pallas kernels for 8% -> 7%
where the time goes in v5:
time: 117 us
  blocking collectives  70.7 us (60%)
  Pallas kernels  29.1 us (25%)
  starting transfers between devices  15.4 us (13%)
  between operations  1.49 us (1%)
    all_to_all x1, blocking collectives, shards(): lax.all_to_all(payload, 'col', split_axis=0, concat_axis=0, tiled=True)  52.3 us
    all_to_all x1, blocking collectives, shards(): lax.all_to_all(table, ('row', 'col'), split_axis=0, concat_axis=0, tiled=...  18.4 us
    ppermute x8, starting transfers between devices, send(): lax.ppermute(strip, axis, [(i, (i + by) % count) for i in range(count)])  15.4 us
    pallas_call x1, Pallas kernels, join(): pl.pallas_call(join_kernel, out_shape=[jax.ShapeDtypeStruct(s, F32) for s...  10.7 us
    pallas_call x1, Pallas kernels, fill(): pl.pallas_call(fill_kernel, out_shape=[jax.ShapeDtypeStruct(x.shape, F32)...  4.9 us
    pallas_call x1, Pallas kernels, moments(): pl.pallas_call(moments_kernel, out_shape=[jax.ShapeDtypeStruct(r.shape, F...  4.53 us
    pallas_call x1, Pallas kernels, finish(): pl.pallas_call(finish_kernel, out_shape=[jax.ShapeDtypeStruct((rows, bloc...  3.03 us
  transfers between devices with their start and end apart: 8, of which 0 were waited for; matrix products, arithmetic and copies ran while one was open for 0% of the time, Pallas kernels for 7%

profile of v5, /device:TPU:1, one launch (start us, length us, event | category | flops | bytes accessed | tf_op | source)
XLA Modules:
  0.0 117.4 jit_solution(3760526890862777636)
XLA Ops:
  0.6 0.0 copy-start.7
  0.6 0.0 copy-start.6
  0.7 0.0 copy-start.4
  0.7 0.0 copy-start.3
  0.7 2.1 %strips.1 = (f32[1,1024]{1,0:T(1,128)}, f32[2,1024]{1,0:T(2,128)}, f32[1,512]{1,0:T(1,128)}, f32[2,512]{1,0:T(2,128)}) custom-call(f32[512,1024]{1,0:T(8,128)} %prior.1, f32[512,1024]{1,0:T(8,128)} %prior.1, f32[512,1024]{1,0:T(8,128)} %kx_in.1, f32[512,1024]{1,0:T(8,128)} %prior.1, f32[512,1024]{1,0:T(8,128)} %prior.1, f32[512,1024]{1,0:T(8,128)} %ky.5), custom_call_target="tpu_custom_call" | custom-call | tf_op jit(solution)/shard_map/strips/pallas_call | solution.py:157
  2.8 2.6 %collective-permute-start = (f32[2,1024]{1,0:T(2,128)}, f32[2,1024]{1,0:T(2,128)S(1)}, u32[]{:S(2)}, u32[]{:S(2)}) collective-permute-start(f32[2,1024]{1,0:T(2,128)} %get-tuple-element.33), channel_id=1, source_target_pairs={{0,16},{16,32},{32,48},{48,64},{64,80},{80,96},{96,112},{112,0},{1... | collective-permute-start | bytes 24584 | tf_op jit(solution)/shard_map/ppermute | solution.py:699
  5.4 0.0 collective-permute-start.1
  5.4 1.3 %collective-permute-start.2 = (f32[2,512]{1,0:T(2,128)}, f32[2,512]{1,0:T(2,128)S(1)}, u32[]{:S(2)}, u32[]{:S(2)}) collective-permute-start(f32[2,512]{1,0:T(2,128)} %get-tuple-element.35.own_ky), channel_id=1, source_target_pairs={{0,1},{1,2},{2,3},{3,4},{4,5},{5,6},{6,7},{7,8},{8,9},{9,10},{10,1... | collective-permute-start | bytes 12296 | tf_op jit(solution)/shard_map/ppermute | solution.py:699
  6.7 4.9 %collective-permute-start.3 = (f32[1,512]{1,0:T(1,128)}, f32[1,512]{1,0:T(1,128)S(1)}, u32[]{:S(2)}, u32[]{:S(2)}) collective-permute-start(f32[1,512]{1,0:T(1,128)} %get-tuple-element.36), channel_id=1, source_target_pairs={{0,15},{1,0},{2,1},{3,2},{4,3},{5,4},{6,5},{7,6},{8,7},{9,8},{10,9... | collective-permute-start | bytes 6152 | tf_op jit(solution)/shard_map/ppermute | solution.py:699
  12.3 0.0 copy-done.7
  12.3 0.0 copy-done.6
  12.3 0.0 copy-done.4
  12.3 0.0 copy-done.3
  12.3 0.0 copy-start
  12.3 0.0 copy-start.2
  12.3 1.6 %pack.1 = bf16[16,1040,128]{2,1,0:T(8,128)(2,1)S(1)} custom-call(s32[1,512]{1,0:T(1,128)S(1)} %copy-done.6, s32[1,1]{1,0:T(1,128)S(6)} %copy.21.count_ref, s32[1,512]{1,0:T(1,128)S(1)} %copy-done.7, bf16[512,1024]{1,0:T(8,128)(2,1)S(1)} %bitcast.6, bf16[512,1024]{1,0:T(8,128)(2,1)S(1)} %bitcast.7), custom_call_target="tpu_custom_call" | custom-call | flops 1048576 | bytes 4194304 | tf_op jit(solution)/shard_map/pack/pallas_call | solution.py:125
  13.9 0.0 copy-done
  13.9 0.6 copy-done.2
  14.5 2.2 %arrange.1 = (f32[512,8,128]{2,1,0:T(8,128)S(1)}, f32[8,528,128]{2,1,0:T(8,128)S(1)}, f32[8,528,128]{2,1,0:T(8,128)S(1)}) custom-call(f32[512,1024]{1,0:T(8,128)S(1)} %copy-done, f32[512,1024]{1,0:T(8,128)S(1)} %copy-done.2), custom_call_target="tpu_custom_call" | custom-call | flops 4194304 | bytes 14680064 | tf_op jit(solution)/shard_map/arrange/pallas_call | solution.py:201
  16.7 0.0 collective-permute-done.3.from_right
  16.8 0.0 collective-permute-done.1.from_down
  16.8 0.0 collective-permute-done.2.from_left.k_left
  16.8 0.0 collective-permute-done.from_up
  16.8 0.0 copy-start.1
  16.8 52.3 %all_to_all.16.got = bf16[16,1040,128]{2,1,0:T(8,128)(2,1)S(1)} all-to-all(bf16[16,1040,128]{2,1,0:T(8,128)(2,1)S(1)} %pack.1), channel_id=1, replica_groups=mesh['row'=8,'col'=16] {'col'}, dimensions={0} | all-to-all | bytes 8519680 | tf_op jit(solution)/shard_map/all_to_all | solution.py:717
  69.1 0.0 copy-done.1
  69.1 10.7 %join.1 = (f32[8,528,128]{2,1,0:T(8,128)S(1)}, f32[8,512,128]{2,1,0:T(8,128)S(1)}, f32[8,528,128]{2,1,0:T(8,128)S(1)}, f32[8,528,128]{2,1,0:T(8,128)S(1)}, f32[5...) custom-call(bf16[16,1040,128]{2,1,0:T(8,128)(2,1)S(1)} %all_to_all.1, ...), custom_call_target="tpu_custom_call", output_to_operand_aliasing={{2}: (2, {}), {3}: (3, {})} | custom-call | flops 15728640 | bytes 12582912 | tf_op jit(solution)/shard_map/join/pallas_call | solution.py:388
  79.9 0.0 collective-permute-start.4
  79.9 1.8 %collective-permute-start.5 = (f32[2,1024]{1,0:T(2,128)S(1)}, f32[2,1024]{1,0:T(2,128)S(1)}, u32[]{:S(2)}, u32[]{:S(2)}) collective-permute-start(f32[2,1024]{1,0:T(2,128)S(1)} %get-tuple-element.57), channel_id=1, source_target_pairs={{0,112},{16,0},{32,16},{48,32},{64,48},{80,64},{96,80},{112,96},{1... | collective-permute-start | bytes 24584 | tf_op jit(solution)/shard_map/ppermute | solution.py:699
  81.7 2.2 %collective-permute-start.6 = (f32[2,512]{1,0:T(2,128)S(1)}, f32[2,512]{1,0:T(2,128)S(1)}, u32[]{:S(2)}, u32[]{:S(2)}) collective-permute-start(f32[2,512]{1,0:T(2,128)S(1)} %get-tuple-element.58.own_right), channel_id=1, source_target_pairs={{0,1},{1,2},{2,3},{3,4},{4,5},{5,6},{6,7},{7,8},{8,9},{9,10},{10,1... | collective-permute-start | bytes 12296 | tf_op jit(solution)/shard_map/ppermute | solution.py:699
  83.9 2.6 %collective-permute-start.7 = (f32[2,512]{1,0:T(2,128)S(1)}, f32[2,512]{1,0:T(2,128)S(1)}, u32[]{:S(2)}, u32[]{:S(2)}) collective-permute-start(f32[2,512]{1,0:T(2,128)S(1)} %get-tuple-element.59.own_left), channel_id=1, source_target_pairs={{0,15},{1,0},{2,1},{3,2},{4,3},{5,4},{6,5},{7,6},{8,7},{9,8},{10,9... | collective-permute-start | bytes 12296 | tf_op jit(solution)/shard_map/ppermute | solution.py:699
  86.5 0.0 copy-start.5
  86.5 4.9 %fill.1 = (f32[8,528,128]{2,1,0:T(8,128)S(1)}, f32[8,512,128]{2,1,0:T(8,128)S(1)}) custom-call(f32[512,8,128]{2,1,0:T(8,128)S(1)} %get-tuple-element.48.weights, f32[512,8,128]{2,1,0:T(8,128)S(1)} %get-tuple-element.49.pulls, f32[8,528,128]{2,1,0:T(8,128)S(1)} %get-tuple-element.50.prior, ...), custom_call_target="tpu_custom_call", output_to_operand_aliasing={{0}: (5, {}), {1}: (6, {})} | custom-call | flops 33554432 | bytes 16777216 | tf_op jit(solution)/shard_map/fill/pallas_call | solution.py:425
  91.4 0.0 collective-permute-done.6.r_left
  91.4 0.0 collective-permute-done.7.r_right
  91.4 0.0 collective-permute-done.4.r_up
  91.4 0.0 collective-permute-done.5.r_down
  91.4 0.0 copy-done.5
  91.4 4.5 %moments.1 = (f32[8,528,128]{2,1,0:T(8,128)S(1)}, f32[8,528,128]{2,1,0:T(8,128)S(1)}, f32[8,512,128]{2,1,0:T(8,128)S(1)}, f32[128,128]{1,0:T(8,128)S(1)}) custom-call(f32[8,528,128]{2,1,0:T(8,128)S(1)} %get-tuple-element.54.r_in, f32[8,512,128]{2,1,0:T(8,128)S(1)} %get-tuple-element.55.diag, ...), custom_call_target="tpu_custom_call", output_to_operand_aliasing={{0}: (0, {})} | custom-call | flops 20971520 | bytes 12582912 | tf_op jit(solution)/shard_map/moments/pallas_call | solution.py:554
  96.0 18.4 %all_to_all.17 = f32[128,1,128]{2,1,0:T(1,128)S(1)} all-to-all(f32[128,1,128]{2,1,0:T(1,128)S(1)} %bitcast.9), channel_id=1, replica_groups=mesh['row'=8,'col'=16] {'row','col'}, dimensions={0} | all-to-all | bytes 131072 | tf_op jit(solution)/shard_map/all_to_all | solution.py:724
  114.4 3.0 %finish.1 = (f32[512,1024]{1,0:T(8,128)}, f32[512,1024]{1,0:T(8,128)}) custom-call(f32[128,128]{1,0:T(8,128)S(1)} %bitcast.8, f32[512,1024]{1,0:T(8,128)S(1)} %copy-done, f32[8,528,128]{2,1,0:T(8,128)S(1)} %get-tuple-element.61.r, f32[8,528,128]{2,1,0:T(8,128)S(1)} %get-tuple-element.62.q, f32[8,512,128]{2,1,0:T(8,128)S(1)} %get-tuple-element.63.s), custom_call_target="tpu_custom_call" | custom-call | flops 4194304 | bytes 12582912 | tf_op jit(solution)/shard_map/finish/pallas_call | solution.py:680
Async XLA Ops:
  0.6 11.6 %copy-start.7 = (s32[1,512]{1,0:T(1,128)S(1)}, s32[1,512]{1,0:T(1,128)}, u32[]{:S(2)}) copy-start(s32[1,512]{1,0:T(1,128)} %offset_ref.1) | copy-start | bytes 6148
  0.6 11.6 %copy-start.6 = (s32[1,512]{1,0:T(1,128)S(1)}, s32[1,512]{1,0:T(1,128)}, u32[]{:S(2)}) copy-start(s32[1,512]{1,0:T(1,128)} %owner_ref.1) | copy-start | bytes 6148
  0.7 11.6 %copy-start.4 = (bf16[1,512,1024]{2,1,0:T(8,128)(2,1)S(1)}, bf16[1,512,1024]{2,1,0:T(8,128)(2,1)}, u32[]{:S(2)}) copy-start(bf16[1,512,1024]{2,1,0:T(8,128)(2,1)} %param.9) | copy-start | bytes 3145732
  0.7 11.6 %copy-start.3 = (bf16[1,512,1024]{2,1,0:T(8,128)(2,1)S(1)}, bf16[1,512,1024]{2,1,0:T(8,128)(2,1)}, u32[]{:S(2)}) copy-start(bf16[1,512,1024]{2,1,0:T(8,128)(2,1)} %param.8) | copy-start | bytes 3145732
  2.8 14.0 %collective-permute-start = (f32[2,1024]{1,0:T(2,128)}, f32[2,1024]{1,0:T(2,128)S(1)}, u32[]{:S(2)}, u32[]{:S(2)}) collective-permute-start(f32[2,1024]{1,0:T(2,128)} %get-tuple-element.33), channel_id=1, source_target_pairs={{0,16},{16,32},{32,48},{48,64},{64,80},{80,96},{96,112},{112,0},{1... | collective-permute-start | bytes 24584 | tf_op jit(solution)/shard_map/ppermute | solution.py:699
  5.4 11.3 %collective-permute-start.1 = (f32[1,1024]{1,0:T(1,128)}, f32[1,1024]{1,0:T(1,128)S(1)}, u32[]{:S(2)}, u32[]{:S(2)}) collective-permute-start(f32[1,1024]{1,0:T(1,128)} %get-tuple-element.34), channel_id=1, source_target_pairs={{0,112},{16,0},{32,16},{48,32},{64,48},{80,64},{96,80},{112,96},{1... | collective-permute-start | bytes 12296 | tf_op jit(solution)/shard_map/ppermute | solution.py:699
  5.4 11.4 %collective-permute-start.2 = (f32[2,512]{1,0:T(2,128)}, f32[2,512]{1,0:T(2,128)S(1)}, u32[]{:S(2)}, u32[]{:S(2)}) collective-permute-start(f32[2,512]{1,0:T(2,128)} %get-tuple-element.35.own_ky), channel_id=1, source_target_pairs={{0,1},{1,2},{2,3},{3,4},{4,5},{5,6},{6,7},{7,8},{8,9},{9,10},{10,1... | collective-permute-start | bytes 12296 | tf_op jit(solution)/shard_map/ppermute | solution.py:699
  6.7 10.0 %collective-permute-start.3 = (f32[1,512]{1,0:T(1,128)}, f32[1,512]{1,0:T(1,128)S(1)}, u32[]{:S(2)}, u32[]{:S(2)}) collective-permute-start(f32[1,512]{1,0:T(1,128)} %get-tuple-element.36), channel_id=1, source_target_pairs={{0,15},{1,0},{2,1},{3,2},{4,3},{5,4},{6,5},{7,6},{8,7},{9,8},{10,9... | collective-permute-start | bytes 6152 | tf_op jit(solution)/shard_map/ppermute | solution.py:699
  12.3 1.6 %copy-start = (f32[512,1024]{1,0:T(8,128)S(1)}, f32[512,1024]{1,0:T(8,128)}, u32[]{:S(2)}) copy-start(f32[512,1024]{1,0:T(8,128)} %prior.1) | copy-start | bytes 6291460
  12.3 2.2 %copy-start.2 = (f32[512,1024]{1,0:T(8,128)S(1)}, f32[512,1024]{1,0:T(8,128)}, u32[]{:S(2)}) copy-start(f32[512,1024]{1,0:T(8,128)} %kx_in.1) | copy-start | bytes 6291460
  16.8 52.3 %copy-start.1 = (f32[512,1024]{1,0:T(8,128)S(1)}, f32[512,1024]{1,0:T(8,128)}, u32[]{:S(2)}) copy-start(f32[512,1024]{1,0:T(8,128)} %ky.5) | copy-start | bytes 6291460
  79.9 11.5 %collective-permute-start.4 = (f32[2,1024]{1,0:T(2,128)S(1)}, f32[2,1024]{1,0:T(2,128)S(1)}, u32[]{:S(2)}, u32[]{:S(2)}) collective-permute-start(f32[2,1024]{1,0:T(2,128)S(1)} %get-tuple-element.56), channel_id=1, source_target_pairs={{0,16},{16,32},{32,48},{48,64},{64,80},{80,96},{96,112},{112,0},{1... | collective-permute-start | bytes 24584 | tf_op jit(solution)/shard_map/ppermute | solution.py:699
  79.9 11.5 %collective-permute-start.5 = (f32[2,1024]{1,0:T(2,128)S(1)}, f32[2,1024]{1,0:T(2,128)S(1)}, u32[]{:S(2)}, u32[]{:S(2)}) collective-permute-start(f32[2,1024]{1,0:T(2,128)S(1)} %get-tuple-element.57), channel_id=1, source_target_pairs={{0,112},{16,0},{32,16},{48,32},{64,48},{80,64},{96,80},{112,96},{1... | collective-permute-start | bytes 24584 | tf_op jit(solution)/shard_map/ppermute | solution.py:699
  81.7 9.7 %collective-permute-start.6 = (f32[2,512]{1,0:T(2,128)S(1)}, f32[2,512]{1,0:T(2,128)S(1)}, u32[]{:S(2)}, u32[]{:S(2)}) collective-permute-start(f32[2,512]{1,0:T(2,128)S(1)} %get-tuple-element.58.own_right), channel_id=1, source_target_pairs={{0,1},{1,2},{2,3},{3,4},{4,5},{5,6},{6,7},{7,8},{8,9},{9,10},{10,1... | collective-permute-start | bytes 12296 | tf_op jit(solution)/shard_map/ppermute | solution.py:699
  83.9 7.5 %collective-permute-start.7 = (f32[2,512]{1,0:T(2,128)S(1)}, f32[2,512]{1,0:T(2,128)S(1)}, u32[]{:S(2)}, u32[]{:S(2)}) collective-permute-start(f32[2,512]{1,0:T(2,128)S(1)} %get-tuple-element.59.own_left), channel_id=1, source_target_pairs={{0,15},{1,0},{2,1},{3,2},{4,3},{5,4},{6,5},{7,6},{8,7},{9,8},{10,9... | collective-permute-start | bytes 12296 | tf_op jit(solution)/shard_map/ppermute | solution.py:699
  86.5 5.0 %copy-start.5 = (f32[2,512]{1,0:T(2,128)S(1)}, f32[2,512]{1,0:T(2,128)}, u32[]{:S(2)}) copy-start(f32[2,512]{1,0:T(2,128)} %get-tuple-element.35.own_ky) | copy-start | bytes 12292

commit v6 on v5

--- a/solution.py
+++ b/solution.py
@@ -110,7 +110,7 @@
                 for c in range(chunks):
                     buffer[pl.ds(c, 16, stride=chunks), :] = block[:, c * LANES : (c + 1) * LANES]
                 first = which * cells + m * 16 * chunks
-                out[slot, first : first + 16 * chunks, :] = buffer[...].astype(jnp.bfloat16)
+                out[slot, first : first + 16 * chunks, :] = buffer[: 16 * chunks, :].astype(jnp.bfloat16)
         return carry
 
     lax.fori_loop(0, GROUPS, one_run, 0)
@@ -127,7 +127,7 @@
         out_shape=jax.ShapeDtypeStruct((slots, rows, LANES), jnp.bfloat16),
         in_specs=[smem, smem, vmem, vmem, vmem],
         out_specs=vmem,
-        scratch_shapes=[pltpu.VMEM((2 * run // 16, 16 * (cells // LANES), LANES), F32)],
+        scratch_shapes=[pltpu.VMEM((2 * run // 16, 16 * (cells // LANES) + PAD, LANES), F32)],
         compiler_params=pltpu.CompilerParams(vmem_limit_bytes=SMALL_VMEM),
         cost_estimate=pl.CostEstimate(flops=1 << 20, bytes_accessed=4 << 20, transcendentals=0),
         name="pack",
@@ -210,10 +210,10 @@
 
 
 BATCH = 32
-UF = 16
+UF = 64
 UO = 16
-US = 32
-UM = 16
+US = 64
+UM = 64
 
 
 def tiles_of(strip, b, blocks):
@@ -263,7 +263,7 @@
 ):
     slots, rows_in = got.shape[0], got.shape[1]
     cells = (rows_in - META) // 2
-    blocks, rows = diag_out.shape[0], diag_out.shape[1]
+    blocks, rows = diag_out.shape[0], diag_out.shape[1] - PAD
     steps = rows // 8
     for s in range(slots):
         fields = got[s, 2 * cells :, :].astype(F32)
@@ -383,7 +383,7 @@
     slots = got.shape[0]
     vmem = pl.BlockSpec(memory_space=pltpu.VMEM)
     strip_shapes = ((2, cols), (2, cols), (2, rows), (2, rows))
-    shapes = (prior.shape, (blocks, rows, LANES), prior.shape, kx.shape, tiles.shape, tiles.shape) + strip_shapes
+    shapes = (prior.shape, (blocks, rows + PAD, LANES), prior.shape, kx.shape, tiles.shape, tiles.shape) + strip_shapes
     cells = rows * cols
     return pl.pallas_call(
         join_kernel,
@@ -405,7 +405,7 @@
 
 
 def fill_kernel(weights, pulls, prior, kx, ky, r_in, diag_in, r, diag):
-    blocks, rows = diag.shape[0], diag.shape[1]
+    blocks, rows = diag.shape[0], diag.shape[1] - PAD
     inner = range(1, blocks - 1)
 
     def grid_step(strip, carry):
@@ -473,7 +473,7 @@
     r_in, diag, kx, ky, r_up, r_down, r_left, r_right, k_left, own_left, own_right, own_ky,
     r, q, s, table_out, side_r, side_q,
 ):
-    blocks, rows = diag.shape[0], diag.shape[1]
+    blocks, rows, _ = s.shape
     steps = rows // 8
     last = blocks - 1
     k = k_left[1:2, :]
@@ -548,7 +548,7 @@
 
 
 def moments(devices, r, diag, *others):
-    blocks, rows, _ = diag.shape
+    blocks, rows = diag.shape[0], diag.shape[1] - PAD
     vmem = pl.BlockSpec(memory_space=pltpu.VMEM)
     cells = blocks * rows * LANES
     return pl.pallas_call(
@@ -556,7 +556,7 @@
         out_shape=[
             jax.ShapeDtypeStruct(r.shape, F32),
             jax.ShapeDtypeStruct(r.shape, F32),
-            jax.ShapeDtypeStruct(diag.shape, F32),
+            jax.ShapeDtypeStruct((blocks, rows, LANES), F32),
             jax.ShapeDtypeStruct((devices, LANES), F32),
         ],
         in_specs=[vmem] * (2 + len(others)),

time: 117 us -> 116 us (level)
  starting transfers between devices: 15.4 us -> 20.4 us
  Pallas kernels: 29.1 us -> 25 us
  blocking collectives: 70.7 us -> 68.5 us
    ppermute x8, starting transfers between devices: 15.4 us -> 20.4 us  [send(): lax.ppermute(strip, axis, [(i, (i + by) % count) for i in range(count)])]
    pallas_call x1, Pallas kernels: 10.7 us -> 7.47 us  [join(): pl.pallas_call(join_kernel, out_shape=[jax.ShapeDtypeStruct(s, F32) for s...]
    all_to_all x1, blocking collectives: 18.4 us -> 16.2 us  [shards(): lax.all_to_all(table, ('row', 'col'), split_axis=0, concat_axis=0, tiled=...]
where the time goes in v6:
time: 116 us
  blocking collectives  68.5 us (59%)
  Pallas kernels  25 us (22%)
  starting transfers between devices  20.4 us (18%)
  between operations  1.49 us (1%)
    all_to_all x1, blocking collectives, shards(): lax.all_to_all(payload, 'col', split_axis=0, concat_axis=0, tiled=True)  52.3 us
    ppermute x8, starting transfers between devices, send(): lax.ppermute(strip, axis, [(i, (i + by) % count) for i in range(count)])  20.4 us
    all_to_all x1, blocking collectives, shards(): lax.all_to_all(table, ('row', 'col'), split_axis=0, concat_axis=0, tiled=...  16.2 us
    pallas_call x1, Pallas kernels, join(): pl.pallas_call(join_kernel, out_shape=[jax.ShapeDtypeStruct(s, F32) for s...  7.47 us
    pallas_call x1, Pallas kernels, fill(): pl.pallas_call(fill_kernel, out_shape=[jax.ShapeDtypeStruct(x.shape, F32)...  4.72 us
    pallas_call x1, Pallas kernels, moments(): pl.pallas_call(moments_kernel, out_shape=[jax.ShapeDtypeStruct(r.shape, F...  3.89 us
    pallas_call x1, Pallas kernels, finish(): pl.pallas_call(finish_kernel, out_shape=[jax.ShapeDtypeStruct((rows, bloc...  3.03 us
  transfers between devices with their start and end apart: 8, of which 0 were waited for; matrix products, arithmetic and copies ran while one was open for 0% of the time, Pallas kernels for 7%

profile of v6, /device:TPU:1, one launch (start us, length us, event | category | flops | bytes accessed | tf_op | source)
XLA Modules:
  0.0 116.1 jit_solution(7694629296915714391)
XLA Ops:
  0.6 0.0 copy-start.7
  0.6 0.0 copy-start.6
  0.7 0.0 copy-start.4
  0.7 0.0 copy-start.3
  0.7 2.1 %strips.1 = (f32[1,1024]{1,0:T(1,128)}, f32[2,1024]{1,0:T(2,128)}, f32[1,512]{1,0:T(1,128)}, f32[2,512]{1,0:T(2,128)}) custom-call(f32[512,1024]{1,0:T(8,128)} %prior.1, f32[512,1024]{1,0:T(8,128)} %prior.1, f32[512,1024]{1,0:T(8,128)} %kx_in.1, f32[512,1024]{1,0:T(8,128)} %prior.1, f32[512,1024]{1,0:T(8,128)} %prior.1, f32[512,1024]{1,0:T(8,128)} %ky.5), custom_call_target="tpu_custom_call" | custom-call | tf_op jit(solution)/shard_map/strips/pallas_call | solution.py:157
  2.8 2.6 %collective-permute-start = (f32[2,1024]{1,0:T(2,128)}, f32[2,1024]{1,0:T(2,128)S(1)}, u32[]{:S(2)}, u32[]{:S(2)}) collective-permute-start(f32[2,1024]{1,0:T(2,128)} %get-tuple-element.33), channel_id=1, source_target_pairs={{0,16},{16,32},{32,48},{48,64},{64,80},{80,96},{96,112},{112,0},{1... | collective-permute-start | bytes 24584 | tf_op jit(solution)/shard_map/ppermute | solution.py:699
  5.4 0.0 collective-permute-start.1
  5.4 1.3 %collective-permute-start.2 = (f32[2,512]{1,0:T(2,128)}, f32[2,512]{1,0:T(2,128)S(1)}, u32[]{:S(2)}, u32[]{:S(2)}) collective-permute-start(f32[2,512]{1,0:T(2,128)} %get-tuple-element.35.own_ky), channel_id=1, source_target_pairs={{0,1},{1,2},{2,3},{3,4},{4,5},{5,6},{6,7},{7,8},{8,9},{9,10},{10,1... | collective-permute-start | bytes 12296 | tf_op jit(solution)/shard_map/ppermute | solution.py:699
  6.7 4.9 %collective-permute-start.3 = (f32[1,512]{1,0:T(1,128)}, f32[1,512]{1,0:T(1,128)S(1)}, u32[]{:S(2)}, u32[]{:S(2)}) collective-permute-start(f32[1,512]{1,0:T(1,128)} %get-tuple-element.36), channel_id=1, source_target_pairs={{0,15},{1,0},{2,1},{3,2},{4,3},{5,4},{6,5},{7,6},{8,7},{9,8},{10,9... | collective-permute-start | bytes 6152 | tf_op jit(solution)/shard_map/ppermute | solution.py:699
  12.3 0.0 copy-done.7
  12.3 0.0 copy-done.6
  12.3 0.0 copy-done.4
  12.3 0.0 copy-done.3
  12.3 0.0 copy-start
  12.3 0.0 copy-start.2
  12.3 1.6 %pack.1 = bf16[16,1040,128]{2,1,0:T(8,128)(2,1)S(1)} custom-call(s32[1,512]{1,0:T(1,128)S(1)} %copy-done.6, s32[1,1]{1,0:T(1,128)S(6)} %copy.21.count_ref, s32[1,512]{1,0:T(1,128)S(1)} %copy-done.7, bf16[512,1024]{1,0:T(8,128)(2,1)S(1)} %bitcast.6, bf16[512,1024]{1,0:T(8,128)(2,1)S(1)} %bitcast.7), custom_call_target="tpu_custom_call" | custom-call | flops 1048576 | bytes 4194304 | tf_op jit(solution)/shard_map/pack/pallas_call | solution.py:125
  13.9 0.0 copy-done
  13.9 0.6 copy-done.2
  14.5 2.2 %arrange.1 = (f32[512,8,128]{2,1,0:T(8,128)S(1)}, f32[8,528,128]{2,1,0:T(8,128)S(1)}, f32[8,528,128]{2,1,0:T(8,128)S(1)}) custom-call(f32[512,1024]{1,0:T(8,128)S(1)} %copy-done, f32[512,1024]{1,0:T(8,128)S(1)} %copy-done.2), custom_call_target="tpu_custom_call" | custom-call | flops 4194304 | bytes 14680064 | tf_op jit(solution)/shard_map/arrange/pallas_call | solution.py:201
  16.7 0.0 collective-permute-done.3.from_right
  16.8 0.0 collective-permute-done.1.from_down
  16.8 0.0 collective-permute-done.2.from_left.k_left
  16.8 0.0 collective-permute-done.from_up
  16.8 0.0 copy-start.1
  16.8 52.3 %all_to_all.16.got = bf16[16,1040,128]{2,1,0:T(8,128)(2,1)S(1)} all-to-all(bf16[16,1040,128]{2,1,0:T(8,128)(2,1)S(1)} %pack.1), channel_id=1, replica_groups=mesh['row'=8,'col'=16] {'col'}, dimensions={0} | all-to-all | bytes 8519680 | tf_op jit(solution)/shard_map/all_to_all | solution.py:717
  69.1 0.0 copy-done.1
  69.1 7.5 %join.1 = (f32[8,528,128]{2,1,0:T(8,128)S(1)}, f32[8,520,128]{2,1,0:T(8,128)S(1)}, f32[8,528,128]{2,1,0:T(8,128)S(1)}, f32[8,528,128]{2,1,0:T(8,128)S(1)}, f32[5...) custom-call(bf16[16,1040,128]{2,1,0:T(8,128)(2,1)S(1)} %all_to_all.1, ...), custom_call_target="tpu_custom_call", output_to_operand_aliasing={{2}: (2, {}), {3}: (3, {})} | custom-call | flops 15728640 | bytes 12582912 | tf_op jit(solution)/shard_map/join/pallas_call | solution.py:388
  76.6 2.4 %collective-permute-start.4 = (f32[2,1024]{1,0:T(2,128)S(1)}, f32[2,1024]{1,0:T(2,128)S(1)}, u32[]{:S(2)}, u32[]{:S(2)}) collective-permute-start(f32[2,1024]{1,0:T(2,128)S(1)} %get-tuple-element.56), channel_id=1, source_target_pairs={{0,16},{16,32},{32,48},{48,64},{64,80},{80,96},{96,112},{112,0},{1... | collective-permute-start | bytes 24584 | tf_op jit(solution)/shard_map/ppermute | solution.py:699
  78.9 4.5 %collective-permute-start.5 = (f32[2,1024]{1,0:T(2,128)S(1)}, f32[2,1024]{1,0:T(2,128)S(1)}, u32[]{:S(2)}, u32[]{:S(2)}) collective-permute-start(f32[2,1024]{1,0:T(2,128)S(1)} %get-tuple-element.57), channel_id=1, source_target_pairs={{0,112},{16,0},{32,16},{48,32},{64,48},{80,64},{96,80},{112,96},{1... | collective-permute-start | bytes 24584 | tf_op jit(solution)/shard_map/ppermute | solution.py:699
  83.4 0.4 collective-permute-start.6
  83.8 4.4 %collective-permute-start.7 = (f32[2,512]{1,0:T(2,128)S(1)}, f32[2,512]{1,0:T(2,128)S(1)}, u32[]{:S(2)}, u32[]{:S(2)}) collective-permute-start(f32[2,512]{1,0:T(2,128)S(1)} %get-tuple-element.59.own_left), channel_id=1, source_target_pairs={{0,15},{1,0},{2,1},{3,2},{4,3},{5,4},{6,5},{7,6},{8,7},{9,8},{10,9... | collective-permute-start | bytes 12296 | tf_op jit(solution)/shard_map/ppermute | solution.py:699
  88.2 0.0 copy-start.5
  88.2 4.7 %fill.1 = (f32[8,528,128]{2,1,0:T(8,128)S(1)}, f32[8,520,128]{2,1,0:T(8,128)S(1)}) custom-call(f32[512,8,128]{2,1,0:T(8,128)S(1)} %get-tuple-element.48.weights, f32[512,8,128]{2,1,0:T(8,128)S(1)} %get-tuple-element.49.pulls, f32[8,528,128]{2,1,0:T(8,128)S(1)} %get-tuple-element.50.prior, ...), custom_call_target="tpu_custom_call", output_to_operand_aliasing={{0}: (5, {}), {1}: (6, {})} | custom-call | flops 33554432 | bytes 16777216 | tf_op jit(solution)/shard_map/fill/pallas_call | solution.py:425
  92.9 0.0 collective-permute-done.6.r_left
  92.9 0.0 collective-permute-done.7.r_right
  92.9 0.0 collective-permute-done.4.r_up
  93.0 0.0 collective-permute-done.5.r_down
  93.0 0.0 copy-done.5
  93.0 3.9 %moments.1 = (f32[8,528,128]{2,1,0:T(8,128)S(1)}, f32[8,528,128]{2,1,0:T(8,128)S(1)}, f32[8,512,128]{2,1,0:T(8,128)S(1)}, f32[128,128]{1,0:T(8,128)S(1)}) custom-call(f32[8,528,128]{2,1,0:T(8,128)S(1)} %get-tuple-element.54.r_in, f32[8,520,128]{2,1,0:T(8,128)S(1)} %get-tuple-element.55.diag, ...), custom_call_target="tpu_custom_call", output_to_operand_aliasing={{0}: (0, {})} | custom-call | flops 20971520 | bytes 12582912 | tf_op jit(solution)/shard_map/moments/pallas_call | solution.py:554
  96.9 16.2 %all_to_all.17 = f32[128,1,128]{2,1,0:T(1,128)S(1)} all-to-all(f32[128,1,128]{2,1,0:T(1,128)S(1)} %bitcast.9), channel_id=1, replica_groups=mesh['row'=8,'col'=16] {'row','col'}, dimensions={0} | all-to-all | bytes 131072 | tf_op jit(solution)/shard_map/all_to_all | solution.py:724
  113.0 3.0 %finish.1 = (f32[512,1024]{1,0:T(8,128)}, f32[512,1024]{1,0:T(8,128)}) custom-call(f32[128,128]{1,0:T(8,128)S(1)} %bitcast.8, f32[512,1024]{1,0:T(8,128)S(1)} %copy-done, f32[8,528,128]{2,1,0:T(8,128)S(1)} %get-tuple-element.61.r, f32[8,528,128]{2,1,0:T(8,128)S(1)} %get-tuple-element.62.q, f32[8,512,128]{2,1,0:T(8,128)S(1)} %get-tuple-element.63.s), custom_call_target="tpu_custom_call" | custom-call | flops 4194304 | bytes 12582912 | tf_op jit(solution)/shard_map/finish/pallas_call | solution.py:680
Async XLA Ops:
  0.6 11.6 %copy-start.7 = (s32[1,512]{1,0:T(1,128)S(1)}, s32[1,512]{1,0:T(1,128)}, u32[]{:S(2)}) copy-start(s32[1,512]{1,0:T(1,128)} %offset_ref.1) | copy-start | bytes 6148
  0.6 11.6 %copy-start.6 = (s32[1,512]{1,0:T(1,128)S(1)}, s32[1,512]{1,0:T(1,128)}, u32[]{:S(2)}) copy-start(s32[1,512]{1,0:T(1,128)} %owner_ref.1) | copy-start | bytes 6148
  0.7 11.6 %copy-start.4 = (bf16[1,512,1024]{2,1,0:T(8,128)(2,1)S(1)}, bf16[1,512,1024]{2,1,0:T(8,128)(2,1)}, u32[]{:S(2)}) copy-start(bf16[1,512,1024]{2,1,0:T(8,128)(2,1)} %param.9) | copy-start | bytes 3145732
  0.7 11.6 %copy-start.3 = (bf16[1,512,1024]{2,1,0:T(8,128)(2,1)S(1)}, bf16[1,512,1024]{2,1,0:T(8,128)(2,1)}, u32[]{:S(2)}) copy-start(bf16[1,512,1024]{2,1,0:T(8,128)(2,1)} %param.8) | copy-start | bytes 3145732
  2.8 14.0 %collective-permute-start = (f32[2,1024]{1,0:T(2,128)}, f32[2,1024]{1,0:T(2,128)S(1)}, u32[]{:S(2)}, u32[]{:S(2)}) collective-permute-start(f32[2,1024]{1,0:T(2,128)} %get-tuple-element.33), channel_id=1, source_target_pairs={{0,16},{16,32},{32,48},{48,64},{64,80},{80,96},{96,112},{112,0},{1... | collective-permute-start | bytes 24584 | tf_op jit(solution)/shard_map/ppermute | solution.py:699
  5.4 11.3 %collective-permute-start.1 = (f32[1,1024]{1,0:T(1,128)}, f32[1,1024]{1,0:T(1,128)S(1)}, u32[]{:S(2)}, u32[]{:S(2)}) collective-permute-start(f32[1,1024]{1,0:T(1,128)} %get-tuple-element.34), channel_id=1, source_target_pairs={{0,112},{16,0},{32,16},{48,32},{64,48},{80,64},{96,80},{112,96},{1... | collective-permute-start | bytes 12296 | tf_op jit(solution)/shard_map/ppermute | solution.py:699
  5.4 11.4 %collective-permute-start.2 = (f32[2,512]{1,0:T(2,128)}, f32[2,512]{1,0:T(2,128)S(1)}, u32[]{:S(2)}, u32[]{:S(2)}) collective-permute-start(f32[2,512]{1,0:T(2,128)} %get-tuple-element.35.own_ky), channel_id=1, source_target_pairs={{0,1},{1,2},{2,3},{3,4},{4,5},{5,6},{6,7},{7,8},{8,9},{9,10},{10,1... | collective-permute-start | bytes 12296 | tf_op jit(solution)/shard_map/ppermute | solution.py:699
  6.7 10.0 %collective-permute-start.3 = (f32[1,512]{1,0:T(1,128)}, f32[1,512]{1,0:T(1,128)S(1)}, u32[]{:S(2)}, u32[]{:S(2)}) collective-permute-start(f32[1,512]{1,0:T(1,128)} %get-tuple-element.36), channel_id=1, source_target_pairs={{0,15},{1,0},{2,1},{3,2},{4,3},{5,4},{6,5},{7,6},{8,7},{9,8},{10,9... | collective-permute-start | bytes 6152 | tf_op jit(solution)/shard_map/ppermute | solution.py:699
  12.3 1.6 %copy-start = (f32[512,1024]{1,0:T(8,128)S(1)}, f32[512,1024]{1,0:T(8,128)}, u32[]{:S(2)}) copy-start(f32[512,1024]{1,0:T(8,128)} %prior.1) | copy-start | bytes 6291460
  12.3 2.2 %copy-start.2 = (f32[512,1024]{1,0:T(8,128)S(1)}, f32[512,1024]{1,0:T(8,128)}, u32[]{:S(2)}) copy-start(f32[512,1024]{1,0:T(8,128)} %kx_in.1) | copy-start | bytes 6291460
  16.8 52.3 %copy-start.1 = (f32[512,1024]{1,0:T(8,128)S(1)}, f32[512,1024]{1,0:T(8,128)}, u32[]{:S(2)}) copy-start(f32[512,1024]{1,0:T(8,128)} %ky.5) | copy-start | bytes 6291460
  76.6 16.4 %collective-permute-start.4 = (f32[2,1024]{1,0:T(2,128)S(1)}, f32[2,1024]{1,0:T(2,128)S(1)}, u32[]{:S(2)}, u32[]{:S(2)}) collective-permute-start(f32[2,1024]{1,0:T(2,128)S(1)} %get-tuple-element.56), channel_id=1, source_target_pairs={{0,16},{16,32},{32,48},{48,64},{64,80},{80,96},{96,112},{112,0},{1... | collective-permute-start | bytes 24584 | tf_op jit(solution)/shard_map/ppermute | solution.py:699
  78.9 14.0 %collective-permute-start.5 = (f32[2,1024]{1,0:T(2,128)S(1)}, f32[2,1024]{1,0:T(2,128)S(1)}, u32[]{:S(2)}, u32[]{:S(2)}) collective-permute-start(f32[2,1024]{1,0:T(2,128)S(1)} %get-tuple-element.57), channel_id=1, source_target_pairs={{0,112},{16,0},{32,16},{48,32},{64,48},{80,64},{96,80},{112,96},{1... | collective-permute-start | bytes 24584 | tf_op jit(solution)/shard_map/ppermute | solution.py:699
  83.4 9.5 %collective-permute-start.6 = (f32[2,512]{1,0:T(2,128)S(1)}, f32[2,512]{1,0:T(2,128)S(1)}, u32[]{:S(2)}, u32[]{:S(2)}) collective-permute-start(f32[2,512]{1,0:T(2,128)S(1)} %get-tuple-element.58.own_right), channel_id=1, source_target_pairs={{0,1},{1,2},{2,3},{3,4},{4,5},{5,6},{6,7},{7,8},{8,9},{9,10},{10,1... | collective-permute-start | bytes 12296 | tf_op jit(solution)/shard_map/ppermute | solution.py:699
  83.8 9.2 %collective-permute-start.7 = (f32[2,512]{1,0:T(2,128)S(1)}, f32[2,512]{1,0:T(2,128)S(1)}, u32[]{:S(2)}, u32[]{:S(2)}) collective-permute-start(f32[2,512]{1,0:T(2,128)S(1)} %get-tuple-element.59.own_left), channel_id=1, source_target_pairs={{0,15},{1,0},{2,1},{3,2},{4,3},{5,4},{6,5},{7,6},{8,7},{9,8},{10,9... | collective-permute-start | bytes 12296 | tf_op jit(solution)/shard_map/ppermute | solution.py:699
  88.2 4.8 %copy-start.5 = (f32[2,512]{1,0:T(2,128)S(1)}, f32[2,512]{1,0:T(2,128)}, u32[]{:S(2)}) copy-start(f32[2,512]{1,0:T(2,128)} %get-tuple-element.35.own_ky) | copy-start | bytes 12292

commit v7 on v6

--- a/solution.py
+++ b/solution.py
@@ -113,7 +113,7 @@
                 out[slot, first : first + 16 * chunks, :] = buffer[: 16 * chunks, :].astype(jnp.bfloat16)
         return carry
 
-    lax.fori_loop(0, GROUPS, one_run, 0)
+    lax.fori_loop(0, GROUPS, one_run, 0, unroll=2)
 
 
 def pack(owners, offsets, count, depth, conf, slots):
@@ -211,7 +211,7 @@
 
 BATCH = 32
 UF = 64
-UO = 16
+UO = 32
 US = 64
 UM = 64
 
@@ -656,7 +656,7 @@
             residual[b, part, :] = x - (one * y - two * s[b, part, :])
             return carry
 
-        lax.fori_loop(0, rows // 8, step, 0, unroll=8)
+        lax.fori_loop(0, rows // 8, step, 0, unroll=16)
         if b == 0:
             mend(0, b, 0)
             mend(2, b, rows - 1)

time: 116 us -> 116 us (level)
  blocking collectives: 68.5 us -> 71.6 us
  Pallas kernels: 25 us -> 22.5 us
    all_to_all x1, blocking collectives: 16.2 us -> 19.3 us  [shards(): lax.all_to_all(table, ('row', 'col'), split_axis=0, concat_axis=0, tiled=...]
    pallas_call x1, Pallas kernels: 7.47 us -> 5.08 us  [join(): pl.pallas_call(join_kernel, out_shape=[jax.ShapeDtypeStruct(s, F32) for s...]
where the time goes in v7:
time: 116 us; the launch traced here: 117 us
  blocking collectives  71.6 us (62%)
  Pallas kernels  22.5 us (19%)
  starting transfers between devices  20.5 us (18%)
  between operations  1.48 us (1%)
    all_to_all x1, blocking collectives, shards(): lax.all_to_all(payload, 'col', split_axis=0, concat_axis=0, tiled=True)  52.3 us
    ppermute x8, starting transfers between devices, send(): lax.ppermute(strip, axis, [(i, (i + by) % count) for i in range(count)])  20.5 us
    all_to_all x1, blocking collectives, shards(): lax.all_to_all(table, ('row', 'col'), split_axis=0, concat_axis=0, tiled=...  19.3 us
    pallas_call x1, Pallas kernels, join(): pl.pallas_call(join_kernel, out_shape=[jax.ShapeDtypeStruct(s, F32) for s...  5.08 us
    pallas_call x1, Pallas kernels, fill(): pl.pallas_call(fill_kernel, out_shape=[jax.ShapeDtypeStruct(x.shape, F32)...  4.72 us
    pallas_call x1, Pallas kernels, moments(): pl.pallas_call(moments_kernel, out_shape=[jax.ShapeDtypeStruct(r.shape, F...  3.89 us
    pallas_call x1, Pallas kernels, finish(): pl.pallas_call(finish_kernel, out_shape=[jax.ShapeDtypeStruct((rows, bloc...  2.89 us
  transfers between devices with their start and end apart: 8, of which 0 were waited for; matrix products, arithmetic and copies ran while one was open for 0% of the time, Pallas kernels for 7%

profile of v7, /device:TPU:1, one launch (start us, length us, event | category | flops | bytes accessed | tf_op | source)
XLA Modules:
  0.0 116.7 jit_solution(10411766320800691150)
XLA Ops:
  0.6 0.0 copy-start.7
  0.6 0.0 copy-start.6
  0.7 0.0 copy-start.4
  0.7 0.0 copy-start.3
  0.7 2.1 %strips.1 = (f32[1,1024]{1,0:T(1,128)}, f32[2,1024]{1,0:T(2,128)}, f32[1,512]{1,0:T(1,128)}, f32[2,512]{1,0:T(2,128)}) custom-call(f32[512,1024]{1,0:T(8,128)} %prior.1, f32[512,1024]{1,0:T(8,128)} %prior.1, f32[512,1024]{1,0:T(8,128)} %kx_in.1, f32[512,1024]{1,0:T(8,128)} %prior.1, f32[512,1024]{1,0:T(8,128)} %prior.1, f32[512,1024]{1,0:T(8,128)} %ky.5), custom_call_target="tpu_custom_call" | custom-call | tf_op jit(solution)/shard_map/strips/pallas_call | solution.py:157
  2.8 2.6 %collective-permute-start = (f32[2,1024]{1,0:T(2,128)}, f32[2,1024]{1,0:T(2,128)S(1)}, u32[]{:S(2)}, u32[]{:S(2)}) collective-permute-start(f32[2,1024]{1,0:T(2,128)} %get-tuple-element.33), channel_id=1, source_target_pairs={{0,16},{16,32},{32,48},{48,64},{64,80},{80,96},{96,112},{112,0},{1... | collective-permute-start | bytes 24584 | tf_op jit(solution)/shard_map/ppermute | solution.py:699
  5.4 0.0 collective-permute-start.1
  5.4 1.3 %collective-permute-start.2 = (f32[2,512]{1,0:T(2,128)}, f32[2,512]{1,0:T(2,128)S(1)}, u32[]{:S(2)}, u32[]{:S(2)}) collective-permute-start(f32[2,512]{1,0:T(2,128)} %get-tuple-element.35.own_ky), channel_id=1, source_target_pairs={{0,1},{1,2},{2,3},{3,4},{4,5},{5,6},{6,7},{7,8},{8,9},{9,10},{10,1... | collective-permute-start | bytes 12296 | tf_op jit(solution)/shard_map/ppermute | solution.py:699
  6.7 4.9 %collective-permute-start.3 = (f32[1,512]{1,0:T(1,128)}, f32[1,512]{1,0:T(1,128)S(1)}, u32[]{:S(2)}, u32[]{:S(2)}) collective-permute-start(f32[1,512]{1,0:T(1,128)} %get-tuple-element.36), channel_id=1, source_target_pairs={{0,15},{1,0},{2,1},{3,2},{4,3},{5,4},{6,5},{7,6},{8,7},{9,8},{10,9... | collective-permute-start | bytes 6152 | tf_op jit(solution)/shard_map/ppermute | solution.py:699
  12.3 0.0 copy-done.7
  12.3 0.0 copy-done.6
  12.3 0.0 copy-done.4
  12.3 0.0 copy-done.3
  12.3 0.0 copy-start
  12.3 0.0 copy-start.2
  12.3 1.6 %pack.1 = bf16[16,1040,128]{2,1,0:T(8,128)(2,1)S(1)} custom-call(s32[1,512]{1,0:T(1,128)S(1)} %copy-done.6, s32[1,1]{1,0:T(1,128)S(6)} %copy.21.count_ref, s32[1,512]{1,0:T(1,128)S(1)} %copy-done.7, bf16[512,1024]{1,0:T(8,128)(2,1)S(1)} %bitcast.6, bf16[512,1024]{1,0:T(8,128)(2,1)S(1)} %bitcast.7), custom_call_target="tpu_custom_call" | custom-call | flops 1048576 | bytes 4194304 | tf_op jit(solution)/shard_map/pack/pallas_call | solution.py:125
  13.9 0.0 copy-done
  13.9 0.6 copy-done.2
  14.5 2.2 %arrange.1 = (f32[512,8,128]{2,1,0:T(8,128)S(1)}, f32[8,528,128]{2,1,0:T(8,128)S(1)}, f32[8,528,128]{2,1,0:T(8,128)S(1)}) custom-call(f32[512,1024]{1,0:T(8,128)S(1)} %copy-done, f32[512,1024]{1,0:T(8,128)S(1)} %copy-done.2), custom_call_target="tpu_custom_call" | custom-call | flops 4194304 | bytes 14680064 | tf_op jit(solution)/shard_map/arrange/pallas_call | solution.py:201
  16.7 0.0 collective-permute-done.3.from_right
  16.8 0.0 collective-permute-done.1.from_down
  16.8 0.0 collective-permute-done.2.from_left.k_left
  16.8 0.0 collective-permute-done.from_up
  16.8 0.0 copy-start.1
  16.8 52.3 %all_to_all.16.got = bf16[16,1040,128]{2,1,0:T(8,128)(2,1)S(1)} all-to-all(bf16[16,1040,128]{2,1,0:T(8,128)(2,1)S(1)} %pack.1), channel_id=1, replica_groups=mesh['row'=8,'col'=16] {'col'}, dimensions={0} | all-to-all | bytes 8519680 | tf_op jit(solution)/shard_map/all_to_all | solution.py:717
  69.1 0.0 copy-done.1
  69.1 5.1 %join.1 = (f32[8,528,128]{2,1,0:T(8,128)S(1)}, f32[8,520,128]{2,1,0:T(8,128)S(1)}, f32[8,528,128]{2,1,0:T(8,128)S(1)}, f32[8,528,128]{2,1,0:T(8,128)S(1)}, f32[5...) custom-call(bf16[16,1040,128]{2,1,0:T(8,128)(2,1)S(1)} %all_to_all.1, ...), custom_call_target="tpu_custom_call", output_to_operand_aliasing={{2}: (2, {}), {3}: (3, {})} | custom-call | flops 15728640 | bytes 12582912 | tf_op jit(solution)/shard_map/join/pallas_call | solution.py:388
  74.2 4.6 %collective-permute-start.4 = (f32[2,1024]{1,0:T(2,128)S(1)}, f32[2,1024]{1,0:T(2,128)S(1)}, u32[]{:S(2)}, u32[]{:S(2)}) collective-permute-start(f32[2,1024]{1,0:T(2,128)S(1)} %get-tuple-element.56), channel_id=1, source_target_pairs={{0,16},{16,32},{32,48},{48,64},{64,80},{80,96},{96,112},{112,0},{1... | collective-permute-start | bytes 24584 | tf_op jit(solution)/shard_map/ppermute | solution.py:699
  78.8 0.0 collective-permute-start.5
  78.8 4.7 %collective-permute-start.6 = (f32[2,512]{1,0:T(2,128)S(1)}, f32[2,512]{1,0:T(2,128)S(1)}, u32[]{:S(2)}, u32[]{:S(2)}) collective-permute-start(f32[2,512]{1,0:T(2,128)S(1)} %get-tuple-element.58.own_right), channel_id=1, source_target_pairs={{0,1},{1,2},{2,3},{3,4},{4,5},{5,6},{6,7},{7,8},{8,9},{9,10},{10,1... | collective-permute-start | bytes 12296 | tf_op jit(solution)/shard_map/ppermute | solution.py:699
  83.5 2.3 %collective-permute-start.7 = (f32[2,512]{1,0:T(2,128)S(1)}, f32[2,512]{1,0:T(2,128)S(1)}, u32[]{:S(2)}, u32[]{:S(2)}) collective-permute-start(f32[2,512]{1,0:T(2,128)S(1)} %get-tuple-element.59.own_left), channel_id=1, source_target_pairs={{0,15},{1,0},{2,1},{3,2},{4,3},{5,4},{6,5},{7,6},{8,7},{9,8},{10,9... | collective-permute-start | bytes 12296 | tf_op jit(solution)/shard_map/ppermute | solution.py:699
  85.8 0.0 copy-start.5
  85.8 4.7 %fill.1 = (f32[8,528,128]{2,1,0:T(8,128)S(1)}, f32[8,520,128]{2,1,0:T(8,128)S(1)}) custom-call(f32[512,8,128]{2,1,0:T(8,128)S(1)} %get-tuple-element.48.weights, f32[512,8,128]{2,1,0:T(8,128)S(1)} %get-tuple-element.49.pulls, f32[8,528,128]{2,1,0:T(8,128)S(1)} %get-tuple-element.50.prior, ...), custom_call_target="tpu_custom_call", output_to_operand_aliasing={{0}: (5, {}), {1}: (6, {})} | custom-call | flops 33554432 | bytes 16777216 | tf_op jit(solution)/shard_map/fill/pallas_call | solution.py:425
  90.6 0.0 collective-permute-done.6.r_left
  90.6 0.0 collective-permute-done.7.r_right
  90.6 0.0 collective-permute-done.4.r_up
  90.6 0.0 collective-permute-done.5.r_down
  90.6 0.0 copy-done.5
  90.6 3.9 %moments.1 = (f32[8,528,128]{2,1,0:T(8,128)S(1)}, f32[8,528,128]{2,1,0:T(8,128)S(1)}, f32[8,512,128]{2,1,0:T(8,128)S(1)}, f32[128,128]{1,0:T(8,128)S(1)}) custom-call(f32[8,528,128]{2,1,0:T(8,128)S(1)} %get-tuple-element.54.r_in, f32[8,520,128]{2,1,0:T(8,128)S(1)} %get-tuple-element.55.diag, ...), custom_call_target="tpu_custom_call", output_to_operand_aliasing={{0}: (0, {})} | custom-call | flops 20971520 | bytes 12582912 | tf_op jit(solution)/shard_map/moments/pallas_call | solution.py:554
  94.5 19.3 %all_to_all.17 = f32[128,1,128]{2,1,0:T(1,128)S(1)} all-to-all(f32[128,1,128]{2,1,0:T(1,128)S(1)} %bitcast.9), channel_id=1, replica_groups=mesh['row'=8,'col'=16] {'row','col'}, dimensions={0} | all-to-all | bytes 131072 | tf_op jit(solution)/shard_map/all_to_all | solution.py:724
  113.8 2.9 %finish.1 = (f32[512,1024]{1,0:T(8,128)}, f32[512,1024]{1,0:T(8,128)}) custom-call(f32[128,128]{1,0:T(8,128)S(1)} %bitcast.8, f32[512,1024]{1,0:T(8,128)S(1)} %copy-done, f32[8,528,128]{2,1,0:T(8,128)S(1)} %get-tuple-element.61.r, f32[8,528,128]{2,1,0:T(8,128)S(1)} %get-tuple-element.62.q, f32[8,512,128]{2,1,0:T(8,128)S(1)} %get-tuple-element.63.s), custom_call_target="tpu_custom_call" | custom-call | flops 4194304 | bytes 12582912 | tf_op jit(solution)/shard_map/finish/pallas_call | solution.py:680
Async XLA Ops:
  0.6 11.6 %copy-start.7 = (s32[1,512]{1,0:T(1,128)S(1)}, s32[1,512]{1,0:T(1,128)}, u32[]{:S(2)}) copy-start(s32[1,512]{1,0:T(1,128)} %offset_ref.1) | copy-start | bytes 6148
  0.6 11.6 %copy-start.6 = (s32[1,512]{1,0:T(1,128)S(1)}, s32[1,512]{1,0:T(1,128)}, u32[]{:S(2)}) copy-start(s32[1,512]{1,0:T(1,128)} %owner_ref.1) | copy-start | bytes 6148
  0.7 11.6 %copy-start.4 = (bf16[1,512,1024]{2,1,0:T(8,128)(2,1)S(1)}, bf16[1,512,1024]{2,1,0:T(8,128)(2,1)}, u32[]{:S(2)}) copy-start(bf16[1,512,1024]{2,1,0:T(8,128)(2,1)} %param.9) | copy-start | bytes 3145732
  0.7 11.6 %copy-start.3 = (bf16[1,512,1024]{2,1,0:T(8,128)(2,1)S(1)}, bf16[1,512,1024]{2,1,0:T(8,128)(2,1)}, u32[]{:S(2)}) copy-start(bf16[1,512,1024]{2,1,0:T(8,128)(2,1)} %param.8) | copy-start | bytes 3145732
  2.8 14.0 %collective-permute-start = (f32[2,1024]{1,0:T(2,128)}, f32[2,1024]{1,0:T(2,128)S(1)}, u32[]{:S(2)}, u32[]{:S(2)}) collective-permute-start(f32[2,1024]{1,0:T(2,128)} %get-tuple-element.33), channel_id=1, source_target_pairs={{0,16},{16,32},{32,48},{48,64},{64,80},{80,96},{96,112},{112,0},{1... | collective-permute-start | bytes 24584 | tf_op jit(solution)/shard_map/ppermute | solution.py:699
  5.4 11.3 %collective-permute-start.1 = (f32[1,1024]{1,0:T(1,128)}, f32[1,1024]{1,0:T(1,128)S(1)}, u32[]{:S(2)}, u32[]{:S(2)}) collective-permute-start(f32[1,1024]{1,0:T(1,128)} %get-tuple-element.34), channel_id=1, source_target_pairs={{0,112},{16,0},{32,16},{48,32},{64,48},{80,64},{96,80},{112,96},{1... | collective-permute-start | bytes 12296 | tf_op jit(solution)/shard_map/ppermute | solution.py:699
  5.4 11.4 %collective-permute-start.2 = (f32[2,512]{1,0:T(2,128)}, f32[2,512]{1,0:T(2,128)S(1)}, u32[]{:S(2)}, u32[]{:S(2)}) collective-permute-start(f32[2,512]{1,0:T(2,128)} %get-tuple-element.35.own_ky), channel_id=1, source_target_pairs={{0,1},{1,2},{2,3},{3,4},{4,5},{5,6},{6,7},{7,8},{8,9},{9,10},{10,1... | collective-permute-start | bytes 12296 | tf_op jit(solution)/shard_map/ppermute | solution.py:699
  6.7 10.0 %collective-permute-start.3 = (f32[1,512]{1,0:T(1,128)}, f32[1,512]{1,0:T(1,128)S(1)}, u32[]{:S(2)}, u32[]{:S(2)}) collective-permute-start(f32[1,512]{1,0:T(1,128)} %get-tuple-element.36), channel_id=1, source_target_pairs={{0,15},{1,0},{2,1},{3,2},{4,3},{5,4},{6,5},{7,6},{8,7},{9,8},{10,9... | collective-permute-start | bytes 6152 | tf_op jit(solution)/shard_map/ppermute | solution.py:699
  12.3 1.6 %copy-start = (f32[512,1024]{1,0:T(8,128)S(1)}, f32[512,1024]{1,0:T(8,128)}, u32[]{:S(2)}) copy-start(f32[512,1024]{1,0:T(8,128)} %prior.1) | copy-start | bytes 6291460
  12.3 2.2 %copy-start.2 = (f32[512,1024]{1,0:T(8,128)S(1)}, f32[512,1024]{1,0:T(8,128)}, u32[]{:S(2)}) copy-start(f32[512,1024]{1,0:T(8,128)} %kx_in.1) | copy-start | bytes 6291460
  16.8 52.3 %copy-start.1 = (f32[512,1024]{1,0:T(8,128)S(1)}, f32[512,1024]{1,0:T(8,128)}, u32[]{:S(2)}) copy-start(f32[512,1024]{1,0:T(8,128)} %ky.5) | copy-start | bytes 6291460
  74.2 16.4 %collective-permute-start.4 = (f32[2,1024]{1,0:T(2,128)S(1)}, f32[2,1024]{1,0:T(2,128)S(1)}, u32[]{:S(2)}, u32[]{:S(2)}) collective-permute-start(f32[2,1024]{1,0:T(2,128)S(1)} %get-tuple-element.56), channel_id=1, source_target_pairs={{0,16},{16,32},{32,48},{48,64},{64,80},{80,96},{96,112},{112,0},{1... | collective-permute-start | bytes 24584 | tf_op jit(solution)/shard_map/ppermute | solution.py:699
  78.8 11.8 %collective-permute-start.5 = (f32[2,1024]{1,0:T(2,128)S(1)}, f32[2,1024]{1,0:T(2,128)S(1)}, u32[]{:S(2)}, u32[]{:S(2)}) collective-permute-start(f32[2,1024]{1,0:T(2,128)S(1)} %get-tuple-element.57), channel_id=1, source_target_pairs={{0,112},{16,0},{32,16},{48,32},{64,48},{80,64},{96,80},{112,96},{1... | collective-permute-start | bytes 24584 | tf_op jit(solution)/shard_map/ppermute | solution.py:699
  78.8 11.8 %collective-permute-start.6 = (f32[2,512]{1,0:T(2,128)S(1)}, f32[2,512]{1,0:T(2,128)S(1)}, u32[]{:S(2)}, u32[]{:S(2)}) collective-permute-start(f32[2,512]{1,0:T(2,128)S(1)} %get-tuple-element.58.own_right), channel_id=1, source_target_pairs={{0,1},{1,2},{2,3},{3,4},{4,5},{5,6},{6,7},{7,8},{8,9},{9,10},{10,1... | collective-permute-start | bytes 12296 | tf_op jit(solution)/shard_map/ppermute | solution.py:699
  83.5 7.0 %collective-permute-start.7 = (f32[2,512]{1,0:T(2,128)S(1)}, f32[2,512]{1,0:T(2,128)S(1)}, u32[]{:S(2)}, u32[]{:S(2)}) collective-permute-start(f32[2,512]{1,0:T(2,128)S(1)} %get-tuple-element.59.own_left), channel_id=1, source_target_pairs={{0,15},{1,0},{2,1},{3,2},{4,3},{5,4},{6,5},{7,6},{8,7},{9,8},{10,9... | collective-permute-start | bytes 12296 | tf_op jit(solution)/shard_map/ppermute | solution.py:699
  85.8 4.8 %copy-start.5 = (f32[2,512]{1,0:T(2,128)S(1)}, f32[2,512]{1,0:T(2,128)}, u32[]{:S(2)}) copy-start(f32[2,512]{1,0:T(2,128)} %get-tuple-element.35.own_ky) | copy-start | bytes 12292
